TPU v7x, 32 devices: a whole 2x2x4 slice. The times are simulated.
32 devices in a mesh: seq: 2 (over core), ctx: 8 (over z, y), head: 2 (over x).
Axes of the slice: x: 2, y: 2, z: 4, core: 2. Of those that a mesh axis runs over, the one named last changes fastest.
Arguments:
- queries: bfloat16 [2048, 8, 128], P(('seq', 'ctx'), 'head'), parts along dimension 0, may hold values from -8 to 8
- key_rows: bfloat16 [2048, 128], P(('seq', 'ctx')), parts along dimension 0, may hold values from -8 to 8
- value_rows: bfloat16 [2048, 128], P(('seq', 'ctx')), parts along dimension 0, may hold values from -6 to 6
- out_grad: bfloat16 [2048, 8, 128], P(('seq', 'ctx'), 'head'), parts along dimension 0, may hold values from -6 to 6
- doc_lengths: int32 [16], P('seq'), parts along dimension 0, may hold values from 1 to 256, 1024 in all
- balance: int32 [2048], P('seq'), parts along dimension 0, may hold values from 0 to 1023, as said below
Outputs:
- attended: bfloat16 [2048, 8, 128], P(('seq', 'ctx'), 'head'), parts along dimension 0
- query_grad: bfloat16 [2048, 8, 128], P(('seq', 'ctx'), 'head'), parts along dimension 0
- key_grad: bfloat16 [2048, 128], P(('seq', 'ctx')), parts along dimension 0
- value_grad: bfloat16 [2048, 128], P(('seq', 'ctx')), parts along dimension 0
There are 2 independent parts, one for each index of `seq`. A program takes and returns all parts, laid end to end along the dimension named above; each array names one. Nothing has to cross between parts.
Inputs may be any that keep to these rules, and one draw needn't show every extreme that they name: `doc_lengths`: the lengths sum to 1024 and the longest is exactly 256. `balance`: A permutation of the positions that moves aligned runs of 64 positions whole and in order.
All inputs are finite; a program needn't handle non-finite values.
Results may differ from a plain program's by a relative error of at most 0.034.
Values may be sent and summed in bfloat16 or wider, within the bound.
No kernel may reach another device: no remote copies, remote signals or barrier semaphores. Data moves between devices by JAX's collectives and lax.ppermute only.
A program may use at most 64 MiB of HBM per device.

v0:
```python
import math

import jax
import jax.numpy as jnp
from jax import lax
from jax.sharding import PartitionSpec as P

NEGATIVE = -1e30


def document_of(positions, doc_lengths):
    doc_ends = jnp.cumsum(doc_lengths)
    return jnp.sum((positions[:, None] >= doc_ends[None, :]).astype(jnp.int32), axis=1)


def body(queries, key_rows, value_rows, out_grad, doc_lengths, balance):
    tok_rows = queries.shape[0]
    heads_here = queries.shape[1]
    head_width = queries.shape[2]
    scaling = 1.0 / math.sqrt(head_width)
    seq_total = balance.shape[0]
    block_len = min(512, seq_total)
    block_count = seq_total // block_len
    docs_all = document_of(balance, doc_lengths)
    my_first = lax.axis_index("ctx") * tok_rows
    my_pos = lax.dynamic_slice_in_dim(balance, my_first, tok_rows)
    my_doc = lax.dynamic_slice_in_dim(docs_all, my_first, tok_rows)
    all_keys, all_values = (
        lax.all_gather(key_rows, "ctx", axis=0, tiled=True),
        lax.all_gather(value_rows, "ctx", axis=0, tiled=True),
    )

    def key_block(row_start):
        key_pos = lax.dynamic_slice_in_dim(balance, row_start, block_len)
        key_doc = lax.dynamic_slice_in_dim(docs_all, row_start, block_len)
        visible_pairs = (key_doc[None, :] == my_doc[:, None]) & (
            key_pos[None, :] <= my_pos[:, None]
        )
        key_blk = lax.dynamic_slice_in_dim(all_keys, row_start, block_len)
        value_blk = lax.dynamic_slice_in_dim(all_values, row_start, block_len)
        return (key_blk, value_blk, visible_pairs)

    def forward_step(step_index, state_now):
        key_blk, value_blk, visible_pairs = key_block(step_index * block_len)
        allowed = visible_pairs[:, None, :]
        running_max, weight_sum, weighted = state_now
        scores = (
            jnp.einsum("qhd,kd->qhk", queries, key_blk, preferred_element_type=jnp.float32)
            * scaling
        )
        scores = jnp.where(allowed, scores, NEGATIVE)
        new_max = jnp.maximum(running_max, jnp.max(scores, axis=2))
        raw_weights = jnp.where(allowed, jnp.exp(scores - new_max[:, :, None]), 0.0)
        factor = jnp.exp(running_max - new_max)
        weight_sum = weight_sum * factor + jnp.sum(raw_weights, axis=2)
        weighted = weighted * factor[:, :, None] + jnp.einsum(
            "qhk,kd->qhd",
            raw_weights.astype(jnp.bfloat16),
            value_blk,
            preferred_element_type=jnp.float32,
        )
        return (new_max, weight_sum, weighted)

    start_state = (
        jnp.full((tok_rows, heads_here), NEGATIVE, jnp.float32),
        jnp.zeros((tok_rows, heads_here), jnp.float32),
        jnp.zeros((tok_rows, heads_here, head_width), jnp.float32),
    )
    running_max, weight_sum, weighted = lax.fori_loop(0, block_count, forward_step, start_state)
    attended = (weighted / weight_sum[:, :, None]).astype(jnp.bfloat16)
    log_total = running_max + jnp.log(weight_sum)
    row_inner = jnp.sum(out_grad.astype(jnp.float32) * attended.astype(jnp.float32), axis=2)

    def backward_tile(query_part, grad_part, total_part, inner_part, key_blk, value_blk, allowed):
        scores = (
            jnp.einsum("qhd,kd->qhk", query_part, key_blk, preferred_element_type=jnp.float32)
            * scaling
        )
        weights = jnp.where(allowed, jnp.exp(scores - total_part[:, :, None]), 0.0)
        grad_weights = jnp.einsum(
            "qhd,kd->qhk", grad_part, value_blk, preferred_element_type=jnp.float32
        )
        grad_scores = (weights * (grad_weights - inner_part[:, :, None])).astype(jnp.bfloat16)
        return (weights.astype(jnp.bfloat16), grad_scores)

    def query_step(step_index, state_now):
        row_start = step_index * block_len
        key_blk, value_blk, visible_pairs = key_block(row_start)
        allowed = visible_pairs[:, None, :]
        grad_acc, key_terms = state_now
        weights_b, grad_scores = backward_tile(
            queries, out_grad, log_total, row_inner, key_blk, value_blk, allowed
        )
        grad_acc = grad_acc + jnp.einsum(
            "qhk,kd->qhd", grad_scores, key_blk, preferred_element_type=jnp.float32
        )
        key_part = (
            jnp.einsum("qhk,qhd->kd", grad_scores, queries, preferred_element_type=jnp.float32)
            * scaling
        )
        value_part = jnp.einsum(
            "qhk,qhd->kd", weights_b, out_grad, preferred_element_type=jnp.float32
        )
        key_terms = lax.dynamic_update_slice_in_dim(
            key_terms, jnp.concatenate([key_part, value_part], axis=1), row_start, 0
        )
        return (grad_acc, key_terms)

    grad_start = (
        jnp.zeros((tok_rows, heads_here, head_width), jnp.float32),
        jnp.zeros((seq_total, 2 * head_width), jnp.float32),
    )
    grad_acc, key_terms = lax.fori_loop(0, block_count, query_step, grad_start)
    query_grad = (grad_acc * scaling).astype(jnp.bfloat16)
    shared = lax.psum_scatter(key_terms, "ctx", scatter_dimension=0, tiled=True)
    combined = lax.psum(shared, "head")
    key_grad = combined[:, :head_width].astype(jnp.bfloat16)
    value_grad = combined[:, head_width:].astype(jnp.bfloat16)
    return (attended, query_grad, key_grad, value_grad)


def solution(mesh):
    return jax.shard_map(
        body,
        mesh=mesh,
        in_specs=(
            P(("seq", "ctx"), "head", None),
            P(("seq", "ctx"), None),
            P(("seq", "ctx"), None),
            P(("seq", "ctx"), "head", None),
            P("seq"),
            P("seq"),
        ),
        out_specs=(
            P(("seq", "ctx"), "head", None),
            P(("seq", "ctx"), "head", None),
            P(("seq", "ctx"), None),
            P(("seq", "ctx"), None),
        ),
        check_vma=False,
    )
```

profile of v0, /device:TPU:0, one launch (start us, length us, event | category | flops | bytes accessed | tf_op | source)
XLA Modules:
  0.0 166.1 jit_solution(3495052994830510164)
XLA Ops:
  7.2 1.0 copy.43
  8.3 0.1 copy.46
  8.4 0.6 copy-done.6
  9.1 0.2 reduce-window.8
  9.3 0.1 dynamic_slice.63
  9.3 0.1 convert_reduce_fusion
  9.4 0.1 dynamic_slice.62
  9.5 0.1 copy.47
  9.7 0.6 copy-done.4
  10.3 32.8 %all_gather.6 = bf16[1024,128]{1,0:T(8,128)(2,1)S(1)} all-gather(bf16[128,128]{1,0:T(8,128)(2,1)S(1)} %copy-done.4), channel_id=1, replica_groups=mesh['seq'=2,'ctx'=8,'head'=2] {'ctx'}, dimensions={0}, use_global_device_ids=true | all-gather | bytes 294912 | tf_op jit(solution)/shard_map/all_gather | solution.py:29
  43.0 30.7 %all_gather.7 = bf16[1024,128]{1,0:T(8,128)(2,1)S(1)} all-gather(bf16[128,128]{1,0:T(8,128)(2,1)S(1)} %copy-done.5), channel_id=1, replica_groups=mesh['seq'=2,'ctx'=8,'head'=2] {'ctx'}, dimensions={0}, use_global_device_ids=true | all-gather | bytes 294912 | tf_op jit(solution)/shard_map/all_gather | solution.py:30
  73.8 2.8 %while.34 = (s32[]{:T(128)}, f32[128,4]{0,1:T(4,128)S(1)}, f32[128,4]{0,1:T(4,128)S(1)}, f32[128,4,128]{2,0,1:T(8,128)S(1)}, s32[1024]{0:T(1024)S(1)}, /*index=5...) while((s32[]{:T(128)}, f32[128,4]{0,1:T(4,128)S(1)}, ...), condition=%wide.region_5.6_spmd.clone, body=%wide.region_2.5_spmd.clone.sunk | while | flops 136972800 | bytes 4371679 | solution.py:69
  73.8 0.1 dynamic_slice.105
  73.9 0.1 dynamic_slice.106
  73.9 0.2 compare_and_fusion.4
  74.1 0.3 fusion.68
  74.5 0.2 fusion.69
  74.7 0.4 convolution_add_fusion.4
  75.2 0.1 dynamic_slice.105
  75.3 0.2 compare_and_fusion.4
  75.5 0.3 fusion.68
  75.9 0.2 fusion.69
  76.1 0.4 convolution_add_fusion.4
  76.6 0.1 copy.44
  76.7 0.9 multiply_reduce_fusion
  77.7 0.1 broadcast_in_dim.114.clone
  77.8 4.7 %while.35 = (s32[]{:T(128)}, f32[128,4,128]{2,0,1:T(8,128)S(1)}, f32[1024,256]{1,0:T(8,128)S(1)}, s32[1024]{0:T(1024)S(1)}, s32[128]{0:T(128)S(1)}, /*index=5*/s...) while((s32[]{:T(128)}, f32[128,4,128]{2,0,1:T(8,128)S(1)}, ...), condition=%wide.region_8.9_spmd.clone, body=%wide.region_7.8_spmd.clone.sunk | while | flops 337903616 | bytes 9979125 | solution.py:113
  77.8 0.1 dynamic_slice.110
  78.0 0.2 compare_and_fusion.5
  78.2 0.3 fusion.81
  78.5 0.3 convolution_bitcast_fusion.3
  78.8 0.3 fusion.82
  79.1 0.4 convolution_add_fusion.5
  79.5 0.3 fusion.83
  79.8 0.2 copy.68
  80.1 0.1 dynamic_slice.110
  80.3 0.2 compare_and_fusion.5
  80.5 0.3 fusion.81
  80.8 0.3 convolution_bitcast_fusion.3
  81.1 0.3 fusion.82
  81.4 0.4 convolution_add_fusion.5
  81.8 0.3 fusion.83
  82.2 0.2 copy.68
  82.4 1.0 copy-done
  83.5 0.9 fusion.34
  84.3 64.0 %reduce-scatter.2.cloned.1.call-done = f32[128,256]{1,0:T(8,128)} async-done(((f32[1024,256]{1,0:T(8,128)}), f32[128,256]{1,0:T(8,128)}) %reduce-scatter.2.cloned.1.call-update) | async-done | bytes 131088 | tf_op jit(solution)/shard_map/reduce_scatter | solution.py:115
  148.3 10.4 %all-reduce.1 = bf16[128,256]{1,0:T(8,128)(2,1)S(1)} all-reduce(f32[128,256]{1,0:T(8,128)} %reduce-scatter.2.cloned.1.call-done), channel_id=1, replica_groups=mesh['seq'=2,'ctx'=8,'head'=2] {'head'}, use_global_device_ids=true, to_apply=%region_10.11 | all-reduce | flops 32768 | bytes 196608 | tf_op jit(solution)/shard_map/psum | solution.py:116
  158.7 0.6 fusion.38
  (32 shorter events, 0.6 us)
Async XLA Ops:
  7.2 141.1 %reduce-scatter.2.cloned.1.call-start = ((), (), s32[]{:S(2)}) async-start(), calls=%async_computation.1 | async-start | bytes 1179648 | tf_op jit(solution)/shard_map/reduce_scatter | solution.py:115
  7.2 1.0 copy-start.2
  8.2 1.3 copy-start.1
  8.4 0.7 copy-start.6
  8.4 0.8 copy-start.3
  9.5 0.8 copy-start.4
  10.3 32.8 %copy-start.5 = (bf16[128,128]{1,0:T(8,128)(2,1)S(1)}, bf16[128,128]{1,0:T(8,128)(2,1)}, u32[]{:S(2)}) copy-start(bf16[128,128]{1,0:T(8,128)(2,1)} %param.12) | copy-start | bytes 98308
  82.4 1.0 copy-start
Sparse Core Ops, SparseCore 0:
  83.6 64.6 reduce-scatter.1
where the time goes:
time: 166 us
  blocking collectives  73.9 us (45%)
  waiting for transfers between devices  64 us (39%)
  between operations  14.2 us (9%)
  local copies, waits for them, and re-layouts  5.65 us (3%)
  matrix products  4.73 us (3%)
  other arithmetic  3.42 us (2%)
    reduce_scatter x1, waiting for transfers between devices, body(): shared = lax.psum_scatter(key_terms, 'ctx', scatter_dimension=0, tiled=True)  64 us
    all_gather x1, blocking collectives, body(): lax.all_gather(key_rows, 'ctx', axis=0, tiled=True)  32.8 us
    all_gather x1, blocking collectives, body(): lax.all_gather(value_rows, 'ctx', axis=0, tiled=True)  30.7 us
    psum x1, blocking collectives, body(): combined = lax.psum(shared, 'head')  10.4 us
    unnamed x18, local copies, waits for them, and re-layouts  3.58 us
  transfers between devices with their start and end apart: 1, of which 1 were waited for; matrix products, arithmetic and copies ran while one was open for 1% of the time, Pallas kernels for 0%

commit v1 on v0

v1 whole, which is shorter than its diff:
```python
import functools
import math

import jax
import jax.numpy as jnp
from jax import lax
from jax.experimental import pallas as pl
from jax.experimental.pallas import tpu as pltpu
from jax.sharding import PartitionSpec as P

NEGATIVE = -1e30
RUN = 64
LONGEST_SHARE = 4

ANY = pl.BlockSpec(memory_space=pl.ANY)
SMEM = pl.BlockSpec(memory_space=pltpu.SMEM)


def contract(a, b, dim_a, dim_b):
    return lax.dot_general(
        a, b, (((dim_a,), (dim_b,)), ((), ())), preferred_element_type=jnp.float32
    )


def attention_kernel(n_ctx, heads, place, balance, doc_lengths, q_in, g_in, *refs):
    blocks = refs[:n_ctx]
    att_out, qg_out = refs[n_ctx : n_ctx + 2]
    terms_out = refs[n_ctx + 2 : 2 * n_ctx + 2]
    scratch = refs[2 * n_ctx + 2 :]
    q_all, g_all, kv_all, window, terms, att_buf, qg_buf, bf_buf, f32_buf, slot_of, in_sem, out_sem = scratch
    me = place[0]
    tok_rows = blocks[0].shape[0]
    width = blocks[0].shape[1] // 2
    seq_total = kv_all.shape[0]
    runs_here = tok_rows // RUN
    reach = window.shape[1] // RUN
    run_rows = RUN * heads
    docs = doc_lengths.shape[0]
    scaling = 1.0 / math.sqrt(width)

    copies = [pltpu.make_async_copy(q_in, q_all, in_sem.at[0]), pltpu.make_async_copy(g_in, g_all, in_sem.at[1])]
    for k in range(n_ctx):
        owner = lax.bitwise_xor(me, k)
        rows = pl.ds(pl.multiple_of(owner * tok_rows, tok_rows), tok_rows)
        copies.append(pltpu.make_async_copy(blocks[k], kv_all.at[rows], in_sem.at[2 + k]))
    for copy in copies:
        copy.start()

    def note(s, carry):
        slot_of[lax.shift_right_logical(balance[s * RUN], 6)] = s
        return carry

    lax.fori_loop(0, seq_total // RUN, note, 0, unroll=seq_total // RUN <= 16)
    terms[...] = jnp.zeros_like(terms)
    for copy in copies:
        copy.wait()

    for r in range(runs_here):
        place_run = lax.shift_right_logical(balance[me * tok_rows + r * RUN], 6)
        slots = []
        for j in range(reach):
            slot = slot_of[jnp.maximum(place_run - (reach - 1) + j, 0)]
            rows = pl.ds(pl.multiple_of(slot * RUN, RUN), RUN)
            slots.append(rows)
            window[r, j * RUN : (j + 1) * RUN, :] = kv_all[rows, :]
        keys = window[r, :, :width]
        values = window[r, :, width:]
        q_rows = q_all[r * run_rows : (r + 1) * run_rows, :]
        g_rows = g_all[r * run_rows : (r + 1) * run_rows, :]

        lane = lax.broadcasted_iota(jnp.int32, (1, run_rows), 1)
        q_pos = place_run * RUN + lax.div(lane, heads)
        doc_start = jnp.zeros_like(q_pos)
        doc_end = jnp.int32(0)
        for d in range(docs):
            doc_end = doc_end + doc_lengths[d]
            doc_start = jnp.where(doc_end <= q_pos, doc_end, doc_start)
        k_pos = (place_run - (reach - 1)) * RUN + lax.broadcasted_iota(jnp.int32, (reach * RUN, run_rows), 0)
        visible = (k_pos >= doc_start) & (k_pos <= q_pos)

        scores = jnp.where(visible, contract(keys, q_rows, 1, 1), NEGATIVE)
        top = jnp.max(scores, axis=0, keepdims=True)
        raw = jnp.exp((scores - top) * scaling)
        one_over = 1.0 / jnp.sum(raw, axis=0, keepdims=True)
        attended = contract(values, raw.astype(jnp.bfloat16), 0, 0) * one_over
        att_buf[r * run_rows : (r + 1) * run_rows, :] = attended.T.astype(jnp.bfloat16)

        weights = raw * one_over
        grad_weights = contract(values, g_rows, 1, 1)
        row_inner = jnp.sum(weights * grad_weights, axis=0, keepdims=True)
        grad_scores = (weights * (grad_weights - row_inner)).astype(jnp.bfloat16)
        value_part = contract(weights.astype(jnp.bfloat16), g_rows, 1, 0)
        key_part = contract(grad_scores, q_rows, 1, 0) * scaling
        query_part = contract(keys, grad_scores, 0, 0) * scaling
        qg_buf[r * run_rows : (r + 1) * run_rows, :] = query_part.T.astype(jnp.bfloat16)
        for j in range(reach):
            part = slice(j * RUN, (j + 1) * RUN)
            terms[slots[j], :width] += key_part[part, :]
            terms[slots[j], width:] += value_part[part, :]

    out_copies = []
    for k in range(n_ctx):
        owner = lax.bitwise_xor(me, k)
        rows = pl.ds(pl.multiple_of(owner * tok_rows, tok_rows), tok_rows)
        if k % 2:
            bf_buf[k // 2] = terms[rows, :].astype(jnp.bfloat16)
            out_copies.append(pltpu.make_async_copy(bf_buf.at[k // 2], terms_out[k], out_sem.at[k]))
        else:
            out_copies.append(pltpu.make_async_copy(terms.at[rows], terms_out[k], out_sem.at[k]))
        out_copies[-1].start()
    out_copies.append(pltpu.make_async_copy(att_buf, att_out, out_sem.at[n_ctx]))
    out_copies.append(pltpu.make_async_copy(qg_buf, qg_out, out_sem.at[n_ctx + 1]))
    out_copies[-2].start()
    out_copies[-1].start()
    for copy in out_copies:
        copy.wait()


def attention(place, balance, doc_lengths, q_rows, g_rows, blocks, heads):
    n_ctx = len(blocks)
    tok_rows, both = blocks[0].shape
    width = both // 2
    seq_total = balance.shape[0]
    reach = seq_total // LONGEST_SHARE // RUN + 1
    rows = q_rows.shape[0]
    outs = [jax.ShapeDtypeStruct((rows, width), jnp.bfloat16)] * 2
    for k in range(n_ctx):
        outs.append(jax.ShapeDtypeStruct((tok_rows, both), jnp.bfloat16 if k % 2 else jnp.float32))
    return pl.pallas_call(
        functools.partial(attention_kernel, n_ctx, heads),
        out_shape=outs,
        in_specs=[SMEM] * 3 + [ANY] * (2 + n_ctx),
        out_specs=[ANY] * len(outs),
        scratch_shapes=[
            pltpu.VMEM((rows, width), jnp.bfloat16),
            pltpu.VMEM((rows, width), jnp.bfloat16),
            pltpu.VMEM((seq_total, both), jnp.bfloat16),
            pltpu.VMEM((tok_rows // RUN, reach * RUN, both), jnp.bfloat16),
            pltpu.VMEM((seq_total, both), jnp.float32),
            pltpu.VMEM((rows, width), jnp.bfloat16),
            pltpu.VMEM((rows, width), jnp.bfloat16),
            pltpu.VMEM((n_ctx // 2, tok_rows, both), jnp.bfloat16),
            pltpu.VMEM((8, 128), jnp.float32),
            pltpu.SMEM((seq_total // RUN,), jnp.int32),
            pltpu.SemaphoreType.DMA((2 + n_ctx,)),
            pltpu.SemaphoreType.DMA((2 + n_ctx,)),
        ],
        compiler_params=pltpu.CompilerParams(
            vmem_limit_bytes=(16 << 20) if seq_total <= 1024 else (56 << 20)
        ),
    )(place, balance, doc_lengths, q_rows, g_rows, *blocks)


def body(n_ctx, n_head, queries, key_rows, value_rows, out_grad, doc_lengths, balance):
    tok_rows, heads, width = queries.shape

    def swap(array, k):
        return lax.ppermute(array, "ctx", [(i, i ^ k) for i in range(n_ctx)])

    mine = jnp.concatenate([key_rows, value_rows], axis=1)
    blocks = {0: mine}
    far_first = list(range(n_ctx - 2, 0, -2))
    for k in far_first:
        blocks[k] = swap(mine, k)
    blocks[1] = swap(mine, 1)
    for k in reversed(far_first):
        blocks[k + 1] = swap(blocks[k], 1)

    place = lax.axis_index("ctx").astype(jnp.int32).reshape(1)
    attended, query_grad, *terms = attention(
        place,
        balance,
        doc_lengths,
        queries.reshape(tok_rows * heads, width),
        out_grad.reshape(tok_rows * heads, width),
        [blocks[k] for k in range(n_ctx)],
        heads,
    )

    arrived = {}
    for k in far_first:
        arrived[k] = swap(terms[k + 1], 1)
    arrived[0] = swap(terms[1], 1)
    total = terms[0] + arrived[0].astype(jnp.float32)
    for k in far_first:
        pair = (terms[k] + arrived[k].astype(jnp.float32)).astype(jnp.bfloat16)
        total = total + swap(pair, k).astype(jnp.float32)
    mine = total.astype(jnp.bfloat16)
    other = lax.ppermute(mine, "head", [(i, (i + 1) % n_head) for i in range(n_head)])
    combined = (mine.astype(jnp.float32) + other.astype(jnp.float32)).astype(jnp.bfloat16)
    return (
        attended.reshape(tok_rows, heads, width),
        query_grad.reshape(tok_rows, heads, width),
        combined[:, :width],
        combined[:, width:],
    )


def solution(mesh):
    return jax.shard_map(
        functools.partial(body, mesh.shape["ctx"], mesh.shape["head"]),
        mesh=mesh,
        in_specs=(
            P(("seq", "ctx"), "head", None),
            P(("seq", "ctx"), None),
            P(("seq", "ctx"), None),
            P(("seq", "ctx"), "head", None),
            P("seq"),
            P("seq"),
        ),
        out_specs=(
            P(("seq", "ctx"), "head", None),
            P(("seq", "ctx"), "head", None),
            P(("seq", "ctx"), None),
            P(("seq", "ctx"), None),
        ),
        check_vma=False,
    )
```

time: 166 us -> 43.8 us (0.26)
  blocking collectives: 73.9 us -> 0 us
  waiting for transfers between devices: 64 us -> 11.8 us
  starting transfers between devices: 0.04 us -> 21.7 us
  between operations: 14.2 us -> 0.69 us
  Pallas kernels: 0 us -> 5.51 us
  matrix products: 4.73 us -> 0 us
  other arithmetic: 3.42 us -> 0.1 us
  local copies, waits for them, and re-layouts: 5.65 us -> 3.76 us
    reduce_scatter x1 -> x0, waiting for transfers between devices: 64 us -> none  [body(): shared = lax.psum_scatter(key_terms, 'ctx', scatter_dimension=0, tiled=True)]
    all_gather x2 -> x0, blocking collectives: 63.5 us -> none  [the longest x1 32.8 us: body(): lax.all_gather(key_rows, 'ctx', axis=0, tiled=True)]
    ppermute x0 -> x15, starting transfers between devices: none -> 21.7 us  [the longest x14 20.2 us: swap(): return lax.ppermute(array, 'ctx', [(i, i ^ k) for i in range(n_ctx)])]
    ppermute x0 -> x15, waiting for transfers between devices: none -> 11.8 us  [the longest x14 9.05 us: swap(): return lax.ppermute(array, 'ctx', [(i, i ^ k) for i in range(n_ctx)])]
    psum x1 -> x0, blocking collectives: 10.4 us -> none  [body(): combined = lax.psum(shared, 'head')]
    pallas_call x0 -> x1, Pallas kernels: none -> 5.51 us  [attention(): pl.pallas_call(functools.partial(attention_kernel, n_ctx, heads), out_sha...]
    dot_general x14 -> x0, matrix products: 4.73 us -> none  [the longest x2 0.89 us: forward_step(): jnp.einsum('qhk,kd->qhd', raw_weights.astype(jnp.bfloat16), value_blk, pr...]
    unnamed x18 -> x9, local copies, waits for them, and re-layouts: 3.58 us -> 2.36 us
  transfers between devices with their start and end apart: 1 -> 15, of which waited for: 1 -> 9; matrix products, arithmetic and copies ran while one was open for 1% -> 0% of each run, Pallas kernels for 0% -> 0%
where the time goes in v1:
time: 43.8 us; the launch traced here: 43.6 us
  starting transfers between devices  21.7 us (50%)
  waiting for transfers between devices  11.8 us (27%)
  Pallas kernels  5.51 us (13%)
  local copies, waits for them, and re-layouts  3.76 us (9%)
  between operations  0.69 us (2%)
    ppermute x14, starting transfers between devices, swap(): return lax.ppermute(array, 'ctx', [(i, i ^ k) for i in range(n_ctx)])  20.2 us
    ppermute x14, waiting for transfers between devices, swap(): return lax.ppermute(array, 'ctx', [(i, i ^ k) for i in range(n_ctx)])  9.05 us
    pallas_call x1, Pallas kernels, attention(): pl.pallas_call(functools.partial(attention_kernel, n_ctx, heads), out_sha...  5.51 us
    ppermute x1, waiting for transfers between devices, body(): lax.ppermute(mine, 'head', [(i, (i + 1) % n_head) for i in range(n_head)])  2.77 us
    unnamed x9, local copies, waits for them, and re-layouts  2.36 us
    ppermute x1, starting transfers between devices, body(): lax.ppermute(mine, 'head', [(i, (i + 1) % n_head) for i in range(n_head)])  1.56 us
  transfers between devices with their start and end apart: 15, of which 9 were waited for; matrix products, arithmetic and copies ran while one was open for 0% of the time, Pallas kernels for 0%

profile of v1, /device:TPU:0, one launch (start us, length us, event | category | flops | bytes accessed | tf_op | source)
XLA Modules:
  0.0 43.6 jit_solution(11374531225793158149)
XLA Ops:
  0.6 0.0 copy-start
  0.6 0.8 %constant_dynamic-update-slice_fusion.1 = bf16[128,256]{1,0:T(8,128)(2,1)S(1)} fusion(bf16[128,128]{1,0:T(8,128)(2,1)} %param.7), kind=kLoop, calls=%fused_computation.6 | loop fusion | bytes 65536
  1.4 0.8 %constant_dynamic-update-slice_fusion.refs_0_ = bf16[128,256]{1,0:T(8,128)(2,1)S(1)} fusion(bf16[128,256]{1,0:T(8,128)(2,1)S(1)} %constant_dynamic-update-slice_fusion.1, bf16[128,128]{1,0:T(8,128)(2,1)} %param.8), kind=kLoop, calls=%fused_computation.5 | loop fusion | bytes 65536 | tf_op jit(solution)/shard_map/concatenate | solution.py:160
  2.2 5.1 %collective-permute-start.5 = (bf16[128,256]{1,0:T(8,128)(2,1)S(1)}, bf16[128,256]{1,0:T(8,128)(2,1)S(1)}, u32[]{:S(2)}, u32[]{:S(2)}) collective-permute-start(bf16[128,256]{1,0:T(8,128)(2,1)S(1)} %constant_dynamic-update-slice_fusion.refs_0_), channel_id=1, source_target_pairs={{0,12},{2,14},{4,8},{6,10},{8,4},{10,6},{12,0},{14,2},{1,13},{3,15... | collective-permute-start | bytes 196616 | tf_op jit(solution)/shard_map/ppermute | solution.py:158
  7.3 0.0 collective-permute-start.3
  7.3 0.6 %collective-permute-start.1 = (bf16[128,256]{1,0:T(8,128)(2,1)S(1)}, bf16[128,256]{1,0:T(8,128)(2,1)S(1)}, u32[]{:S(2)}, u32[]{:S(2)}) collective-permute-start(bf16[128,256]{1,0:T(8,128)(2,1)S(1)} %constant_dynamic-update-slice_fusion.refs_0_), channel_id=1, source_target_pairs={{0,4},{2,6},{4,0},{6,2},{8,12},{10,14},{12,8},{14,10},{1,5},{3,7},... | collective-permute-start | bytes 196616 | tf_op jit(solution)/shard_map/ppermute | solution.py:158
  8.0 1.7 %collective-permute-start = (bf16[128,256]{1,0:T(8,128)(2,1)S(1)}, bf16[128,256]{1,0:T(8,128)(2,1)S(1)}, u32[]{:S(2)}, u32[]{:S(2)}) collective-permute-start(bf16[128,256]{1,0:T(8,128)(2,1)S(1)} %constant_dynamic-update-slice_fusion.refs_0_), channel_id=1, source_target_pairs={{0,2},{2,0},{4,6},{6,4},{8,10},{10,8},{12,14},{14,12},{1,3},{3,1},... | collective-permute-start | bytes 196616 | tf_op jit(solution)/shard_map/ppermute | solution.py:158
  9.6 0.3 collective-permute-done.5.refs_6_
  9.9 1.9 %collective-permute-start.6 = (bf16[128,256]{1,0:T(8,128)(2,1)S(1)}, bf16[128,256]{1,0:T(8,128)(2,1)S(1)}, u32[]{:S(2)}, u32[]{:S(2)}) collective-permute-start(bf16[128,256]{1,0:T(8,128)(2,1)S(1)} %collective-permute-done.5.refs_6_), channel_id=1, source_target_pairs={{0,2},{2,0},{4,6},{6,4},{8,10},{10,8},{12,14},{14,12},{1,3},{3,1},... | collective-permute-start | bytes 196616 | tf_op jit(solution)/shard_map/ppermute | solution.py:158
  11.8 1.1 %collective-permute-done.3.refs_4_ = bf16[128,256]{1,0:T(8,128)(2,1)S(1)} collective-permute-done((bf16[128,256]{1,0:T(8,128)(2,1)S(1)}, bf16[128,256]{1,0:T(8,128)(2,1)S(1)}, u32[]{:S(2)}, u32[]{:S(2)}) %collective-permute-start.3) | collective-permute-done | bytes 65568 | tf_op jit(solution)/shard_map/ppermute | solution.py:158
  12.9 1.5 %collective-permute-start.4 = (bf16[128,256]{1,0:T(8,128)(2,1)S(1)}, bf16[128,256]{1,0:T(8,128)(2,1)S(1)}, u32[]{:S(2)}, u32[]{:S(2)}) collective-permute-start(bf16[128,256]{1,0:T(8,128)(2,1)S(1)} %collective-permute-done.3.refs_4_), channel_id=1, source_target_pairs={{0,2},{2,0},{4,6},{6,4},{8,10},{10,8},{12,14},{14,12},{1,3},{3,1},... | collective-permute-start | bytes 196616 | tf_op jit(solution)/shard_map/ppermute | solution.py:158
  14.4 0.0 collective-permute-done.1.refs_2_
  14.4 0.5 %collective-permute-start.2 = (bf16[128,256]{1,0:T(8,128)(2,1)S(1)}, bf16[128,256]{1,0:T(8,128)(2,1)S(1)}, u32[]{:S(2)}, u32[]{:S(2)}) collective-permute-start(bf16[128,256]{1,0:T(8,128)(2,1)S(1)} %collective-permute-done.1.refs_2_), channel_id=1, source_target_pairs={{0,2},{2,0},{4,6},{6,4},{8,10},{10,8},{12,14},{14,12},{1,3},{3,1},... | collective-permute-start | bytes 196616 | tf_op jit(solution)/shard_map/ppermute | solution.py:158
  15.0 0.0 copy-start.2
  15.0 0.0 collective-permute-done.refs_1_
  15.0 0.0 collective-permute-done.6.refs_7_
  15.0 2.8 %collective-permute-done.4.refs_5_ = bf16[128,256]{1,0:T(8,128)(2,1)S(1)} collective-permute-done((bf16[128,256]{1,0:T(8,128)(2,1)S(1)}, bf16[128,256]{1,0:T(8,128)(2,1)S(1)}, u32[]{:S(2)}, u32[]{:S(2)}) %collective-permute-start.4) | collective-permute-done | bytes 65568 | tf_op jit(solution)/shard_map/ppermute | solution.py:158
  17.8 0.9 %collective-permute-done.2.refs_3_ = bf16[128,256]{1,0:T(8,128)(2,1)S(1)} collective-permute-done((bf16[128,256]{1,0:T(8,128)(2,1)S(1)}, bf16[128,256]{1,0:T(8,128)(2,1)S(1)}, u32[]{:S(2)}, u32[]{:S(2)}) %collective-permute-start.2) | collective-permute-done | bytes 65568 | tf_op jit(solution)/shard_map/ppermute | solution.py:158
  18.7 0.0 copy-start.3
  18.7 0.0 copy-done
  18.7 0.0 copy-done.2
  18.7 0.6 %copy-done.3 = s32[8]{0:T(128)S(1)} copy-done((s32[8]{0:T(128)S(1)}, s32[8]{0:T(128)}, u32[]{:S(2)}) %copy-start.3) | copy-done | bytes 56
  19.4 0.0 copy-start.1
  19.4 0.9 %copy-done.1 = bf16[128,4,128]{2,1,0:T(4,128)(2,1)S(1)} copy-done((bf16[128,4,128]{2,1,0:T(4,128)(2,1)S(1)}, bf16[128,4,128]{2,1,0:T(4,128)(2,1)}, u32[]{:S(2)}) %copy-start.1) | copy-done | bytes 131096
  20.3 5.5 %shard_map.93 = (bf16[512,128]{1,0:T(8,128)(2,1)}, bf16[512,128]{1,0:T(8,128)(2,1)}, f32[128,256]{1,0:T(8,128)S(1)}, bf16[128,256]{1,0:T(8,128)(2,1)S(1)}, f32[1...) custom-call(s32[1]{0:T(128)} %bitcast.place, ...), custom_call_target="tpu_custom_call" | custom-call | tf_op jit(solution)/shard_map/pallas_call | solution.py:129
  25.8 1.0 %collective-permute-start.8 = (bf16[128,256]{1,0:T(8,128)(2,1)S(1)}, bf16[128,256]{1,0:T(8,128)(2,1)S(1)}, u32[]{:S(2)}, u32[]{:S(2)}) collective-permute-start(bf16[128,256]{1,0:T(8,128)(2,1)S(1)} %get-tuple-element.19), channel_id=1, source_target_pairs={{0,2},{2,0},{4,6},{6,4},{8,10},{10,8},{12,14},{14,12},{1,3},{3,1},... | collective-permute-start | bytes 196616 | tf_op jit(solution)/shard_map/ppermute | solution.py:158
  26.8 1.0 %collective-permute-start.7 = (bf16[128,256]{1,0:T(8,128)(2,1)S(1)}, bf16[128,256]{1,0:T(8,128)(2,1)S(1)}, u32[]{:S(2)}, u32[]{:S(2)}) collective-permute-start(bf16[128,256]{1,0:T(8,128)(2,1)S(1)} %get-tuple-element.17), channel_id=1, source_target_pairs={{0,2},{2,0},{4,6},{6,4},{8,10},{10,8},{12,14},{14,12},{1,3},{3,1},... | collective-permute-start | bytes 196616 | tf_op jit(solution)/shard_map/ppermute | solution.py:158
  27.9 1.0 %collective-permute-start.10 = (bf16[128,256]{1,0:T(8,128)(2,1)S(1)}, bf16[128,256]{1,0:T(8,128)(2,1)S(1)}, u32[]{:S(2)}, u32[]{:S(2)}) collective-permute-start(bf16[128,256]{1,0:T(8,128)(2,1)S(1)} %get-tuple-element.21), channel_id=1, source_target_pairs={{0,2},{2,0},{4,6},{6,4},{8,10},{10,8},{12,14},{14,12},{1,3},{3,1},... | collective-permute-start | bytes 196616 | tf_op jit(solution)/shard_map/ppermute | solution.py:158
  28.9 1.0 %collective-permute-start.12 = (bf16[128,256]{1,0:T(8,128)(2,1)S(1)}, bf16[128,256]{1,0:T(8,128)(2,1)S(1)}, u32[]{:S(2)}, u32[]{:S(2)}) collective-permute-start(bf16[128,256]{1,0:T(8,128)(2,1)S(1)} %get-tuple-element.23), channel_id=1, source_target_pairs={{0,2},{2,0},{4,6},{6,4},{8,10},{10,8},{12,14},{14,12},{1,3},{3,1},... | collective-permute-start | bytes 196616 | tf_op jit(solution)/shard_map/ppermute | solution.py:158
  29.9 0.9 %collective-permute-done.8 = bf16[128,256]{1,0:T(8,128)(2,1)S(1)} collective-permute-done((bf16[128,256]{1,0:T(8,128)(2,1)S(1)}, bf16[128,256]{1,0:T(8,128)(2,1)S(1)}, u32[]{:S(2)}, u32[]{:S(2)}) %collective-permute-start.8) | collective-permute-done | bytes 65568 | tf_op jit(solution)/shard_map/ppermute | solution.py:158
  30.8 2.1 %collective-permute-start.9 = (bf16[128,256]{1,0:T(8,128)(2,1)S(1)}, bf16[128,256]{1,0:T(8,128)(2,1)S(1)}, u32[]{:S(2)}, u32[]{:S(2)}) collective-permute-start(bf16[128,256]{1,0:T(8,128)(2,1)S(1)} %add_convert_fusion.4), channel_id=1, source_target_pairs={{0,12},{2,14},{4,8},{6,10},{8,4},{10,6},{12,0},{14,2},{1,13},{3,15... | collective-permute-start | bytes 196616 | tf_op jit(solution)/shard_map/ppermute | solution.py:158
  32.9 0.0 collective-permute-done.10
  32.9 0.6 %collective-permute-start.11 = (bf16[128,256]{1,0:T(8,128)(2,1)S(1)}, bf16[128,256]{1,0:T(8,128)(2,1)S(1)}, u32[]{:S(2)}, u32[]{:S(2)}) collective-permute-start(bf16[128,256]{1,0:T(8,128)(2,1)S(1)} %add_convert_fusion.3), channel_id=1, source_target_pairs={{0,8},{2,10},{4,12},{6,14},{8,0},{10,2},{12,4},{14,6},{1,9},{3,11}... | collective-permute-start | bytes 196616 | tf_op jit(solution)/shard_map/ppermute | solution.py:158
  33.5 0.0 collective-permute-done.12
  33.5 2.1 %collective-permute-start.13 = (bf16[128,256]{1,0:T(8,128)(2,1)S(1)}, bf16[128,256]{1,0:T(8,128)(2,1)S(1)}, u32[]{:S(2)}, u32[]{:S(2)}) collective-permute-start(bf16[128,256]{1,0:T(8,128)(2,1)S(1)} %add_convert_fusion.2), channel_id=1, source_target_pairs={{0,4},{2,6},{4,0},{6,2},{8,12},{10,14},{12,8},{14,10},{1,5},{3,7},... | collective-permute-start | bytes 196616 | tf_op jit(solution)/shard_map/ppermute | solution.py:158
  35.6 0.0 collective-permute-done.7
  35.6 1.4 %collective-permute-done.9 = bf16[128,256]{1,0:T(8,128)(2,1)S(1)} collective-permute-done((bf16[128,256]{1,0:T(8,128)(2,1)S(1)}, bf16[128,256]{1,0:T(8,128)(2,1)S(1)}, u32[]{:S(2)}, u32[]{:S(2)}) %collective-permute-start.9) | collective-permute-done | bytes 65568 | tf_op jit(solution)/shard_map/ppermute | solution.py:158
  37.0 1.5 %collective-permute-done.11 = bf16[128,256]{1,0:T(8,128)(2,1)S(1)} collective-permute-done((bf16[128,256]{1,0:T(8,128)(2,1)S(1)}, bf16[128,256]{1,0:T(8,128)(2,1)S(1)}, u32[]{:S(2)}, u32[]{:S(2)}) %collective-permute-start.11) | collective-permute-done | bytes 65568 | tf_op jit(solution)/shard_map/ppermute | solution.py:158
  38.5 0.1 collective-permute-done.13
  38.6 1.6 %collective-permute-start.14 = (bf16[128,256]{1,0:T(8,128)(2,1)S(1)}, bf16[128,256]{1,0:T(8,128)(2,1)S(1)}, u32[]{:S(2)}, u32[]{:S(2)}) collective-permute-start(bf16[128,256]{1,0:T(8,128)(2,1)S(1)} %add_convert_fusion.1), channel_id=1, source_target_pairs={{0,1},{1,0},{2,3},{3,2},{4,5},{5,4},{6,7},{7,6},{8,9},{9,8},{10,11... | collective-permute-start | bytes 196616 | tf_op jit(solution)/shard_map/ppermute | solution.py:189
  40.2 2.8 %collective-permute-done.14 = bf16[128,256]{1,0:T(8,128)(2,1)S(1)} collective-permute-done((bf16[128,256]{1,0:T(8,128)(2,1)S(1)}, bf16[128,256]{1,0:T(8,128)(2,1)S(1)}, u32[]{:S(2)}, u32[]{:S(2)}) %collective-permute-start.14) | collective-permute-done | bytes 65568 | tf_op jit(solution)/shard_map/ppermute | solution.py:189
  43.0 0.6 %fusion = (bf16[128,128]{1,0:T(8,128)(2,1)}, bf16[128,128]{1,0:T(8,128)(2,1)}) fusion(bf16[128,256]{1,0:T(8,128)(2,1)S(1)} %add_convert_fusion), kind=kLoop, calls=%fused_computation.7 | loop fusion | bytes 131072 | tf_op jit(solution)/shard_map/slice | solution.py:195
  (5 shorter events, 0.1 us)
Async XLA Ops:
  0.6 18.1 %copy-start = (bf16[128,4,128]{2,1,0:T(4,128)(2,1)S(1)}, bf16[128,4,128]{2,1,0:T(4,128)(2,1)}, u32[]{:S(2)}) copy-start(bf16[128,4,128]{2,1,0:T(4,128)(2,1)} %param.6) | copy-start | bytes 393220
  2.2 7.7 %collective-permute-start.5 = (bf16[128,256]{1,0:T(8,128)(2,1)S(1)}, bf16[128,256]{1,0:T(8,128)(2,1)S(1)}, u32[]{:S(2)}, u32[]{:S(2)}) collective-permute-start(bf16[128,256]{1,0:T(8,128)(2,1)S(1)} %constant_dynamic-update-slice_fusion.refs_0_), channel_id=1, source_target_pairs={{0,12},{2,14},{4,8},{6,10},{8,4},{10,6},{12,0},{14,2},{1,13},{3,15... | collective-permute-start | bytes 196616 | tf_op jit(solution)/shard_map/ppermute | solution.py:158
  7.3 5.6 %collective-permute-start.3 = (bf16[128,256]{1,0:T(8,128)(2,1)S(1)}, bf16[128,256]{1,0:T(8,128)(2,1)S(1)}, u32[]{:S(2)}, u32[]{:S(2)}) collective-permute-start(bf16[128,256]{1,0:T(8,128)(2,1)S(1)} %constant_dynamic-update-slice_fusion.refs_0_), channel_id=1, source_target_pairs={{0,8},{2,10},{4,12},{6,14},{8,0},{10,2},{12,4},{14,6},{1,9},{3,11}... | collective-permute-start | bytes 196616 | tf_op jit(solution)/shard_map/ppermute | solution.py:158
  7.3 7.1 %collective-permute-start.1 = (bf16[128,256]{1,0:T(8,128)(2,1)S(1)}, bf16[128,256]{1,0:T(8,128)(2,1)S(1)}, u32[]{:S(2)}, u32[]{:S(2)}) collective-permute-start(bf16[128,256]{1,0:T(8,128)(2,1)S(1)} %constant_dynamic-update-slice_fusion.refs_0_), channel_id=1, source_target_pairs={{0,4},{2,6},{4,0},{6,2},{8,12},{10,14},{12,8},{14,10},{1,5},{3,7},... | collective-permute-start | bytes 196616 | tf_op jit(solution)/shard_map/ppermute | solution.py:158
  8.0 7.0 %collective-permute-start = (bf16[128,256]{1,0:T(8,128)(2,1)S(1)}, bf16[128,256]{1,0:T(8,128)(2,1)S(1)}, u32[]{:S(2)}, u32[]{:S(2)}) collective-permute-start(bf16[128,256]{1,0:T(8,128)(2,1)S(1)} %constant_dynamic-update-slice_fusion.refs_0_), channel_id=1, source_target_pairs={{0,2},{2,0},{4,6},{6,4},{8,10},{10,8},{12,14},{14,12},{1,3},{3,1},... | collective-permute-start | bytes 196616 | tf_op jit(solution)/shard_map/ppermute | solution.py:158
  9.9 5.1 %collective-permute-start.6 = (bf16[128,256]{1,0:T(8,128)(2,1)S(1)}, bf16[128,256]{1,0:T(8,128)(2,1)S(1)}, u32[]{:S(2)}, u32[]{:S(2)}) collective-permute-start(bf16[128,256]{1,0:T(8,128)(2,1)S(1)} %collective-permute-done.5.refs_6_), channel_id=1, source_target_pairs={{0,2},{2,0},{4,6},{6,4},{8,10},{10,8},{12,14},{14,12},{1,3},{3,1},... | collective-permute-start | bytes 196616 | tf_op jit(solution)/shard_map/ppermute | solution.py:158
  12.9 4.8 %collective-permute-start.4 = (bf16[128,256]{1,0:T(8,128)(2,1)S(1)}, bf16[128,256]{1,0:T(8,128)(2,1)S(1)}, u32[]{:S(2)}, u32[]{:S(2)}) collective-permute-start(bf16[128,256]{1,0:T(8,128)(2,1)S(1)} %collective-permute-done.3.refs_4_), channel_id=1, source_target_pairs={{0,2},{2,0},{4,6},{6,4},{8,10},{10,8},{12,14},{14,12},{1,3},{3,1},... | collective-permute-start | bytes 196616 | tf_op jit(solution)/shard_map/ppermute | solution.py:158
  14.4 4.3 %collective-permute-start.2 = (bf16[128,256]{1,0:T(8,128)(2,1)S(1)}, bf16[128,256]{1,0:T(8,128)(2,1)S(1)}, u32[]{:S(2)}, u32[]{:S(2)}) collective-permute-start(bf16[128,256]{1,0:T(8,128)(2,1)S(1)} %collective-permute-done.1.refs_2_), channel_id=1, source_target_pairs={{0,2},{2,0},{4,6},{6,4},{8,10},{10,8},{12,14},{14,12},{1,3},{3,1},... | collective-permute-start | bytes 196616 | tf_op jit(solution)/shard_map/ppermute | solution.py:158
  15.0 3.8 %copy-start.2 = (s32[1024]{0:T(1024)S(1)}, s32[1024]{0:T(1024)}, u32[]{:S(2)}) copy-start(s32[1024]{0:T(1024)} %balance.1) | copy-start | bytes 12292
  18.7 0.7 %copy-start.3 = (s32[8]{0:T(128)S(1)}, s32[8]{0:T(128)}, u32[]{:S(2)}) copy-start(s32[8]{0:T(128)} %doc_lengths.1) | copy-start | bytes 100
  19.4 0.9 %copy-start.1 = (bf16[128,4,128]{2,1,0:T(4,128)(2,1)S(1)}, bf16[128,4,128]{2,1,0:T(4,128)(2,1)}, u32[]{:S(2)}) copy-start(bf16[128,4,128]{2,1,0:T(4,128)(2,1)} %param.9) | copy-start | bytes 393220
  25.8 5.0 %collective-permute-start.8 = (bf16[128,256]{1,0:T(8,128)(2,1)S(1)}, bf16[128,256]{1,0:T(8,128)(2,1)S(1)}, u32[]{:S(2)}, u32[]{:S(2)}) collective-permute-start(bf16[128,256]{1,0:T(8,128)(2,1)S(1)} %get-tuple-element.19), channel_id=1, source_target_pairs={{0,2},{2,0},{4,6},{6,4},{8,10},{10,8},{12,14},{14,12},{1,3},{3,1},... | collective-permute-start | bytes 196616 | tf_op jit(solution)/shard_map/ppermute | solution.py:158
  26.8 8.8 %collective-permute-start.7 = (bf16[128,256]{1,0:T(8,128)(2,1)S(1)}, bf16[128,256]{1,0:T(8,128)(2,1)S(1)}, u32[]{:S(2)}, u32[]{:S(2)}) collective-permute-start(bf16[128,256]{1,0:T(8,128)(2,1)S(1)} %get-tuple-element.17), channel_id=1, source_target_pairs={{0,2},{2,0},{4,6},{6,4},{8,10},{10,8},{12,14},{14,12},{1,3},{3,1},... | collective-permute-start | bytes 196616 | tf_op jit(solution)/shard_map/ppermute | solution.py:158
  27.9 5.0 %collective-permute-start.10 = (bf16[128,256]{1,0:T(8,128)(2,1)S(1)}, bf16[128,256]{1,0:T(8,128)(2,1)S(1)}, u32[]{:S(2)}, u32[]{:S(2)}) collective-permute-start(bf16[128,256]{1,0:T(8,128)(2,1)S(1)} %get-tuple-element.21), channel_id=1, source_target_pairs={{0,2},{2,0},{4,6},{6,4},{8,10},{10,8},{12,14},{14,12},{1,3},{3,1},... | collective-permute-start | bytes 196616 | tf_op jit(solution)/shard_map/ppermute | solution.py:158
  28.9 4.6 %collective-permute-start.12 = (bf16[128,256]{1,0:T(8,128)(2,1)S(1)}, bf16[128,256]{1,0:T(8,128)(2,1)S(1)}, u32[]{:S(2)}, u32[]{:S(2)}) collective-permute-start(bf16[128,256]{1,0:T(8,128)(2,1)S(1)} %get-tuple-element.23), channel_id=1, source_target_pairs={{0,2},{2,0},{4,6},{6,4},{8,10},{10,8},{12,14},{14,12},{1,3},{3,1},... | collective-permute-start | bytes 196616 | tf_op jit(solution)/shard_map/ppermute | solution.py:158
  30.8 6.1 %collective-permute-start.9 = (bf16[128,256]{1,0:T(8,128)(2,1)S(1)}, bf16[128,256]{1,0:T(8,128)(2,1)S(1)}, u32[]{:S(2)}, u32[]{:S(2)}) collective-permute-start(bf16[128,256]{1,0:T(8,128)(2,1)S(1)} %add_convert_fusion.4), channel_id=1, source_target_pairs={{0,12},{2,14},{4,8},{6,10},{8,4},{10,6},{12,0},{14,2},{1,13},{3,15... | collective-permute-start | bytes 196616 | tf_op jit(solution)/shard_map/ppermute | solution.py:158
  32.9 5.5 %collective-permute-start.11 = (bf16[128,256]{1,0:T(8,128)(2,1)S(1)}, bf16[128,256]{1,0:T(8,128)(2,1)S(1)}, u32[]{:S(2)}, u32[]{:S(2)}) collective-permute-start(bf16[128,256]{1,0:T(8,128)(2,1)S(1)} %add_convert_fusion.3), channel_id=1, source_target_pairs={{0,8},{2,10},{4,12},{6,14},{8,0},{10,2},{12,4},{14,6},{1,9},{3,11}... | collective-permute-start | bytes 196616 | tf_op jit(solution)/shard_map/ppermute | solution.py:158
  33.5 5.0 %collective-permute-start.13 = (bf16[128,256]{1,0:T(8,128)(2,1)S(1)}, bf16[128,256]{1,0:T(8,128)(2,1)S(1)}, u32[]{:S(2)}, u32[]{:S(2)}) collective-permute-start(bf16[128,256]{1,0:T(8,128)(2,1)S(1)} %add_convert_fusion.2), channel_id=1, source_target_pairs={{0,4},{2,6},{4,0},{6,2},{8,12},{10,14},{12,8},{14,10},{1,5},{3,7},... | collective-permute-start | bytes 196616 | tf_op jit(solution)/shard_map/ppermute | solution.py:158
  38.6 4.3 %collective-permute-start.14 = (bf16[128,256]{1,0:T(8,128)(2,1)S(1)}, bf16[128,256]{1,0:T(8,128)(2,1)S(1)}, u32[]{:S(2)}, u32[]{:S(2)}) collective-permute-start(bf16[128,256]{1,0:T(8,128)(2,1)S(1)} %add_convert_fusion.1), channel_id=1, source_target_pairs={{0,1},{1,0},{2,3},{3,2},{4,5},{5,4},{6,7},{7,6},{8,9},{9,8},{10,11... | collective-permute-start | bytes 196616 | tf_op jit(solution)/shard_map/ppermute | solution.py:189

commit v2 on v1

v2 whole, which is shorter than its diff:
```python
import functools
import math

import jax
import jax.numpy as jnp
from jax import lax
from jax.experimental import pallas as pl
from jax.experimental.pallas import tpu as pltpu
from jax.sharding import PartitionSpec as P

NEGATIVE = -1e30
RUN = 64
LONGEST_SHARE = 4

ANY = pl.BlockSpec(memory_space=pl.ANY)
VMEM = pl.BlockSpec(memory_space=pltpu.VMEM)
HBM = pl.BlockSpec(memory_space=pltpu.HBM)
SMEM = pl.BlockSpec(memory_space=pltpu.SMEM)


def contract(a, b, dim_a, dim_b):
    return lax.dot_general(
        a, b, (((dim_a,), (dim_b,)), ((), ())), preferred_element_type=jnp.float32
    )


def limit(seq_total):
    return pltpu.CompilerParams(vmem_limit_bytes=(16 << 20) if seq_total <= 1024 else (56 << 20))


def goes_first_over_y(k):
    return k % 2 == 1 and k > 3


def pack_kernel(key_rows, value_rows, q_rows, g_rows, kv_out, qg_out, sems):
    tok_rows, rows = key_rows.shape[0], q_rows.shape[0]
    copies = [
        pltpu.make_async_copy(key_rows, kv_out.at[pl.ds(0, tok_rows)], sems.at[0]),
        pltpu.make_async_copy(value_rows, kv_out.at[pl.ds(tok_rows, tok_rows)], sems.at[1]),
        pltpu.make_async_copy(q_rows, qg_out.at[pl.ds(0, rows)], sems.at[2]),
        pltpu.make_async_copy(g_rows, qg_out.at[pl.ds(rows, rows)], sems.at[3]),
    ]
    for copy in copies:
        copy.start()
    for copy in copies:
        copy.wait()


def pack(key_rows, value_rows, q_rows, g_rows, seq_total):
    return pl.pallas_call(
        pack_kernel,
        out_shape=[
            jax.ShapeDtypeStruct((2 * key_rows.shape[0], key_rows.shape[1]), jnp.bfloat16),
            jax.ShapeDtypeStruct((2 * q_rows.shape[0], q_rows.shape[1]), jnp.bfloat16),
        ],
        in_specs=[ANY] * 4,
        out_specs=[ANY] * 2,
        scratch_shapes=[pltpu.SemaphoreType.DMA((4,))],
        compiler_params=limit(seq_total),
    )(*[pltpu.with_memory_space_constraint(a, pltpu.HBM) for a in (key_rows, value_rows, q_rows, g_rows)])


def table_size(runs_here, reach, docs):
    return -(-(2 + runs_here * (1 + reach) + docs) // 128) * 128


def table_kernel(runs_here, reach, place, balance, doc_lengths, after, table_out, table, slot_of, sem):
    runs = balance.shape[0] // RUN
    docs = doc_lengths.shape[0]

    def note(s, carry):
        slot_of[lax.shift_right_logical(balance[s * RUN], 6)] = s
        return carry

    lax.fori_loop(0, runs, note, 0, unroll=runs <= 16)
    table[0] = place[0]
    table[1] = place[1]
    for r in range(runs_here):
        at = 2 + r * (1 + reach)
        place_run = lax.shift_right_logical(balance[(place[0] * runs_here + r) * RUN], 6)
        table[at] = place_run
        for j in range(reach):
            table[at + 1 + j] = slot_of[jnp.maximum(place_run - (reach - 1) + j, 0)]
    end = jnp.int32(0)
    for d in range(docs):
        end = end + doc_lengths[d]
        table[2 + runs_here * (1 + reach) + d] = end
    copy = pltpu.make_async_copy(table, table_out, sem)
    copy.start()
    copy.wait()


def make_table(place, balance, doc_lengths, after, runs_here, reach):
    size = table_size(runs_here, reach, doc_lengths.shape[0])
    runs = balance.shape[0] // RUN
    return pl.pallas_call(
        functools.partial(table_kernel, runs_here, reach),
        out_shape=jax.ShapeDtypeStruct((size,), jnp.int32),
        in_specs=[SMEM] * 3 + [ANY],
        out_specs=ANY,
        scratch_shapes=[
            pltpu.SMEM((size,), jnp.int32),
            pltpu.SMEM((runs,), jnp.int32),
            pltpu.SemaphoreType.DMA,
        ],
        compiler_params=limit(balance.shape[0]),
    )(place, balance, doc_lengths, after)


def run_window(table, kv_all, key_win, value_win, r, reach, runs_here, tok_rows):
    at = 2 + r * (1 + reach)
    rows = []
    for j in range(reach):
        slot = table[at + 1 + j]
        row = lax.div(slot, runs_here) * (2 * tok_rows) + lax.rem(slot, runs_here) * RUN
        row = pl.multiple_of(row, RUN)
        rows.append(row)
        key_win[r, j * RUN : (j + 1) * RUN, :] = kv_all[pl.ds(row, RUN), :]
        value_win[r, j * RUN : (j + 1) * RUN, :] = kv_all[pl.ds(row + tok_rows, RUN), :]
    return rows


def weights_of(table, keys, q_rows, r, reach, runs_here, docs, heads):
    count = q_rows.shape[0]
    place_run = table[2 + r * (1 + reach)]
    scaling = math.log2(math.e) / math.sqrt(keys.shape[1])
    lane = lax.broadcasted_iota(jnp.int32, (1, count), 1)
    q_off = lax.div(lax.rem(lane, RUN * heads), heads)
    q_pos = place_run * RUN + q_off
    doc_start = jnp.zeros_like(q_pos)
    for d in range(docs):
        doc_end = table[2 + runs_here * (1 + reach) + d]
        doc_start = jnp.where(doc_end <= q_pos, doc_end, doc_start)
    doc_start = doc_start - (place_run - (reach - 1)) * RUN
    scores = contract(keys, q_rows, 1, 1)
    early = (reach - 1) * RUN
    k_early = lax.broadcasted_iota(jnp.int32, (early, count), 0)
    k_own = lax.broadcasted_iota(jnp.int32, (RUN, count), 0)
    scores = jnp.concatenate(
        [
            jnp.where(k_early >= doc_start, scores[:early], NEGATIVE),
            jnp.where((k_own + early >= doc_start) & (k_own <= q_off), scores[early:], NEGATIVE),
        ],
        axis=0,
    )
    top = jnp.max(scores, axis=0, keepdims=True)
    raw = jnp.exp2((scores - top) * scaling)
    return raw, 1.0 / jnp.sum(raw, axis=0, keepdims=True)


def score_gradients(raw, one_over, values, g_rows):
    weights = raw * one_over
    grad_weights = contract(values, g_rows, 1, 1)
    row_inner = jnp.sum(weights * grad_weights, axis=0, keepdims=True)
    return weights, (weights * (grad_weights - row_inner)).astype(jnp.bfloat16)


def start_blocks(me, blocks, kv_all, sems):
    rows = blocks[0].shape[0]
    copies = []
    for k, block in enumerate(blocks):
        owner = lax.bitwise_xor(me, k)
        at = pl.ds(pl.multiple_of(owner * rows, rows), rows)
        copies.append(pltpu.make_async_copy(block, kv_all.at[at], sems.at[k]))
        copies[-1].start()
    return copies


def terms_kernel(n_ctx, heads, reach, docs, table_in, own_in, other_in, *refs):
    blocks, outs, scratch = refs[:n_ctx], refs[n_ctx : 2 * n_ctx], refs[2 * n_ctx :]
    table, qg_all, kv_all, key_win, value_win, terms, bf_buf, in_sem, out_sem, table_sem = scratch
    me, head = lax.axis_index("ctx"), lax.axis_index("head")
    both, width = blocks[0].shape
    tok_rows = both // 2
    runs_here = tok_rows // RUN
    run_rows = RUN * heads
    rows_here = tok_rows * heads

    table_copy = pltpu.make_async_copy(table_in, table, table_sem)
    table_copy.start()
    copies = start_blocks(me, blocks, kv_all, in_sem)
    for i, (source, part) in enumerate(((own_in, head), (other_in, 1 - head))):
        for w in range(2):
            for r in range(runs_here):
                at = pl.ds(pl.multiple_of(part * run_rows, run_rows), run_rows)
                copies.append(
                    pltpu.make_async_copy(
                        source.at[pl.ds(w * rows_here + r * run_rows, run_rows)],
                        qg_all.at[w, r, at],
                        in_sem.at[n_ctx + (i * 2 + w) * runs_here + r],
                    )
                )
                copies[-1].start()
    terms[...] = jnp.zeros_like(terms)
    table_copy.wait()
    for copy in copies:
        copy.wait()

    for r in range(runs_here):
        rows = run_window(table, kv_all, key_win, value_win, r, reach, runs_here, tok_rows)
        q_rows, g_rows = qg_all[0, r], qg_all[1, r]
        raw, one_over = weights_of(table, key_win[r], q_rows, r, reach, runs_here, docs, heads)
        weights, grad_scores = score_gradients(raw, one_over, value_win[r], g_rows)
        value_part = contract(weights.astype(jnp.bfloat16), g_rows, 1, 0)
        key_part = contract(grad_scores, q_rows, 1, 0) * (1.0 / math.sqrt(width))
        for j, row in enumerate(rows):
            part = slice(j * RUN, (j + 1) * RUN)
            terms[pl.ds(row, RUN), :] += key_part[part, :]
            terms[pl.ds(row + tok_rows, RUN), :] += value_part[part, :]

    out_copies = []
    for k in range(n_ctx):
        owner = lax.bitwise_xor(me, k)
        at = pl.ds(pl.multiple_of(owner * both, both), both)
        if outs[k].dtype == jnp.bfloat16:
            bf_buf[k] = terms[at, :].astype(jnp.bfloat16)
            source = bf_buf.at[k]
        else:
            source = terms.at[at]
        out_copies.append(pltpu.make_async_copy(source, outs[k], out_sem.at[k]))
        out_copies[-1].start()
    for copy in out_copies:
        copy.wait()


def gradient_terms(table, own, other, blocks, heads, reach, docs, seq_total):
    n_ctx = len(blocks)
    both, width = blocks[0].shape
    tok_rows = both // 2
    runs_here = tok_rows // RUN
    outs = []
    for k in range(n_ctx):
        leaves_first = goes_first_over_y(k) or k in (1, 2, 3)
        outs.append(jax.ShapeDtypeStruct((both, width), jnp.bfloat16 if leaves_first else jnp.float32))
    return pl.pallas_call(
        functools.partial(terms_kernel, n_ctx, heads, reach, docs),
        out_shape=outs,
        in_specs=[ANY] * (3 + n_ctx),
        out_specs=[ANY] * n_ctx,
        scratch_shapes=[
            pltpu.SMEM(table.shape, jnp.int32),
            pltpu.VMEM((2, runs_here, 2 * RUN * heads, width), jnp.bfloat16),
            pltpu.VMEM((n_ctx * both, width), jnp.bfloat16),
            pltpu.VMEM((runs_here, reach * RUN, width), jnp.bfloat16),
            pltpu.VMEM((runs_here, reach * RUN, width), jnp.bfloat16),
            pltpu.VMEM((n_ctx * both, width), jnp.float32),
            pltpu.VMEM((n_ctx, both, width), jnp.bfloat16),
            pltpu.SemaphoreType.DMA((n_ctx + 4 * runs_here,)),
            pltpu.SemaphoreType.DMA((n_ctx,)),
            pltpu.SemaphoreType.DMA,
        ],
        compiler_params=limit(seq_total),
    )(table, own, other, *blocks)


def rows_kernel(n_after, n_ctx, heads, reach, docs, table_in, own_in, *refs):
    refs = refs[n_after:]
    blocks, (att_out, qg_out), scratch = refs[:n_ctx], refs[n_ctx : n_ctx + 2], refs[n_ctx + 2 :]
    table, qg_all, kv_all, key_win, value_win, att_buf, grad_buf, in_sem, out_sem, table_sem = scratch
    me = lax.axis_index("ctx")
    both, width = blocks[0].shape
    tok_rows = both // 2
    runs_here = tok_rows // RUN
    run_rows = RUN * heads
    rows_here = tok_rows * heads

    table_copy = pltpu.make_async_copy(table_in, table, table_sem)
    table_copy.start()
    copies = start_blocks(me, blocks, kv_all, in_sem)
    copies.append(pltpu.make_async_copy(own_in, qg_all, in_sem.at[n_ctx]))
    copies[-1].start()
    table_copy.wait()
    for copy in copies:
        copy.wait()

    out_copies = []
    for r in range(runs_here):
        run_window(table, kv_all, key_win, value_win, r, reach, runs_here, tok_rows)
        here = slice(r * run_rows, (r + 1) * run_rows)
        q_rows = qg_all[here, :]
        g_rows = qg_all[rows_here + r * run_rows : rows_here + (r + 1) * run_rows, :]
        raw, one_over = weights_of(table, key_win[r], q_rows, r, reach, runs_here, docs, heads)
        attended = contract(value_win[r], raw.astype(jnp.bfloat16), 0, 0) * one_over
        att_buf[here, :] = attended.T.astype(jnp.bfloat16)
        _, grad_scores = score_gradients(raw, one_over, value_win[r], g_rows)
        query_part = contract(key_win[r], grad_scores, 0, 0) * (1.0 / math.sqrt(width))
        grad_buf[here, :] = query_part.T.astype(jnp.bfloat16)
        for i, (source, out) in enumerate(((att_buf, att_out), (grad_buf, qg_out))):
            at = pl.ds(r * run_rows, run_rows)
            out_copies.append(pltpu.make_async_copy(source.at[at], out.at[at], out_sem.at[2 * r + i]))
            out_copies[-1].start()
    for copy in out_copies:
        copy.wait()


def query_side(table, own, after, blocks, heads, reach, docs, seq_total):
    n_ctx = len(blocks)
    both, width = blocks[0].shape
    tok_rows = both // 2
    runs_here = tok_rows // RUN
    rows = own.shape[0] // 2
    return pl.pallas_call(
        functools.partial(rows_kernel, len(after), n_ctx, heads, reach, docs),
        out_shape=[jax.ShapeDtypeStruct((rows, width), jnp.bfloat16)] * 2,
        in_specs=[ANY] * (2 + len(after) + n_ctx),
        out_specs=[HBM] * 2,
        scratch_shapes=[
            pltpu.SMEM(table.shape, jnp.int32),
            pltpu.VMEM((2 * rows, width), jnp.bfloat16),
            pltpu.VMEM((n_ctx * both, width), jnp.bfloat16),
            pltpu.VMEM((runs_here, reach * RUN, width), jnp.bfloat16),
            pltpu.VMEM((runs_here, reach * RUN, width), jnp.bfloat16),
            pltpu.VMEM((rows, width), jnp.bfloat16),
            pltpu.VMEM((rows, width), jnp.bfloat16),
            pltpu.SemaphoreType.DMA((n_ctx + 1,)),
            pltpu.SemaphoreType.DMA((2 * runs_here,)),
            pltpu.SemaphoreType.DMA,
        ],
        compiler_params=limit(seq_total),
    )(table, own, *after, *blocks)


def body(n_ctx, n_head, queries, key_rows, value_rows, out_grad, doc_lengths, balance):
    tok_rows, heads, width = queries.shape
    seq_total = balance.shape[0]
    docs = doc_lengths.shape[0]
    runs_here = tok_rows // RUN
    reach = seq_total // LONGEST_SHARE // RUN + 1

    def swap(array, k):
        return lax.ppermute(array, "ctx", [(i, i ^ k) for i in range(n_ctx)])

    mine, own = pack(
        key_rows,
        value_rows,
        queries.reshape(tok_rows * heads, width),
        out_grad.reshape(tok_rows * heads, width),
        seq_total,
    )
    blocks = {0: mine}
    direct = [k for k in range(n_ctx - 1, 0, -1) if not goes_first_over_y(k)]
    for k in direct:
        blocks[k] = swap(mine, k)
    other = lax.ppermute(own, "head", [(i, n_head - 1 - i) for i in range(n_head)])
    for k in reversed(direct):
        if goes_first_over_y(k + 1):
            blocks[k + 1] = swap(blocks[k], 1)
    blocks = [blocks[k] for k in range(n_ctx)]

    place = jnp.stack([lax.axis_index("ctx"), lax.axis_index("head")]).astype(jnp.int32)
    table = make_table(place, balance, doc_lengths, blocks[1], runs_here, reach)
    terms = gradient_terms(table, own, other, blocks, heads, reach, docs, seq_total)

    far = [k for k in range(n_ctx - 2, 2, -2)]
    arrived = {k: swap(terms[k + 1], 1) for k in far}
    total = terms[0]
    for k in (2, 3, 1):
        total = total + swap(terms[k], k).astype(jnp.float32)
    after = []
    for k in far:
        pair = (terms[k] + arrived[k].astype(jnp.float32)).astype(jnp.bfloat16)
        total = total + swap(pair, k).astype(jnp.float32)
        after.append(pair)
    attended, query_grad = query_side(table, own, after, blocks, heads, reach, docs, seq_total)
    combined = total.astype(jnp.bfloat16)
    return (
        attended.reshape(tok_rows, heads, width),
        query_grad.reshape(tok_rows, heads, width),
        combined[:tok_rows],
        combined[tok_rows:],
    )


def solution(mesh):
    return jax.shard_map(
        functools.partial(body, mesh.shape["ctx"], mesh.shape["head"]),
        mesh=mesh,
        in_specs=(
            P(("seq", "ctx"), "head", None),
            P(("seq", "ctx"), None),
            P(("seq", "ctx"), None),
            P(("seq", "ctx"), "head", None),
            P("seq"),
            P("seq"),
        ),
        out_specs=(
            P(("seq", "ctx"), "head", None),
            P(("seq", "ctx"), "head", None),
            P(("seq", "ctx"), None),
            P(("seq", "ctx"), None),
        ),
        check_vma=False,
    )
```

time: 43.8 us -> 38.1 us (0.87)
  waiting for transfers between devices: 11.8 us -> 7.15 us
  Pallas kernels: 5.51 us -> 9.55 us
  starting transfers between devices: 21.7 us -> 19.1 us
  local copies, waits for them, and re-layouts: 3.76 us -> 1.21 us
    pallas_call x1 -> x4, Pallas kernels: 5.51 us -> 9.55 us  [the longest x1 4.19 us: gradient_terms(): pl.pallas_call(functools.partial(terms_kernel, n_ctx, heads, reach, docs)...]
    ppermute x14, starting transfers between devices: 20.2 us -> 16.1 us  [swap(): return lax.ppermute(array, 'ctx', [(i, i ^ k) for i in range(n_ctx)])]
    ppermute x1, waiting for transfers between devices: 2.77 us -> 0.01 us  [body(): lax.ppermute(own, 'head', [(i, n_head - 1 - i) for i in range(n_head)])]
    ppermute x14, waiting for transfers between devices: 9.05 us -> 7.15 us  [swap(): return lax.ppermute(array, 'ctx', [(i, i ^ k) for i in range(n_ctx)])]
    unnamed x9 -> x4, local copies, waits for them, and re-layouts: 2.36 us -> 0.58 us
    ppermute x1, starting transfers between devices: 1.56 us -> 3 us  [body(): lax.ppermute(own, 'head', [(i, n_head - 1 - i) for i in range(n_head)])]
    concatenate x1 -> x0, local copies, waits for them, and re-layouts: 0.77 us -> none  [body(): mine = jnp.concatenate([key_rows, value_rows], axis=1)]
  transfers between devices with their start and end apart: 15 -> 15, of which waited for: 9 -> 6; matrix products, arithmetic and copies ran while one was open for 0% -> 0% of each run, Pallas kernels for 0% -> 11%
where the time goes in v2:
time: 38.1 us; the launch traced here: 37.9 us
  starting transfers between devices  19.1 us (50%)
  Pallas kernels  9.55 us (25%)
  waiting for transfers between devices  7.15 us (19%)
  local copies, waits for them, and re-layouts  1.21 us (3%)
  between operations  0.74 us (2%)
    ppermute x14, starting transfers between devices, swap(): return lax.ppermute(array, 'ctx', [(i, i ^ k) for i in range(n_ctx)])  16.1 us
    ppermute x14, waiting for transfers between devices, swap(): return lax.ppermute(array, 'ctx', [(i, i ^ k) for i in range(n_ctx)])  7.15 us
    pallas_call x1, Pallas kernels, gradient_terms(): pl.pallas_call(functools.partial(terms_kernel, n_ctx, heads, reach, docs)...  4.19 us
    pallas_call x1, Pallas kernels, query_side(): pl.pallas_call(functools.partial(rows_kernel, len(after), n_ctx, heads, r...  3.07 us
    ppermute x1, starting transfers between devices, body(): lax.ppermute(own, 'head', [(i, n_head - 1 - i) for i in range(n_head)])  3 us
    pallas_call x1, Pallas kernels, make_table(): pl.pallas_call(functools.partial(table_kernel, runs_here, reach), out_sha...  1.25 us
    pallas_call x1, Pallas kernels, pack(): pl.pallas_call(pack_kernel, out_shape=[jax.ShapeDtypeStruct((2 * key_rows...  1.04 us
  transfers between devices with their start and end apart: 15, of which 6 were waited for; matrix products, arithmetic and copies ran while one was open for 0% of the time, Pallas kernels for 11%

profile of v2, /device:TPU:0, one launch (start us, length us, event | category | flops | bytes accessed | tf_op | source)
XLA Modules:
  0.0 37.9 jit_solution(10270482072535506348)
XLA Ops:
  0.6 1.0 %shard_map.93 = (bf16[256,128]{1,0:T(8,128)(2,1)S(1)}, bf16[1024,128]{1,0:T(8,128)(2,1)S(1)}) custom-call(bf16[128,128]{1,0:T(8,128)(2,1)} %key_rows.1, bf16[128,128]{1,0:T(8,128)(2,1)} %value_rows.1, bf16[512,128]{1,0:T(8,128)(2,1)} %bitcast.6, bf16[512,128]{1,0:T(8,128)(2,1)} %bitcast.7), custom_call_target="tpu_custom_call" | custom-call | tf_op jit(solution)/shard_map/pallas_call | solution.py:50
  1.7 3.0 %collective-permute-start.1 = (bf16[1024,128]{1,0:T(8,128)(2,1)S(1)}, bf16[1024,128]{1,0:T(8,128)(2,1)S(1)}, u32[]{:S(2)}, u32[]{:S(2)}) collective-permute-start(bf16[1024,128]{1,0:T(8,128)(2,1)S(1)} %get-tuple-element.17.own_in), channel_id=1, source_target_pairs={{0,1},{1,0},{2,3},{3,2},{4,5},{5,4},{6,7},{7,6},{8,9},{9,8},{10,11... | collective-permute-start | bytes 786440 | tf_op jit(solution)/shard_map/ppermute | solution.py:344
  4.7 3.6 %collective-permute-start.6 = (bf16[256,128]{1,0:T(8,128)(2,1)S(1)}, bf16[256,128]{1,0:T(8,128)(2,1)S(1)}, u32[]{:S(2)}, u32[]{:S(2)}) collective-permute-start(bf16[256,128]{1,0:T(8,128)(2,1)S(1)} %get-tuple-element.16.refs_0_.refs_2_), channel_id=1, source_target_pairs={{0,12},{2,14},{4,8},{6,10},{8,4},{10,6},{12,0},{14,2},{1,13},{3,15... | collective-permute-start | bytes 196616 | tf_op jit(solution)/shard_map/ppermute | solution.py:331
  8.3 0.0 collective-permute-start.4
  8.3 1.5 %collective-permute-start = (bf16[256,128]{1,0:T(8,128)(2,1)S(1)}, bf16[256,128]{1,0:T(8,128)(2,1)S(1)}, u32[]{:S(2)}, u32[]{:S(2)}) collective-permute-start(bf16[256,128]{1,0:T(8,128)(2,1)S(1)} %get-tuple-element.16.refs_0_.refs_2_), channel_id=1, source_target_pairs={{0,2},{2,0},{4,6},{6,4},{8,10},{10,8},{12,14},{14,12},{1,3},{3,1},... | collective-permute-start | bytes 196616 | tf_op jit(solution)/shard_map/ppermute | solution.py:331
  9.8 0.7 %collective-permute-start.3 = (bf16[256,128]{1,0:T(8,128)(2,1)S(1)}, bf16[256,128]{1,0:T(8,128)(2,1)S(1)}, u32[]{:S(2)}, u32[]{:S(2)}) collective-permute-start(bf16[256,128]{1,0:T(8,128)(2,1)S(1)} %get-tuple-element.16.refs_0_.refs_2_), channel_id=1, source_target_pairs={{0,6},{2,4},{4,2},{6,0},{8,14},{10,12},{12,10},{14,8},{1,7},{3,5},... | collective-permute-start | bytes 196616 | tf_op jit(solution)/shard_map/ppermute | solution.py:331
  10.5 0.0 copy-start
  10.5 1.0 %collective-permute-done.6.refs_6_.refs_8_ = bf16[256,128]{1,0:T(8,128)(2,1)S(1)} collective-permute-done((bf16[256,128]{1,0:T(8,128)(2,1)S(1)}, bf16[256,128]{1,0:T(8,128)(2,1)S(1)}, u32[]{:S(2)}, u32[]{:S(2)}) %collective-permute-start.6) | collective-permute-done | bytes 65568 | tf_op jit(solution)/shard_map/ppermute | solution.py:331
  11.6 0.2 collective-permute-start.2
  11.8 1.9 %collective-permute-done.4.refs_4_.refs_6_ = bf16[256,128]{1,0:T(8,128)(2,1)S(1)} collective-permute-done((bf16[256,128]{1,0:T(8,128)(2,1)S(1)}, bf16[256,128]{1,0:T(8,128)(2,1)S(1)}, u32[]{:S(2)}, u32[]{:S(2)}) %collective-permute-start.4) | collective-permute-done | bytes 65568 | tf_op jit(solution)/shard_map/ppermute | solution.py:331
  13.7 1.5 %collective-permute-start.7 = (bf16[256,128]{1,0:T(8,128)(2,1)S(1)}, bf16[256,128]{1,0:T(8,128)(2,1)S(1)}, u32[]{:S(2)}, u32[]{:S(2)}) collective-permute-start(bf16[256,128]{1,0:T(8,128)(2,1)S(1)} %collective-permute-done.6.refs_6_.refs_8_), channel_id=1, source_target_pairs={{0,2},{2,0},{4,6},{6,4},{8,10},{10,8},{12,14},{14,12},{1,3},{3,1},... | collective-permute-start | bytes 196616 | tf_op jit(solution)/shard_map/ppermute | solution.py:331
  15.2 0.0 collective-permute-done.after.refs_1_.refs_3_
  15.2 0.5 %collective-permute-start.5 = (bf16[256,128]{1,0:T(8,128)(2,1)S(1)}, bf16[256,128]{1,0:T(8,128)(2,1)S(1)}, u32[]{:S(2)}, u32[]{:S(2)}) collective-permute-start(bf16[256,128]{1,0:T(8,128)(2,1)S(1)} %collective-permute-done.4.refs_4_.refs_6_), channel_id=1, source_target_pairs={{0,2},{2,0},{4,6},{6,4},{8,10},{10,8},{12,14},{14,12},{1,3},{3,1},... | collective-permute-start | bytes 196616 | tf_op jit(solution)/shard_map/ppermute | solution.py:331
  15.7 0.0 copy-start.1
  15.7 0.1 pad_add_fusion.place
  15.8 0.0 copy-done
  15.8 0.6 %copy-done.1 = s32[8]{0:T(128)S(1)} copy-done((s32[8]{0:T(128)S(1)}, s32[8]{0:T(128)}, u32[]{:S(2)}) %copy-start.1) | copy-done | bytes 56
  16.4 1.3 %shard_map.94.table_in = s32[128]{0:T(128)S(1)} custom-call(s32[2]{0:T(128)S(1)} %pad_add_fusion.place, s32[1024]{0:T(1024)S(1)} %copy-done, s32[8]{0:T(128)S(1)} %copy-done.1, bf16[256,128]{1,0:T(8,128)(2,1)S(1)} %collective-permute-done.after.refs_1_.refs_3_), custom_call_target="tpu_custom_call" | custom-call | tf_op jit(solution)/shard_map/pallas_call | solution.py:96
  17.7 0.0 collective-permute-done.3.refs_3_.refs_5_
  17.7 0.0 collective-permute-done.2.refs_2_.refs_4_
  17.7 0.7 %collective-permute-done.7.refs_7_.refs_9_ = bf16[256,128]{1,0:T(8,128)(2,1)S(1)} collective-permute-done((bf16[256,128]{1,0:T(8,128)(2,1)S(1)}, bf16[256,128]{1,0:T(8,128)(2,1)S(1)}, u32[]{:S(2)}, u32[]{:S(2)}) %collective-permute-start.7) | collective-permute-done | bytes 65568 | tf_op jit(solution)/shard_map/ppermute | solution.py:331
  18.4 1.1 %collective-permute-done.5.refs_5_.refs_7_ = bf16[256,128]{1,0:T(8,128)(2,1)S(1)} collective-permute-done((bf16[256,128]{1,0:T(8,128)(2,1)S(1)}, bf16[256,128]{1,0:T(8,128)(2,1)S(1)}, u32[]{:S(2)}, u32[]{:S(2)}) %collective-permute-start.5) | collective-permute-done | bytes 65568 | tf_op jit(solution)/shard_map/ppermute | solution.py:331
  19.5 0.0 collective-permute-done.1.other_in
  19.5 4.2 %shard_map.95 = (f32[256,128]{1,0:T(8,128)S(1)}, bf16[256,128]{1,0:T(8,128)(2,1)S(1)}, bf16[256,128]{1,0:T(8,128)(2,1)S(1)}, bf16[256,128]{1,0:T(8,128)(2,1)S(1)...) custom-call(s32[128]{0:T(128)S(1)} %shard_map.94.table_in, ...), custom_call_target="tpu_custom_call" | custom-call | tf_op jit(solution)/shard_map/pallas_call | solution.py:235
  23.7 0.8 %collective-permute-start.8 = (bf16[256,128]{1,0:T(8,128)(2,1)S(1)}, bf16[256,128]{1,0:T(8,128)(2,1)S(1)}, u32[]{:S(2)}, u32[]{:S(2)}) collective-permute-start(bf16[256,128]{1,0:T(8,128)(2,1)S(1)} %get-tuple-element.19), channel_id=1, source_target_pairs={{0,2},{2,0},{4,6},{6,4},{8,10},{10,8},{12,14},{14,12},{1,3},{3,1},... | collective-permute-start | bytes 196616 | tf_op jit(solution)/shard_map/ppermute | solution.py:331
  24.5 1.3 %collective-permute-start.9 = (bf16[256,128]{1,0:T(8,128)(2,1)S(1)}, bf16[256,128]{1,0:T(8,128)(2,1)S(1)}, u32[]{:S(2)}, u32[]{:S(2)}) collective-permute-start(bf16[256,128]{1,0:T(8,128)(2,1)S(1)} %get-tuple-element.21), channel_id=1, source_target_pairs={{0,2},{2,0},{4,6},{6,4},{8,10},{10,8},{12,14},{14,12},{1,3},{3,1},... | collective-permute-start | bytes 196616 | tf_op jit(solution)/shard_map/ppermute | solution.py:331
  25.8 0.0 collective-permute-start.10
  25.8 2.2 %collective-permute-start.11 = (bf16[256,128]{1,0:T(8,128)(2,1)S(1)}, bf16[256,128]{1,0:T(8,128)(2,1)S(1)}, u32[]{:S(2)}, u32[]{:S(2)}) collective-permute-start(bf16[256,128]{1,0:T(8,128)(2,1)S(1)} %get-tuple-element.26), channel_id=1, source_target_pairs={{0,6},{2,4},{4,2},{6,0},{8,14},{10,12},{12,10},{14,8},{1,7},{3,5},... | collective-permute-start | bytes 196616 | tf_op jit(solution)/shard_map/ppermute | solution.py:331
  27.9 1.3 %collective-permute-start.12 = (bf16[256,128]{1,0:T(8,128)(2,1)S(1)}, bf16[256,128]{1,0:T(8,128)(2,1)S(1)}, u32[]{:S(2)}, u32[]{:S(2)}) collective-permute-start(bf16[256,128]{1,0:T(8,128)(2,1)S(1)} %get-tuple-element.27), channel_id=1, source_target_pairs={{0,2},{2,0},{4,6},{6,4},{8,10},{10,8},{12,14},{14,12},{1,3},{3,1},... | collective-permute-start | bytes 196616 | tf_op jit(solution)/shard_map/ppermute | solution.py:331
  29.3 0.0 collective-permute-done.8
  29.3 2.4 %collective-permute-start.13 = (bf16[256,128]{1,0:T(8,128)(2,1)S(1)}, bf16[256,128]{1,0:T(8,128)(2,1)S(1)}, u32[]{:S(2)}, u32[]{:S(2)}) collective-permute-start(bf16[256,128]{1,0:T(8,128)(2,1)S(1)} %add_convert_fusion.2.refs_0_), channel_id=1, source_target_pairs={{0,12},{2,14},{4,8},{6,10},{8,4},{10,6},{12,0},{14,2},{1,13},{3,15... | collective-permute-start | bytes 196616 | tf_op jit(solution)/shard_map/ppermute | solution.py:331
  31.7 0.0 collective-permute-done.9
  31.7 0.1 collective-permute-start.14
  31.8 3.1 %shard_map.96 = (bf16[512,128]{1,0:T(8,128)(2,1)}, bf16[512,128]{1,0:T(8,128)(2,1)}) custom-call(s32[128]{0:T(128)S(1)} %shard_map.94.table_in, bf16[1024,128]{1,0:T(8,128)(2,1)S(1)} %get-tuple-element.17.own_in, bf16[256,128]{1,0:T(8,128)(2,1)S(1)} %add_convert_fusion.2.refs_0_, bf16[256,128]{1,0:T(8,128)(2,1)S(1)} %add_convert_fusion.1.refs_1_, ...), custom_call_target="tpu_custom_call" | custom-call | tf_op jit(solution)/shard_map/pallas_call | solution.py:302
  34.9 0.0 collective-permute-done.10
  34.9 0.0 collective-permute-done.11
  34.9 0.0 collective-permute-done.12
  34.9 0.5 %collective-permute-done.13 = bf16[256,128]{1,0:T(8,128)(2,1)S(1)} collective-permute-done((bf16[256,128]{1,0:T(8,128)(2,1)S(1)}, bf16[256,128]{1,0:T(8,128)(2,1)S(1)}, u32[]{:S(2)}, u32[]{:S(2)}) %collective-permute-start.13) | collective-permute-done | bytes 65568 | tf_op jit(solution)/shard_map/ppermute | solution.py:331
  35.4 1.8 %collective-permute-done.14 = bf16[256,128]{1,0:T(8,128)(2,1)S(1)} collective-permute-done((bf16[256,128]{1,0:T(8,128)(2,1)S(1)}, bf16[256,128]{1,0:T(8,128)(2,1)S(1)}, u32[]{:S(2)}, u32[]{:S(2)}) %collective-permute-start.14) | collective-permute-done | bytes 65568 | tf_op jit(solution)/shard_map/ppermute | solution.py:331
  37.3 0.1 add_convert_fusion
  37.3 0.6 %fusion = (bf16[128,128]{1,0:T(8,128)(2,1)}, bf16[128,128]{1,0:T(8,128)(2,1)}) fusion(bf16[256,128]{1,0:T(8,128)(2,1)S(1)} %add_convert_fusion), kind=kLoop, calls=%fused_computation.4 | loop fusion | bytes 131072 | tf_op jit(solution)/shard_map/slice | solution.py:370
  (2 shorter events, 0.0 us)
Async XLA Ops:
  1.7 17.8 %collective-permute-start.1 = (bf16[1024,128]{1,0:T(8,128)(2,1)S(1)}, bf16[1024,128]{1,0:T(8,128)(2,1)S(1)}, u32[]{:S(2)}, u32[]{:S(2)}) collective-permute-start(bf16[1024,128]{1,0:T(8,128)(2,1)S(1)} %get-tuple-element.17.own_in), channel_id=1, source_target_pairs={{0,1},{1,0},{2,3},{3,2},{4,5},{5,4},{6,7},{7,6},{8,9},{9,8},{10,11... | collective-permute-start | bytes 786440 | tf_op jit(solution)/shard_map/ppermute | solution.py:344
  4.7 6.9 %collective-permute-start.6 = (bf16[256,128]{1,0:T(8,128)(2,1)S(1)}, bf16[256,128]{1,0:T(8,128)(2,1)S(1)}, u32[]{:S(2)}, u32[]{:S(2)}) collective-permute-start(bf16[256,128]{1,0:T(8,128)(2,1)S(1)} %get-tuple-element.16.refs_0_.refs_2_), channel_id=1, source_target_pairs={{0,12},{2,14},{4,8},{6,10},{8,4},{10,6},{12,0},{14,2},{1,13},{3,15... | collective-permute-start | bytes 196616 | tf_op jit(solution)/shard_map/ppermute | solution.py:331
  8.3 5.4 %collective-permute-start.4 = (bf16[256,128]{1,0:T(8,128)(2,1)S(1)}, bf16[256,128]{1,0:T(8,128)(2,1)S(1)}, u32[]{:S(2)}, u32[]{:S(2)}) collective-permute-start(bf16[256,128]{1,0:T(8,128)(2,1)S(1)} %get-tuple-element.16.refs_0_.refs_2_), channel_id=1, source_target_pairs={{0,8},{2,10},{4,12},{6,14},{8,0},{10,2},{12,4},{14,6},{1,9},{3,11}... | collective-permute-start | bytes 196616 | tf_op jit(solution)/shard_map/ppermute | solution.py:331
  8.3 6.9 %collective-permute-start = (bf16[256,128]{1,0:T(8,128)(2,1)S(1)}, bf16[256,128]{1,0:T(8,128)(2,1)S(1)}, u32[]{:S(2)}, u32[]{:S(2)}) collective-permute-start(bf16[256,128]{1,0:T(8,128)(2,1)S(1)} %get-tuple-element.16.refs_0_.refs_2_), channel_id=1, source_target_pairs={{0,2},{2,0},{4,6},{6,4},{8,10},{10,8},{12,14},{14,12},{1,3},{3,1},... | collective-permute-start | bytes 196616 | tf_op jit(solution)/shard_map/ppermute | solution.py:331
  9.8 7.8 %collective-permute-start.3 = (bf16[256,128]{1,0:T(8,128)(2,1)S(1)}, bf16[256,128]{1,0:T(8,128)(2,1)S(1)}, u32[]{:S(2)}, u32[]{:S(2)}) collective-permute-start(bf16[256,128]{1,0:T(8,128)(2,1)S(1)} %get-tuple-element.16.refs_0_.refs_2_), channel_id=1, source_target_pairs={{0,6},{2,4},{4,2},{6,0},{8,14},{10,12},{12,10},{14,8},{1,7},{3,5},... | collective-permute-start | bytes 196616 | tf_op jit(solution)/shard_map/ppermute | solution.py:331
  10.5 5.3 %copy-start = (s32[1024]{0:T(1024)S(1)}, s32[1024]{0:T(1024)}, u32[]{:S(2)}) copy-start(s32[1024]{0:T(1024)} %balance.1) | copy-start | bytes 12292
  11.6 6.1 %collective-permute-start.2 = (bf16[256,128]{1,0:T(8,128)(2,1)S(1)}, bf16[256,128]{1,0:T(8,128)(2,1)S(1)}, u32[]{:S(2)}, u32[]{:S(2)}) collective-permute-start(bf16[256,128]{1,0:T(8,128)(2,1)S(1)} %get-tuple-element.16.refs_0_.refs_2_), channel_id=1, source_target_pairs={{0,4},{2,6},{4,0},{6,2},{8,12},{10,14},{12,8},{14,10},{1,5},{3,7},... | collective-permute-start | bytes 196616 | tf_op jit(solution)/shard_map/ppermute | solution.py:331
  13.7 4.6 %collective-permute-start.7 = (bf16[256,128]{1,0:T(8,128)(2,1)S(1)}, bf16[256,128]{1,0:T(8,128)(2,1)S(1)}, u32[]{:S(2)}, u32[]{:S(2)}) collective-permute-start(bf16[256,128]{1,0:T(8,128)(2,1)S(1)} %collective-permute-done.6.refs_6_.refs_8_), channel_id=1, source_target_pairs={{0,2},{2,0},{4,6},{6,4},{8,10},{10,8},{12,14},{14,12},{1,3},{3,1},... | collective-permute-start | bytes 196616 | tf_op jit(solution)/shard_map/ppermute | solution.py:331
  15.2 4.3 %collective-permute-start.5 = (bf16[256,128]{1,0:T(8,128)(2,1)S(1)}, bf16[256,128]{1,0:T(8,128)(2,1)S(1)}, u32[]{:S(2)}, u32[]{:S(2)}) collective-permute-start(bf16[256,128]{1,0:T(8,128)(2,1)S(1)} %collective-permute-done.4.refs_4_.refs_6_), channel_id=1, source_target_pairs={{0,2},{2,0},{4,6},{6,4},{8,10},{10,8},{12,14},{14,12},{1,3},{3,1},... | collective-permute-start | bytes 196616 | tf_op jit(solution)/shard_map/ppermute | solution.py:331
  15.7 0.7 %copy-start.1 = (s32[8]{0:T(128)S(1)}, s32[8]{0:T(128)}, u32[]{:S(2)}) copy-start(s32[8]{0:T(128)} %doc_lengths.1) | copy-start | bytes 100
  23.7 5.6 %collective-permute-start.8 = (bf16[256,128]{1,0:T(8,128)(2,1)S(1)}, bf16[256,128]{1,0:T(8,128)(2,1)S(1)}, u32[]{:S(2)}, u32[]{:S(2)}) collective-permute-start(bf16[256,128]{1,0:T(8,128)(2,1)S(1)} %get-tuple-element.19), channel_id=1, source_target_pairs={{0,2},{2,0},{4,6},{6,4},{8,10},{10,8},{12,14},{14,12},{1,3},{3,1},... | collective-permute-start | bytes 196616 | tf_op jit(solution)/shard_map/ppermute | solution.py:331
  24.5 7.2 %collective-permute-start.9 = (bf16[256,128]{1,0:T(8,128)(2,1)S(1)}, bf16[256,128]{1,0:T(8,128)(2,1)S(1)}, u32[]{:S(2)}, u32[]{:S(2)}) collective-permute-start(bf16[256,128]{1,0:T(8,128)(2,1)S(1)} %get-tuple-element.21), channel_id=1, source_target_pairs={{0,2},{2,0},{4,6},{6,4},{8,10},{10,8},{12,14},{14,12},{1,3},{3,1},... | collective-permute-start | bytes 196616 | tf_op jit(solution)/shard_map/ppermute | solution.py:331
  25.8 9.1 %collective-permute-start.10 = (bf16[256,128]{1,0:T(8,128)(2,1)S(1)}, bf16[256,128]{1,0:T(8,128)(2,1)S(1)}, u32[]{:S(2)}, u32[]{:S(2)}) collective-permute-start(bf16[256,128]{1,0:T(8,128)(2,1)S(1)} %get-tuple-element.25), channel_id=1, source_target_pairs={{0,4},{2,6},{4,0},{6,2},{8,12},{10,14},{12,8},{14,10},{1,5},{3,7},... | collective-permute-start | bytes 196616 | tf_op jit(solution)/shard_map/ppermute | solution.py:331
  25.8 9.1 %collective-permute-start.11 = (bf16[256,128]{1,0:T(8,128)(2,1)S(1)}, bf16[256,128]{1,0:T(8,128)(2,1)S(1)}, u32[]{:S(2)}, u32[]{:S(2)}) collective-permute-start(bf16[256,128]{1,0:T(8,128)(2,1)S(1)} %get-tuple-element.26), channel_id=1, source_target_pairs={{0,6},{2,4},{4,2},{6,0},{8,14},{10,12},{12,10},{14,8},{1,7},{3,5},... | collective-permute-start | bytes 196616 | tf_op jit(solution)/shard_map/ppermute | solution.py:331
  27.9 6.9 %collective-permute-start.12 = (bf16[256,128]{1,0:T(8,128)(2,1)S(1)}, bf16[256,128]{1,0:T(8,128)(2,1)S(1)}, u32[]{:S(2)}, u32[]{:S(2)}) collective-permute-start(bf16[256,128]{1,0:T(8,128)(2,1)S(1)} %get-tuple-element.27), channel_id=1, source_target_pairs={{0,2},{2,0},{4,6},{6,4},{8,10},{10,8},{12,14},{14,12},{1,3},{3,1},... | collective-permute-start | bytes 196616 | tf_op jit(solution)/shard_map/ppermute | solution.py:331
  29.3 6.1 %collective-permute-start.13 = (bf16[256,128]{1,0:T(8,128)(2,1)S(1)}, bf16[256,128]{1,0:T(8,128)(2,1)S(1)}, u32[]{:S(2)}, u32[]{:S(2)}) collective-permute-start(bf16[256,128]{1,0:T(8,128)(2,1)S(1)} %add_convert_fusion.2.refs_0_), channel_id=1, source_target_pairs={{0,12},{2,14},{4,8},{6,10},{8,4},{10,6},{12,0},{14,2},{1,13},{3,15... | collective-permute-start | bytes 196616 | tf_op jit(solution)/shard_map/ppermute | solution.py:331
  31.7 5.5 %collective-permute-start.14 = (bf16[256,128]{1,0:T(8,128)(2,1)S(1)}, bf16[256,128]{1,0:T(8,128)(2,1)S(1)}, u32[]{:S(2)}, u32[]{:S(2)}) collective-permute-start(bf16[256,128]{1,0:T(8,128)(2,1)S(1)} %add_convert_fusion.1.refs_1_), channel_id=1, source_target_pairs={{0,8},{2,10},{4,12},{6,14},{8,0},{10,2},{12,4},{14,6},{1,9},{3,11}... | collective-permute-start | bytes 196616 | tf_op jit(solution)/shard_map/ppermute | solution.py:331

commit v3 on v2

v3 whole, which is shorter than its diff:
```python
import functools
import math

import jax
import jax.numpy as jnp
from jax import lax
from jax.experimental import pallas as pl
from jax.experimental.pallas import tpu as pltpu
from jax.sharding import PartitionSpec as P

NEGATIVE = -1e30
RUN = 64
LONGEST_SHARE = 4

ANY = pl.BlockSpec(memory_space=pl.ANY)
VMEM = pl.BlockSpec(memory_space=pltpu.VMEM)
HBM = pl.BlockSpec(memory_space=pltpu.HBM)


def contract(a, b, dim_a, dim_b):
    return lax.dot_general(
        a, b, (((dim_a,), (dim_b,)), ((), ())), preferred_element_type=jnp.float32
    )


def limit(seq_total):
    return pltpu.CompilerParams(vmem_limit_bytes=(16 << 20) if seq_total <= 1024 else (56 << 20))


NEAR = (1, 2, 3, 4)


def high_bits(n_ctx):
    return [(1 << b, range(1 << b)) for b in range(3, n_ctx.bit_length() - 1)]


BLOCK_ORDER = (0, 4, 1, 2, 3, 7, 6, 5)
FAR_ORDER = (7, 6, 5)
SUM_ORDER = (4, 2, 3, 1)


def pack_kernel(key_rows, value_rows, q_rows, g_rows, balance, doc_lengths, kv_out, qg_out, balance_out, docs_out, sems):
    tok_rows, rows = key_rows.shape[0], q_rows.shape[0]
    copies = [
        pltpu.make_async_copy(key_rows, kv_out.at[pl.ds(0, tok_rows)], sems.at[0]),
        pltpu.make_async_copy(value_rows, kv_out.at[pl.ds(tok_rows, tok_rows)], sems.at[1]),
        pltpu.make_async_copy(q_rows, qg_out.at[pl.ds(0, rows)], sems.at[2]),
        pltpu.make_async_copy(g_rows, qg_out.at[pl.ds(rows, rows)], sems.at[3]),
        pltpu.make_async_copy(balance, balance_out, sems.at[4]),
        pltpu.make_async_copy(doc_lengths, docs_out, sems.at[5]),
    ]
    for copy in copies:
        copy.start()
    for copy in copies:
        copy.wait()


def pack(key_rows, value_rows, q_rows, g_rows, balance, doc_lengths):
    return pl.pallas_call(
        pack_kernel,
        out_shape=[
            jax.ShapeDtypeStruct((2 * key_rows.shape[0], key_rows.shape[1]), jnp.bfloat16),
            jax.ShapeDtypeStruct((2 * q_rows.shape[0], q_rows.shape[1]), jnp.bfloat16),
            jax.ShapeDtypeStruct(balance.shape, jnp.int32),
            jax.ShapeDtypeStruct(doc_lengths.shape, jnp.int32),
        ],
        in_specs=[ANY] * 6,
        out_specs=[ANY] * 4,
        scratch_shapes=[pltpu.SemaphoreType.DMA((6,))],
        compiler_params=limit(balance.shape[0]),
    )(
        *[
            pltpu.with_memory_space_constraint(a, pltpu.HBM)
            for a in (key_rows, value_rows, q_rows, g_rows, balance, doc_lengths)
        ]
    )


def start_lists(balance_in, docs_in, lists):
    balance, doc_lengths, _, sems = lists
    copies = [
        pltpu.make_async_copy(balance_in, balance, sems.at[0]),
        pltpu.make_async_copy(docs_in, doc_lengths, sems.at[1]),
    ]
    for copy in copies:
        copy.start()
    return copies


def finish_lists(copies, lists):
    balance, _, slot_of, _ = lists
    runs = slot_of.shape[0]
    for copy in copies:
        copy.wait()

    def note(s, carry):
        slot_of[lax.shift_right_logical(balance[s * RUN], 6)] = s
        return carry

    lax.fori_loop(0, runs, note, 0, unroll=runs <= 16)


def run_window(me, lists, kv_all, key_win, value_win, r, reach, runs_here, tok_rows):
    balance, _, slot_of, _ = lists
    place_run = lax.shift_right_logical(balance[(me * runs_here + r) * RUN], 6)
    rows = []
    for j in range(reach):
        slot = slot_of[jnp.maximum(place_run - (reach - 1) + j, 0)]
        row = lax.div(slot, runs_here) * (2 * tok_rows) + lax.rem(slot, runs_here) * RUN
        row = pl.multiple_of(row, RUN)
        rows.append(row)
        key_win[r, j * RUN : (j + 1) * RUN, :] = kv_all[pl.ds(row, RUN), :]
        value_win[r, j * RUN : (j + 1) * RUN, :] = kv_all[pl.ds(row + tok_rows, RUN), :]
    return place_run, rows


def weights_of(doc_lengths, place_run, keys, q_rows, reach, heads):
    count = q_rows.shape[0]
    scaling = math.log2(math.e) / math.sqrt(keys.shape[1])
    lane = lax.broadcasted_iota(jnp.int32, (1, count), 1)
    q_off = lax.div(lax.rem(lane, RUN * heads), heads)
    q_pos = place_run * RUN + q_off
    doc_start = jnp.zeros_like(q_pos)
    doc_end = jnp.int32(0)
    for d in range(doc_lengths.shape[0]):
        doc_end = doc_end + doc_lengths[d]
        doc_start = jnp.where(doc_end <= q_pos, doc_end, doc_start)
    doc_start = doc_start - (place_run - (reach - 1)) * RUN
    scores = contract(keys, q_rows, 1, 1)
    early = (reach - 1) * RUN
    k_early = lax.broadcasted_iota(jnp.int32, (early, count), 0)
    k_own = lax.broadcasted_iota(jnp.int32, (RUN, count), 0)
    scores = jnp.concatenate(
        [
            jnp.where(k_early >= doc_start, scores[:early], NEGATIVE),
            jnp.where((k_own + early >= doc_start) & (k_own <= q_off), scores[early:], NEGATIVE),
        ],
        axis=0,
    )
    top = jnp.max(scores, axis=0, keepdims=True)
    raw = jnp.exp2((scores - top) * scaling)
    return raw, 1.0 / jnp.sum(raw, axis=0, keepdims=True)


def score_gradients(raw, one_over, values, g_rows):
    weights = raw * one_over
    grad_weights = contract(values, g_rows, 1, 1)
    row_inner = jnp.sum(weights * grad_weights, axis=0, keepdims=True)
    return weights, (weights * (grad_weights - row_inner)).astype(jnp.bfloat16)


def load_blocks(me, listed, blocks, kv_all):
    rows = blocks[0].shape[0]
    for k, block in zip(listed, blocks):
        owner = lax.bitwise_xor(me, k)
        kv_all[pl.ds(pl.multiple_of(owner * rows, rows), rows), :] = block[...]


def terms_kernel(listed, heads, reach, balance_in, docs_in, own_in, other_in, *refs):
    n_ctx = len(listed)
    blocks, outs, scratch = refs[:n_ctx], refs[n_ctx : 2 * n_ctx], refs[2 * n_ctx :]
    qg_all, kv_all, key_win, value_win, terms, *lists = scratch
    me, head = lax.axis_index("ctx"), lax.axis_index("head")
    both, width = blocks[0].shape
    tok_rows = both // 2
    runs_here = tok_rows // RUN
    run_rows = RUN * heads
    rows_here = tok_rows * heads

    copies = start_lists(balance_in, docs_in, lists)
    load_blocks(me, listed, blocks, kv_all)
    for source, part in ((own_in, head), (other_in, 1 - head)):
        at = pl.ds(pl.multiple_of(part * run_rows, run_rows), run_rows)
        for w in range(2):
            for r in range(runs_here):
                here = w * rows_here + r * run_rows
                qg_all[w, r, at, :] = source[here : here + run_rows, :]
    terms[...] = jnp.zeros_like(terms)
    finish_lists(copies, lists)

    for r in range(runs_here):
        place_run, rows = run_window(me, lists, kv_all, key_win, value_win, r, reach, runs_here, tok_rows)
        q_rows, g_rows = qg_all[0, r], qg_all[1, r]
        raw, one_over = weights_of(lists[1], place_run, key_win[r], q_rows, reach, heads)
        weights, grad_scores = score_gradients(raw, one_over, value_win[r], g_rows)
        value_part = contract(weights.astype(jnp.bfloat16), g_rows, 1, 0)
        key_part = contract(grad_scores, q_rows, 1, 0) * (1.0 / math.sqrt(width))
        for j, row in enumerate(rows):
            part = slice(j * RUN, (j + 1) * RUN)
            terms[pl.ds(row, RUN), :] += key_part[part, :]
            terms[pl.ds(row + tok_rows, RUN), :] += value_part[part, :]

    for k in range(n_ctx):
        owner = lax.bitwise_xor(me, k)
        at = pl.ds(pl.multiple_of(owner * both, both), both)
        outs[k][...] = terms[at, :].astype(outs[k].dtype)


def gradient_terms(balance, doc_lengths, own, other, blocks, heads, reach):
    listed, blocks = zip(*blocks)
    n_ctx = len(blocks)
    both, width = blocks[0].shape
    tok_rows = both // 2
    runs_here = tok_rows // RUN
    kept = [k for k in range(n_ctx) if k in (0, 4) or 8 <= k < n_ctx // 2 or k < min(8, n_ctx // 2) and n_ctx > 8]
    outs = [
        jax.ShapeDtypeStruct((both, width), jnp.float32 if k in kept else jnp.bfloat16) for k in range(n_ctx)
    ]
    return pl.pallas_call(
        functools.partial(terms_kernel, listed, heads, reach),
        out_shape=outs,
        in_specs=[ANY] * 2 + [VMEM] * (2 + n_ctx),
        out_specs=[VMEM] * n_ctx,
        scratch_shapes=[
            pltpu.VMEM((2, runs_here, 2 * RUN * heads, width), jnp.bfloat16),
            pltpu.VMEM((n_ctx * both, width), jnp.bfloat16),
            pltpu.VMEM((runs_here, reach * RUN, width), jnp.bfloat16),
            pltpu.VMEM((runs_here, reach * RUN, width), jnp.bfloat16),
            pltpu.VMEM((n_ctx * both, width), jnp.float32),
            pltpu.SMEM(balance.shape, jnp.int32),
            pltpu.SMEM(doc_lengths.shape, jnp.int32),
            pltpu.SMEM((balance.shape[0] // RUN,), jnp.int32),
            pltpu.SemaphoreType.DMA((2,)),
        ],
        compiler_params=limit(balance.shape[0]),
    )(balance, doc_lengths, own, other, *blocks)


def rows_kernel(n_after, listed, heads, reach, balance_in, docs_in, own_in, *refs):
    refs = refs[n_after:]
    n_ctx = len(listed)
    blocks, (att_out, qg_out), scratch = refs[:n_ctx], refs[n_ctx : n_ctx + 2], refs[n_ctx + 2 :]
    kv_all, key_win, value_win, att_buf, grad_buf, out_sem, *lists = scratch
    me = lax.axis_index("ctx")
    both, width = blocks[0].shape
    tok_rows = both // 2
    runs_here = tok_rows // RUN
    run_rows = RUN * heads
    rows_here = tok_rows * heads

    copies = start_lists(balance_in, docs_in, lists)
    load_blocks(me, listed, blocks, kv_all)
    finish_lists(copies, lists)

    out_copies = []
    for r in range(runs_here):
        place_run, _ = run_window(me, lists, kv_all, key_win, value_win, r, reach, runs_here, tok_rows)
        here = slice(r * run_rows, (r + 1) * run_rows)
        q_rows = own_in[here, :]
        g_rows = own_in[rows_here + r * run_rows : rows_here + (r + 1) * run_rows, :]
        raw, one_over = weights_of(lists[1], place_run, key_win[r], q_rows, reach, heads)
        attended = contract(value_win[r], raw.astype(jnp.bfloat16), 0, 0) * one_over
        att_buf[here, :] = attended.T.astype(jnp.bfloat16)
        _, grad_scores = score_gradients(raw, one_over, value_win[r], g_rows)
        query_part = contract(key_win[r], grad_scores, 0, 0) * (1.0 / math.sqrt(width))
        grad_buf[here, :] = query_part.T.astype(jnp.bfloat16)
        for i, (source, out) in enumerate(((att_buf, att_out), (grad_buf, qg_out))):
            at = pl.ds(r * run_rows, run_rows)
            out_copies.append(pltpu.make_async_copy(source.at[at], out.at[at], out_sem.at[2 * r + i]))
            out_copies[-1].start()
    for copy in out_copies:
        copy.wait()


def query_side(balance, doc_lengths, own, after, blocks, heads, reach):
    listed, blocks = zip(*blocks)
    n_ctx = len(blocks)
    both, width = blocks[0].shape
    tok_rows = both // 2
    runs_here = tok_rows // RUN
    rows = own.shape[0] // 2
    return pl.pallas_call(
        functools.partial(rows_kernel, len(after), listed, heads, reach),
        out_shape=[jax.ShapeDtypeStruct((rows, width), jnp.bfloat16)] * 2,
        in_specs=[ANY, ANY, VMEM] + [ANY] * len(after) + [VMEM] * n_ctx,
        out_specs=[HBM] * 2,
        scratch_shapes=[
            pltpu.VMEM((n_ctx * both, width), jnp.bfloat16),
            pltpu.VMEM((runs_here, reach * RUN, width), jnp.bfloat16),
            pltpu.VMEM((runs_here, reach * RUN, width), jnp.bfloat16),
            pltpu.VMEM((rows, width), jnp.bfloat16),
            pltpu.VMEM((rows, width), jnp.bfloat16),
            pltpu.SemaphoreType.DMA((2 * runs_here,)),
            pltpu.SMEM(balance.shape, jnp.int32),
            pltpu.SMEM(doc_lengths.shape, jnp.int32),
            pltpu.SMEM((balance.shape[0] // RUN,), jnp.int32),
            pltpu.SemaphoreType.DMA((2,)),
        ],
        compiler_params=limit(balance.shape[0]),
    )(balance, doc_lengths, own, *after, *blocks)


def body(n_ctx, n_head, queries, key_rows, value_rows, out_grad, doc_lengths, balance):
    tok_rows, heads, width = queries.shape
    seq_total = balance.shape[0]
    reach = seq_total // LONGEST_SHARE // RUN + 1

    def swap(array, k):
        return lax.ppermute(array, "ctx", [(i, i ^ k) for i in range(n_ctx)])

    mine, own, balance, doc_lengths = pack(
        key_rows,
        value_rows,
        queries.reshape(tok_rows * heads, width),
        out_grad.reshape(tok_rows * heads, width),
        balance,
        doc_lengths,
    )
    blocks = {0: mine}
    other = lax.ppermute(own, "head", [(i, n_head - 1 - i) for i in range(n_head)])
    for k in (4, 1, 2, 3):
        blocks[k] = swap(mine, k)
    for k in FAR_ORDER:
        blocks[k] = swap(blocks[4], k - 4)
    for bit, below in high_bits(n_ctx):
        for k in below:
            blocks[bit + k] = swap(blocks[k], bit)

    listed = BLOCK_ORDER + tuple(range(8, n_ctx))
    blocks = [(k, blocks[k]) for k in listed]
    terms = list(gradient_terms(balance, doc_lengths, own, other, blocks, heads, reach))

    for bit, below in reversed(high_bits(n_ctx)):
        for k in below:
            terms[k] = terms[k] + swap(terms[bit + k].astype(jnp.bfloat16), bit).astype(jnp.float32)
    far = terms[4]
    for k in FAR_ORDER:
        far = far + swap(terms[k].astype(jnp.bfloat16), k - 4).astype(jnp.float32)
    far = far.astype(jnp.bfloat16)
    total = terms[0]
    for k in SUM_ORDER:
        term = far if k == 4 else terms[k].astype(jnp.bfloat16)
        total = total + swap(term, k).astype(jnp.float32)
    after = [far]
    attended, query_grad = query_side(balance, doc_lengths, own, after, blocks, heads, reach)
    combined = total.astype(jnp.bfloat16)
    return (
        attended.reshape(tok_rows, heads, width),
        query_grad.reshape(tok_rows, heads, width),
        combined[:tok_rows],
        combined[tok_rows:],
    )


def solution(mesh):
    return jax.shard_map(
        functools.partial(body, mesh.shape["ctx"], mesh.shape["head"]),
        mesh=mesh,
        in_specs=(
            P(("seq", "ctx"), "head", None),
            P(("seq", "ctx"), None),
            P(("seq", "ctx"), None),
            P(("seq", "ctx"), "head", None),
            P("seq"),
            P("seq"),
        ),
        out_specs=(
            P(("seq", "ctx"), "head", None),
            P(("seq", "ctx"), "head", None),
            P(("seq", "ctx"), None),
            P(("seq", "ctx"), None),
        ),
        check_vma=False,
    )
```

time: 38.1 us -> 35.6 us (0.934)
  Pallas kernels: 9.55 us -> 5.96 us
  starting transfers between devices: 19.1 us -> 22.2 us
  waiting for transfers between devices: 7.15 us -> 5.94 us
  local copies, waits for them, and re-layouts: 1.21 us -> 0.63 us
    pallas_call x3 -> x2, Pallas kernels: 8.51 us -> 4.9 us  [the longest x1 2.87 us: query_side(): pl.pallas_call(functools.partial(rows_kernel, len(after), listed, heads,...]
    ppermute x14, starting transfers between devices: 16.1 us -> 19.2 us  [swap(): return lax.ppermute(array, 'ctx', [(i, i ^ k) for i in range(n_ctx)])]
    ppermute x14, waiting for transfers between devices: 7.15 us -> 5.94 us  [swap(): return lax.ppermute(array, 'ctx', [(i, i ^ k) for i in range(n_ctx)])]
    unnamed x4 -> x0, local copies, waits for them, and re-layouts: 0.58 us -> none
  transfers between devices with their start and end apart: 15 -> 15, of which waited for: 6 -> 4; matrix products, arithmetic and copies ran while one was open for 0% -> 0% of each run, Pallas kernels for 11% -> 8%
where the time goes in v3:
time: 35.6 us; the launch traced here: 35.5 us
  starting transfers between devices  22.2 us (62%)
  Pallas kernels  5.96 us (17%)
  waiting for transfers between devices  5.94 us (17%)
  between operations  0.7 us (2%)
  local copies, waits for them, and re-layouts  0.63 us (2%)
    ppermute x14, starting transfers between devices, swap(): return lax.ppermute(array, 'ctx', [(i, i ^ k) for i in range(n_ctx)])  19.2 us
    ppermute x14, waiting for transfers between devices, swap(): return lax.ppermute(array, 'ctx', [(i, i ^ k) for i in range(n_ctx)])  5.94 us
    ppermute x1, starting transfers between devices, body(): lax.ppermute(own, 'head', [(i, n_head - 1 - i) for i in range(n_head)])  3 us
    pallas_call x1, Pallas kernels, query_side(): pl.pallas_call(functools.partial(rows_kernel, len(after), listed, heads,...  2.87 us
    pallas_call x1, Pallas kernels, gradient_terms(): pl.pallas_call(functools.partial(terms_kernel, listed, heads, reach), out...  2.03 us
    pallas_call x1, Pallas kernels, pack(): pl.pallas_call(pack_kernel, out_shape=[jax.ShapeDtypeStruct((2 * key_rows...  1.06 us
  transfers between devices with their start and end apart: 15, of which 4 were waited for; matrix products, arithmetic and copies ran while one was open for 0% of the time, Pallas kernels for 8%

profile of v3, /device:TPU:0, one launch (start us, length us, event | category | flops | bytes accessed | tf_op | source)
XLA Modules:
  0.0 35.5 jit_solution(2351483939590778825)
XLA Ops:
  0.6 1.1 %shard_map.93 = (bf16[256,128]{1,0:T(8,128)(2,1)S(1)}, bf16[1024,128]{1,0:T(8,128)(2,1)S(1)}, s32[1024]{0:T(1024)S(1)}, s32[8]{0:T(128)S(1)}) custom-call(bf16[128,128]{1,0:T(8,128)(2,1)} %key_rows.1, bf16[128,128]{1,0:T(8,128)(2,1)} %value_rows.1, bf16[512,128]{1,0:T(8,128)(2,1)} %bitcast.4, bf16[512,128]{1,0:T(8,128)(2,1)} %bitcast.5, s32[1024]{0:T(1024)} %balance.1, ...), custom_call_target="tpu_custom_call" | custom-call | tf_op jit(solution)/shard_map/pallas_call | solution.py:59
  1.7 3.0 %collective-permute-start = (bf16[1024,128]{1,0:T(8,128)(2,1)S(1)}, bf16[1024,128]{1,0:T(8,128)(2,1)S(1)}, u32[]{:S(2)}, u32[]{:S(2)}) collective-permute-start(bf16[1024,128]{1,0:T(8,128)(2,1)S(1)} %get-tuple-element.20.own_in), channel_id=1, source_target_pairs={{0,1},{1,0},{2,3},{3,2},{4,5},{5,4},{6,7},{7,6},{8,9},{9,8},{10,11... | collective-permute-start | bytes 786440 | tf_op jit(solution)/shard_map/ppermute | solution.py:310
  4.7 2.6 %collective-permute-start.1 = (bf16[256,128]{1,0:T(8,128)(2,1)S(1)}, bf16[256,128]{1,0:T(8,128)(2,1)S(1)}, u32[]{:S(2)}, u32[]{:S(2)}) collective-permute-start(bf16[256,128]{1,0:T(8,128)(2,1)S(1)} %get-tuple-element.21.refs_0_.refs_1_), channel_id=1, source_target_pairs={{0,8},{2,10},{4,12},{6,14},{8,0},{10,2},{12,4},{14,6},{1,9},{3,11}... | collective-permute-start | bytes 196616 | tf_op jit(solution)/shard_map/ppermute | solution.py:299
  7.3 2.5 %collective-permute-start.4 = (bf16[256,128]{1,0:T(8,128)(2,1)S(1)}, bf16[256,128]{1,0:T(8,128)(2,1)S(1)}, u32[]{:S(2)}, u32[]{:S(2)}) collective-permute-start(bf16[256,128]{1,0:T(8,128)(2,1)S(1)} %get-tuple-element.21.refs_0_.refs_1_), channel_id=1, source_target_pairs={{0,6},{2,4},{4,2},{6,0},{8,14},{10,12},{12,10},{14,8},{1,7},{3,5},... | collective-permute-start | bytes 196616 | tf_op jit(solution)/shard_map/ppermute | solution.py:299
  9.8 0.4 %collective-permute-start.3 = (bf16[256,128]{1,0:T(8,128)(2,1)S(1)}, bf16[256,128]{1,0:T(8,128)(2,1)S(1)}, u32[]{:S(2)}, u32[]{:S(2)}) collective-permute-start(bf16[256,128]{1,0:T(8,128)(2,1)S(1)} %get-tuple-element.21.refs_0_.refs_1_), channel_id=1, source_target_pairs={{0,4},{2,6},{4,0},{6,2},{8,12},{10,14},{12,8},{14,10},{1,5},{3,7},... | collective-permute-start | bytes 196616 | tf_op jit(solution)/shard_map/ppermute | solution.py:299
  10.3 0.5 %collective-permute-start.2 = (bf16[256,128]{1,0:T(8,128)(2,1)S(1)}, bf16[256,128]{1,0:T(8,128)(2,1)S(1)}, u32[]{:S(2)}, u32[]{:S(2)}) collective-permute-start(bf16[256,128]{1,0:T(8,128)(2,1)S(1)} %get-tuple-element.21.refs_0_.refs_1_), channel_id=1, source_target_pairs={{0,2},{2,0},{4,6},{6,4},{8,10},{10,8},{12,14},{14,12},{1,3},{3,1},... | collective-permute-start | bytes 196616 | tf_op jit(solution)/shard_map/ppermute | solution.py:299
  10.8 0.0 collective-permute-done.1.refs_1_.refs_2_
  10.8 1.5 %collective-permute-start.7 = (bf16[256,128]{1,0:T(8,128)(2,1)S(1)}, bf16[256,128]{1,0:T(8,128)(2,1)S(1)}, u32[]{:S(2)}, u32[]{:S(2)}) collective-permute-start(bf16[256,128]{1,0:T(8,128)(2,1)S(1)} %collective-permute-done.1.refs_1_.refs_2_), channel_id=1, source_target_pairs={{0,2},{2,0},{4,6},{6,4},{8,10},{10,8},{12,14},{14,12},{1,3},{3,1},... | collective-permute-start | bytes 196616 | tf_op jit(solution)/shard_map/ppermute | solution.py:299
  12.3 0.7 %collective-permute-done.4.refs_4_.refs_5_ = bf16[256,128]{1,0:T(8,128)(2,1)S(1)} collective-permute-done((bf16[256,128]{1,0:T(8,128)(2,1)S(1)}, bf16[256,128]{1,0:T(8,128)(2,1)S(1)}, u32[]{:S(2)}, u32[]{:S(2)}) %collective-permute-start.4) | collective-permute-done | bytes 65568 | tf_op jit(solution)/shard_map/ppermute | solution.py:299
  13.0 1.6 %collective-permute-start.6 = (bf16[256,128]{1,0:T(8,128)(2,1)S(1)}, bf16[256,128]{1,0:T(8,128)(2,1)S(1)}, u32[]{:S(2)}, u32[]{:S(2)}) collective-permute-start(bf16[256,128]{1,0:T(8,128)(2,1)S(1)} %collective-permute-done.1.refs_1_.refs_2_), channel_id=1, source_target_pairs={{0,4},{2,6},{4,0},{6,2},{8,12},{10,14},{12,8},{14,10},{1,5},{3,7},... | collective-permute-start | bytes 196616 | tf_op jit(solution)/shard_map/ppermute | solution.py:299
  14.6 0.0 collective-permute-done.3.refs_3_.refs_4_
  14.6 1.2 %collective-permute-start.5 = (bf16[256,128]{1,0:T(8,128)(2,1)S(1)}, bf16[256,128]{1,0:T(8,128)(2,1)S(1)}, u32[]{:S(2)}, u32[]{:S(2)}) collective-permute-start(bf16[256,128]{1,0:T(8,128)(2,1)S(1)} %collective-permute-done.1.refs_1_.refs_2_), channel_id=1, source_target_pairs={{0,6},{2,4},{4,2},{6,0},{8,14},{10,12},{12,10},{14,8},{1,7},{3,5},... | collective-permute-start | bytes 196616 | tf_op jit(solution)/shard_map/ppermute | solution.py:299
  15.8 0.0 collective-permute-done.2.refs_2_.refs_3_
  15.8 0.0 collective-permute-done.7.refs_7_.refs_8_
  15.8 1.5 %collective-permute-done.6.refs_6_.refs_7_ = bf16[256,128]{1,0:T(8,128)(2,1)S(1)} collective-permute-done((bf16[256,128]{1,0:T(8,128)(2,1)S(1)}, bf16[256,128]{1,0:T(8,128)(2,1)S(1)}, u32[]{:S(2)}, u32[]{:S(2)}) %collective-permute-start.6) | collective-permute-done | bytes 65568 | tf_op jit(solution)/shard_map/ppermute | solution.py:299
  17.2 2.5 %collective-permute-done.5.refs_5_.refs_6_ = bf16[256,128]{1,0:T(8,128)(2,1)S(1)} collective-permute-done((bf16[256,128]{1,0:T(8,128)(2,1)S(1)}, bf16[256,128]{1,0:T(8,128)(2,1)S(1)}, u32[]{:S(2)}, u32[]{:S(2)}) %collective-permute-start.5) | collective-permute-done | bytes 65568 | tf_op jit(solution)/shard_map/ppermute | solution.py:299
  19.7 0.0 collective-permute-done.other_in
  19.7 2.0 %shard_map.94 = (f32[256,128]{1,0:T(8,128)S(1)}, bf16[256,128]{1,0:T(8,128)(2,1)S(1)}, bf16[256,128]{1,0:T(8,128)(2,1)S(1)}, bf16[256,128]{1,0:T(8,128)(2,1)S(1)...) custom-call(s32[1024]{0:T(1024)S(1)} %get-tuple-element.18.balance_i, ...), custom_call_target="tpu_custom_call" | custom-call | tf_op jit(solution)/shard_map/pallas_call | solution.py:209
  21.8 1.3 %collective-permute-start.8 = (bf16[256,128]{1,0:T(8,128)(2,1)S(1)}, bf16[256,128]{1,0:T(8,128)(2,1)S(1)}, u32[]{:S(2)}, u32[]{:S(2)}) collective-permute-start(bf16[256,128]{1,0:T(8,128)(2,1)S(1)} %get-tuple-element.23), channel_id=1, source_target_pairs={{0,6},{2,4},{4,2},{6,0},{8,14},{10,12},{12,10},{14,8},{1,7},{3,5},... | collective-permute-start | bytes 196616 | tf_op jit(solution)/shard_map/ppermute | solution.py:299
  23.1 1.3 %collective-permute-start.9 = (bf16[256,128]{1,0:T(8,128)(2,1)S(1)}, bf16[256,128]{1,0:T(8,128)(2,1)S(1)}, u32[]{:S(2)}, u32[]{:S(2)}) collective-permute-start(bf16[256,128]{1,0:T(8,128)(2,1)S(1)} %get-tuple-element.24), channel_id=1, source_target_pairs={{0,4},{2,6},{4,0},{6,2},{8,12},{10,14},{12,8},{14,10},{1,5},{3,7},... | collective-permute-start | bytes 196616 | tf_op jit(solution)/shard_map/ppermute | solution.py:299
  24.4 1.0 %collective-permute-start.10 = (bf16[256,128]{1,0:T(8,128)(2,1)S(1)}, bf16[256,128]{1,0:T(8,128)(2,1)S(1)}, u32[]{:S(2)}, u32[]{:S(2)}) collective-permute-start(bf16[256,128]{1,0:T(8,128)(2,1)S(1)} %get-tuple-element.25), channel_id=1, source_target_pairs={{0,2},{2,0},{4,6},{6,4},{8,10},{10,8},{12,14},{14,12},{1,3},{3,1},... | collective-permute-start | bytes 196616 | tf_op jit(solution)/shard_map/ppermute | solution.py:299
  25.3 0.4 %collective-permute-start.12 = (bf16[256,128]{1,0:T(8,128)(2,1)S(1)}, bf16[256,128]{1,0:T(8,128)(2,1)S(1)}, u32[]{:S(2)}, u32[]{:S(2)}) collective-permute-start(bf16[256,128]{1,0:T(8,128)(2,1)S(1)} %get-tuple-element.29), channel_id=1, source_target_pairs={{0,4},{2,6},{4,0},{6,2},{8,12},{10,14},{12,8},{14,10},{1,5},{3,7},... | collective-permute-start | bytes 196616 | tf_op jit(solution)/shard_map/ppermute | solution.py:299
  25.8 2.1 %collective-permute-start.13 = (bf16[256,128]{1,0:T(8,128)(2,1)S(1)}, bf16[256,128]{1,0:T(8,128)(2,1)S(1)}, u32[]{:S(2)}, u32[]{:S(2)}) collective-permute-start(bf16[256,128]{1,0:T(8,128)(2,1)S(1)} %get-tuple-element.30), channel_id=1, source_target_pairs={{0,6},{2,4},{4,2},{6,0},{8,14},{10,12},{12,10},{14,8},{1,7},{3,5},... | collective-permute-start | bytes 196616 | tf_op jit(solution)/shard_map/ppermute | solution.py:299
  27.9 0.0 collective-permute-done.8
  27.9 1.0 %collective-permute-start.14 = (bf16[256,128]{1,0:T(8,128)(2,1)S(1)}, bf16[256,128]{1,0:T(8,128)(2,1)S(1)}, u32[]{:S(2)}, u32[]{:S(2)}) collective-permute-start(bf16[256,128]{1,0:T(8,128)(2,1)S(1)} %get-tuple-element.31), channel_id=1, source_target_pairs={{0,2},{2,0},{4,6},{6,4},{8,10},{10,8},{12,14},{14,12},{1,3},{3,1},... | collective-permute-start | bytes 196616 | tf_op jit(solution)/shard_map/ppermute | solution.py:299
  28.8 0.0 collective-permute-done.9
  28.8 0.0 collective-permute-done.10
  28.9 1.7 %collective-permute-start.11 = (bf16[256,128]{1,0:T(8,128)(2,1)S(1)}, bf16[256,128]{1,0:T(8,128)(2,1)S(1)}, u32[]{:S(2)}, u32[]{:S(2)}) collective-permute-start(bf16[256,128]{1,0:T(8,128)(2,1)S(1)} %add_convert_fusion.1.refs_0_), channel_id=1, source_target_pairs={{0,8},{2,10},{4,12},{6,14},{8,0},{10,2},{12,4},{14,6},{1,9},{3,11}... | collective-permute-start | bytes 196616 | tf_op jit(solution)/shard_map/ppermute | solution.py:299
  30.6 2.9 %shard_map.95 = (bf16[512,128]{1,0:T(8,128)(2,1)}, bf16[512,128]{1,0:T(8,128)(2,1)}) custom-call(s32[1024]{0:T(1024)S(1)} %get-tuple-element.18.balance_in, s32[8]{0:T(128)S(1)} %get-tuple-element.19.docs_in, bf16[1024,128]{1,0:T(8,128)(2,1)S(1)} %get-tuple-element.20.own_in, bf16[256,128]{1,0:T(8,128)(2,1)S(1)} %add_convert_fusion.1.refs_0_, ...), custom_call_target="tpu_custom_call" | custom-call | tf_op jit(solution)/shard_map/pallas_call | solution.py:272
  33.5 0.0 collective-permute-done.12
  33.5 0.0 collective-permute-done.13
  33.5 0.0 collective-permute-done.14
  33.5 1.3 %collective-permute-done.11 = bf16[256,128]{1,0:T(8,128)(2,1)S(1)} collective-permute-done((bf16[256,128]{1,0:T(8,128)(2,1)S(1)}, bf16[256,128]{1,0:T(8,128)(2,1)S(1)}, u32[]{:S(2)}, u32[]{:S(2)}) %collective-permute-start.11) | collective-permute-done | bytes 65568 | tf_op jit(solution)/shard_map/ppermute | solution.py:299
  34.8 0.1 add_convert_fusion
  34.9 0.6 %fusion = (bf16[128,128]{1,0:T(8,128)(2,1)}, bf16[128,128]{1,0:T(8,128)(2,1)}) fusion(bf16[256,128]{1,0:T(8,128)(2,1)S(1)} %add_convert_fusion), kind=kLoop, calls=%fused_computation.2 | loop fusion | bytes 131072 | tf_op jit(solution)/shard_map/slice | solution.py:341
  (1 shorter events, 0.0 us)
Async XLA Ops:
  1.7 18.0 %collective-permute-start = (bf16[1024,128]{1,0:T(8,128)(2,1)S(1)}, bf16[1024,128]{1,0:T(8,128)(2,1)S(1)}, u32[]{:S(2)}, u32[]{:S(2)}) collective-permute-start(bf16[1024,128]{1,0:T(8,128)(2,1)S(1)} %get-tuple-element.20.own_in), channel_id=1, source_target_pairs={{0,1},{1,0},{2,3},{3,2},{4,5},{5,4},{6,7},{7,6},{8,9},{9,8},{10,11... | collective-permute-start | bytes 786440 | tf_op jit(solution)/shard_map/ppermute | solution.py:310
  4.7 6.1 %collective-permute-start.1 = (bf16[256,128]{1,0:T(8,128)(2,1)S(1)}, bf16[256,128]{1,0:T(8,128)(2,1)S(1)}, u32[]{:S(2)}, u32[]{:S(2)}) collective-permute-start(bf16[256,128]{1,0:T(8,128)(2,1)S(1)} %get-tuple-element.21.refs_0_.refs_1_), channel_id=1, source_target_pairs={{0,8},{2,10},{4,12},{6,14},{8,0},{10,2},{12,4},{14,6},{1,9},{3,11}... | collective-permute-start | bytes 196616 | tf_op jit(solution)/shard_map/ppermute | solution.py:299
  7.3 5.7 %collective-permute-start.4 = (bf16[256,128]{1,0:T(8,128)(2,1)S(1)}, bf16[256,128]{1,0:T(8,128)(2,1)S(1)}, u32[]{:S(2)}, u32[]{:S(2)}) collective-permute-start(bf16[256,128]{1,0:T(8,128)(2,1)S(1)} %get-tuple-element.21.refs_0_.refs_1_), channel_id=1, source_target_pairs={{0,6},{2,4},{4,2},{6,0},{8,14},{10,12},{12,10},{14,8},{1,7},{3,5},... | collective-permute-start | bytes 196616 | tf_op jit(solution)/shard_map/ppermute | solution.py:299
  9.8 4.7 %collective-permute-start.3 = (bf16[256,128]{1,0:T(8,128)(2,1)S(1)}, bf16[256,128]{1,0:T(8,128)(2,1)S(1)}, u32[]{:S(2)}, u32[]{:S(2)}) collective-permute-start(bf16[256,128]{1,0:T(8,128)(2,1)S(1)} %get-tuple-element.21.refs_0_.refs_1_), channel_id=1, source_target_pairs={{0,4},{2,6},{4,0},{6,2},{8,12},{10,14},{12,8},{14,10},{1,5},{3,7},... | collective-permute-start | bytes 196616 | tf_op jit(solution)/shard_map/ppermute | solution.py:299
  10.3 5.5 %collective-permute-start.2 = (bf16[256,128]{1,0:T(8,128)(2,1)S(1)}, bf16[256,128]{1,0:T(8,128)(2,1)S(1)}, u32[]{:S(2)}, u32[]{:S(2)}) collective-permute-start(bf16[256,128]{1,0:T(8,128)(2,1)S(1)} %get-tuple-element.21.refs_0_.refs_1_), channel_id=1, source_target_pairs={{0,2},{2,0},{4,6},{6,4},{8,10},{10,8},{12,14},{14,12},{1,3},{3,1},... | collective-permute-start | bytes 196616 | tf_op jit(solution)/shard_map/ppermute | solution.py:299
  10.8 5.0 %collective-permute-start.7 = (bf16[256,128]{1,0:T(8,128)(2,1)S(1)}, bf16[256,128]{1,0:T(8,128)(2,1)S(1)}, u32[]{:S(2)}, u32[]{:S(2)}) collective-permute-start(bf16[256,128]{1,0:T(8,128)(2,1)S(1)} %collective-permute-done.1.refs_1_.refs_2_), channel_id=1, source_target_pairs={{0,2},{2,0},{4,6},{6,4},{8,10},{10,8},{12,14},{14,12},{1,3},{3,1},... | collective-permute-start | bytes 196616 | tf_op jit(solution)/shard_map/ppermute | solution.py:299
  13.0 4.3 %collective-permute-start.6 = (bf16[256,128]{1,0:T(8,128)(2,1)S(1)}, bf16[256,128]{1,0:T(8,128)(2,1)S(1)}, u32[]{:S(2)}, u32[]{:S(2)}) collective-permute-start(bf16[256,128]{1,0:T(8,128)(2,1)S(1)} %collective-permute-done.1.refs_1_.refs_2_), channel_id=1, source_target_pairs={{0,4},{2,6},{4,0},{6,2},{8,12},{10,14},{12,8},{14,10},{1,5},{3,7},... | collective-permute-start | bytes 196616 | tf_op jit(solution)/shard_map/ppermute | solution.py:299
  14.6 5.2 %collective-permute-start.5 = (bf16[256,128]{1,0:T(8,128)(2,1)S(1)}, bf16[256,128]{1,0:T(8,128)(2,1)S(1)}, u32[]{:S(2)}, u32[]{:S(2)}) collective-permute-start(bf16[256,128]{1,0:T(8,128)(2,1)S(1)} %collective-permute-done.1.refs_1_.refs_2_), channel_id=1, source_target_pairs={{0,6},{2,4},{4,2},{6,0},{8,14},{10,12},{12,10},{14,8},{1,7},{3,5},... | collective-permute-start | bytes 196616 | tf_op jit(solution)/shard_map/ppermute | solution.py:299
  21.8 6.1 %collective-permute-start.8 = (bf16[256,128]{1,0:T(8,128)(2,1)S(1)}, bf16[256,128]{1,0:T(8,128)(2,1)S(1)}, u32[]{:S(2)}, u32[]{:S(2)}) collective-permute-start(bf16[256,128]{1,0:T(8,128)(2,1)S(1)} %get-tuple-element.23), channel_id=1, source_target_pairs={{0,6},{2,4},{4,2},{6,0},{8,14},{10,12},{12,10},{14,8},{1,7},{3,5},... | collective-permute-start | bytes 196616 | tf_op jit(solution)/shard_map/ppermute | solution.py:299
  23.1 5.8 %collective-permute-start.9 = (bf16[256,128]{1,0:T(8,128)(2,1)S(1)}, bf16[256,128]{1,0:T(8,128)(2,1)S(1)}, u32[]{:S(2)}, u32[]{:S(2)}) collective-permute-start(bf16[256,128]{1,0:T(8,128)(2,1)S(1)} %get-tuple-element.24), channel_id=1, source_target_pairs={{0,4},{2,6},{4,0},{6,2},{8,12},{10,14},{12,8},{14,10},{1,5},{3,7},... | collective-permute-start | bytes 196616 | tf_op jit(solution)/shard_map/ppermute | solution.py:299
  24.4 4.5 %collective-permute-start.10 = (bf16[256,128]{1,0:T(8,128)(2,1)S(1)}, bf16[256,128]{1,0:T(8,128)(2,1)S(1)}, u32[]{:S(2)}, u32[]{:S(2)}) collective-permute-start(bf16[256,128]{1,0:T(8,128)(2,1)S(1)} %get-tuple-element.25), channel_id=1, source_target_pairs={{0,2},{2,0},{4,6},{6,4},{8,10},{10,8},{12,14},{14,12},{1,3},{3,1},... | collective-permute-start | bytes 196616 | tf_op jit(solution)/shard_map/ppermute | solution.py:299
  25.3 8.1 %collective-permute-start.12 = (bf16[256,128]{1,0:T(8,128)(2,1)S(1)}, bf16[256,128]{1,0:T(8,128)(2,1)S(1)}, u32[]{:S(2)}, u32[]{:S(2)}) collective-permute-start(bf16[256,128]{1,0:T(8,128)(2,1)S(1)} %get-tuple-element.29), channel_id=1, source_target_pairs={{0,4},{2,6},{4,0},{6,2},{8,12},{10,14},{12,8},{14,10},{1,5},{3,7},... | collective-permute-start | bytes 196616 | tf_op jit(solution)/shard_map/ppermute | solution.py:299
  25.8 7.7 %collective-permute-start.13 = (bf16[256,128]{1,0:T(8,128)(2,1)S(1)}, bf16[256,128]{1,0:T(8,128)(2,1)S(1)}, u32[]{:S(2)}, u32[]{:S(2)}) collective-permute-start(bf16[256,128]{1,0:T(8,128)(2,1)S(1)} %get-tuple-element.30), channel_id=1, source_target_pairs={{0,6},{2,4},{4,2},{6,0},{8,14},{10,12},{12,10},{14,8},{1,7},{3,5},... | collective-permute-start | bytes 196616 | tf_op jit(solution)/shard_map/ppermute | solution.py:299
  27.9 5.6 %collective-permute-start.14 = (bf16[256,128]{1,0:T(8,128)(2,1)S(1)}, bf16[256,128]{1,0:T(8,128)(2,1)S(1)}, u32[]{:S(2)}, u32[]{:S(2)}) collective-permute-start(bf16[256,128]{1,0:T(8,128)(2,1)S(1)} %get-tuple-element.31), channel_id=1, source_target_pairs={{0,2},{2,0},{4,6},{6,4},{8,10},{10,8},{12,14},{14,12},{1,3},{3,1},... | collective-permute-start | bytes 196616 | tf_op jit(solution)/shard_map/ppermute | solution.py:299
  28.9 5.9 %collective-permute-start.11 = (bf16[256,128]{1,0:T(8,128)(2,1)S(1)}, bf16[256,128]{1,0:T(8,128)(2,1)S(1)}, u32[]{:S(2)}, u32[]{:S(2)}) collective-permute-start(bf16[256,128]{1,0:T(8,128)(2,1)S(1)} %add_convert_fusion.1.refs_0_), channel_id=1, source_target_pairs={{0,8},{2,10},{4,12},{6,14},{8,0},{10,2},{12,4},{14,6},{1,9},{3,11}... | collective-permute-start | bytes 196616 | tf_op jit(solution)/shard_map/ppermute | solution.py:299

commit v4 on v3

--- a/solution.py
+++ b/solution.py
@@ -27,16 +27,15 @@
     return pltpu.CompilerParams(vmem_limit_bytes=(16 << 20) if seq_total <= 1024 else (56 << 20))
 
 
-NEAR = (1, 2, 3, 4)
+GATHER_FROM = {1: 0, 2: 0, 3: 0, 4: 0, 5: 4, 6: 4, 7: 4}
+SCATTER_OVER = {1: 0, 2: 0, 3: 0, 4: 0, 5: 4, 6: 4, 7: 4}
+BLOCK_ORDER = (0, 6, 3, 5, 2, 4, 1, 7)
+GATHER_ORDER = (4, 1, 2, 3, 6, 5, 7)
+SUM_ORDER = (4, 3, 1, 2, 7, 6, 5)
 
 
 def high_bits(n_ctx):
     return [(1 << b, range(1 << b)) for b in range(3, n_ctx.bit_length() - 1)]
-
-
-BLOCK_ORDER = (0, 4, 1, 2, 3, 7, 6, 5)
-FAR_ORDER = (7, 6, 5)
-SUM_ORDER = (4, 2, 3, 1)
 
 
 def pack_kernel(key_rows, value_rows, q_rows, g_rows, balance, doc_lengths, kv_out, qg_out, balance_out, docs_out, sems):
@@ -202,7 +201,7 @@
     both, width = blocks[0].shape
     tok_rows = both // 2
     runs_here = tok_rows // RUN
-    kept = [k for k in range(n_ctx) if k in (0, 4) or 8 <= k < n_ctx // 2 or k < min(8, n_ctx // 2) and n_ctx > 8]
+    kept = [0, *SCATTER_OVER.values()] if n_ctx == 8 else range(n_ctx // 2)
     outs = [
         jax.ShapeDtypeStruct((both, width), jnp.float32 if k in kept else jnp.bfloat16) for k in range(n_ctx)
     ]
@@ -308,10 +307,8 @@
     )
     blocks = {0: mine}
     other = lax.ppermute(own, "head", [(i, n_head - 1 - i) for i in range(n_head)])
-    for k in (4, 1, 2, 3):
-        blocks[k] = swap(mine, k)
-    for k in FAR_ORDER:
-        blocks[k] = swap(blocks[4], k - 4)
+    for k in GATHER_ORDER:
+        blocks[k] = swap(blocks[GATHER_FROM[k]], k ^ GATHER_FROM[k])
     for bit, below in high_bits(n_ctx):
         for k in below:
             blocks[bit + k] = swap(blocks[k], bit)
@@ -323,15 +320,18 @@
     for bit, below in reversed(high_bits(n_ctx)):
         for k in below:
             terms[k] = terms[k] + swap(terms[bit + k].astype(jnp.bfloat16), bit).astype(jnp.float32)
-    far = terms[4]
-    for k in FAR_ORDER:
-        far = far + swap(terms[k].astype(jnp.bfloat16), k - 4).astype(jnp.float32)
-    far = far.astype(jnp.bfloat16)
-    total = terms[0]
-    for k in SUM_ORDER:
-        term = far if k == 4 else terms[k].astype(jnp.bfloat16)
-        total = total + swap(term, k).astype(jnp.float32)
-    after = [far]
+    sums = {}
+
+    def summed(k):
+        total = terms[k]
+        for child in SUM_ORDER:
+            if SCATTER_OVER[child] == k:
+                sums[child] = summed(child).astype(jnp.bfloat16)
+                total = total + swap(sums[child], child ^ k).astype(jnp.float32)
+        return total
+
+    total = summed(0)
+    after = [sums[k] for k in sums if k in SCATTER_OVER.values()]
     attended, query_grad = query_side(balance, doc_lengths, own, after, blocks, heads, reach)
     combined = total.astype(jnp.bfloat16)
     return (

time: 35.6 us -> 33.6 us (0.944)
  waiting for transfers between devices: 5.94 us -> 3 us
  starting transfers between devices: 22.2 us -> 23 us
    ppermute x14, waiting for transfers between devices: 5.94 us -> 2.99 us  [swap(): return lax.ppermute(array, 'ctx', [(i, i ^ k) for i in range(n_ctx)])]
    ppermute x14, starting transfers between devices: 19.2 us -> 20 us  [swap(): return lax.ppermute(array, 'ctx', [(i, i ^ k) for i in range(n_ctx)])]
  transfers between devices with their start and end apart: 15 -> 15, of which waited for: 4 -> 5; matrix products, arithmetic and copies ran while one was open for 0% -> 0% of each run, Pallas kernels for 8% -> 9%
where the time goes in v4:
time: 33.6 us; the launch traced here: 33.4 us
  starting transfers between devices  23 us (68%)
  Pallas kernels  5.96 us (18%)
  waiting for transfers between devices  3 us (9%)
  between operations  0.71 us (2%)
  local copies, waits for them, and re-layouts  0.63 us (2%)
    ppermute x14, starting transfers between devices, swap(): return lax.ppermute(array, 'ctx', [(i, i ^ k) for i in range(n_ctx)])  20 us
    ppermute x1, starting transfers between devices, body(): lax.ppermute(own, 'head', [(i, n_head - 1 - i) for i in range(n_head)])  3 us
    ppermute x14, waiting for transfers between devices, swap(): return lax.ppermute(array, 'ctx', [(i, i ^ k) for i in range(n_ctx)])  2.99 us
    pallas_call x1, Pallas kernels, query_side(): pl.pallas_call(functools.partial(rows_kernel, len(after), listed, heads,...  2.87 us
    pallas_call x1, Pallas kernels, gradient_terms(): pl.pallas_call(functools.partial(terms_kernel, listed, heads, reach), out...  2.03 us
    pallas_call x1, Pallas kernels, pack(): pl.pallas_call(pack_kernel, out_shape=[jax.ShapeDtypeStruct((2 * key_rows...  1.06 us
  transfers between devices with their start and end apart: 15, of which 5 were waited for; matrix products, arithmetic and copies ran while one was open for 0% of the time, Pallas kernels for 9%

profile of v4, /device:TPU:0, one launch (start us, length us, event | category | flops | bytes accessed | tf_op | source)
XLA Modules:
  0.0 33.4 jit_solution(4105780110270938037)
XLA Ops:
  0.6 1.1 %shard_map.93 = (bf16[256,128]{1,0:T(8,128)(2,1)S(1)}, bf16[1024,128]{1,0:T(8,128)(2,1)S(1)}, s32[1024]{0:T(1024)S(1)}, s32[8]{0:T(128)S(1)}) custom-call(bf16[128,128]{1,0:T(8,128)(2,1)} %key_rows.1, bf16[128,128]{1,0:T(8,128)(2,1)} %value_rows.1, bf16[512,128]{1,0:T(8,128)(2,1)} %bitcast.4, bf16[512,128]{1,0:T(8,128)(2,1)} %bitcast.5, s32[1024]{0:T(1024)} %balance.1, ...), custom_call_target="tpu_custom_call" | custom-call | tf_op jit(solution)/shard_map/pallas_call | solution.py:58
  1.7 3.0 %collective-permute-start = (bf16[1024,128]{1,0:T(8,128)(2,1)S(1)}, bf16[1024,128]{1,0:T(8,128)(2,1)S(1)}, u32[]{:S(2)}, u32[]{:S(2)}) collective-permute-start(bf16[1024,128]{1,0:T(8,128)(2,1)S(1)} %get-tuple-element.20.own_in), channel_id=1, source_target_pairs={{0,1},{1,0},{2,3},{3,2},{4,5},{5,4},{6,7},{7,6},{8,9},{9,8},{10,11... | collective-permute-start | bytes 786440 | tf_op jit(solution)/shard_map/ppermute | solution.py:309
  4.7 2.6 %collective-permute-start.1 = (bf16[256,128]{1,0:T(8,128)(2,1)S(1)}, bf16[256,128]{1,0:T(8,128)(2,1)S(1)}, u32[]{:S(2)}, u32[]{:S(2)}) collective-permute-start(bf16[256,128]{1,0:T(8,128)(2,1)S(1)} %get-tuple-element.21.refs_0_.refs_1_), channel_id=1, source_target_pairs={{0,8},{2,10},{4,12},{6,14},{8,0},{10,2},{12,4},{14,6},{1,9},{3,11}... | collective-permute-start | bytes 196616 | tf_op jit(solution)/shard_map/ppermute | solution.py:298
  7.3 1.5 %collective-permute-start.6 = (bf16[256,128]{1,0:T(8,128)(2,1)S(1)}, bf16[256,128]{1,0:T(8,128)(2,1)S(1)}, u32[]{:S(2)}, u32[]{:S(2)}) collective-permute-start(bf16[256,128]{1,0:T(8,128)(2,1)S(1)} %get-tuple-element.21.refs_0_.refs_1_), channel_id=1, source_target_pairs={{0,2},{2,0},{4,6},{6,4},{8,10},{10,8},{12,14},{14,12},{1,3},{3,1},... | collective-permute-start | bytes 196616 | tf_op jit(solution)/shard_map/ppermute | solution.py:298
  8.8 1.6 %collective-permute-start.5 = (bf16[256,128]{1,0:T(8,128)(2,1)S(1)}, bf16[256,128]{1,0:T(8,128)(2,1)S(1)}, u32[]{:S(2)}, u32[]{:S(2)}) collective-permute-start(bf16[256,128]{1,0:T(8,128)(2,1)S(1)} %get-tuple-element.21.refs_0_.refs_1_), channel_id=1, source_target_pairs={{0,4},{2,6},{4,0},{6,2},{8,12},{10,14},{12,8},{14,10},{1,5},{3,7},... | collective-permute-start | bytes 196616 | tf_op jit(solution)/shard_map/ppermute | solution.py:298
  10.4 0.4 %collective-permute-start.3 = (bf16[256,128]{1,0:T(8,128)(2,1)S(1)}, bf16[256,128]{1,0:T(8,128)(2,1)S(1)}, u32[]{:S(2)}, u32[]{:S(2)}) collective-permute-start(bf16[256,128]{1,0:T(8,128)(2,1)S(1)} %get-tuple-element.21.refs_0_.refs_1_), channel_id=1, source_target_pairs={{0,6},{2,4},{4,2},{6,0},{8,14},{10,12},{12,10},{14,8},{1,7},{3,5},... | collective-permute-start | bytes 196616 | tf_op jit(solution)/shard_map/ppermute | solution.py:298
  10.8 0.0 collective-permute-done.1.refs_5_.refs_6_
  10.8 2.5 %collective-permute-start.7 = (bf16[256,128]{1,0:T(8,128)(2,1)S(1)}, bf16[256,128]{1,0:T(8,128)(2,1)S(1)}, u32[]{:S(2)}, u32[]{:S(2)}) collective-permute-start(bf16[256,128]{1,0:T(8,128)(2,1)S(1)} %collective-permute-done.1.refs_5_.refs_6_), channel_id=1, source_target_pairs={{0,6},{2,4},{4,2},{6,0},{8,14},{10,12},{12,10},{14,8},{1,7},{3,5},... | collective-permute-start | bytes 196616 | tf_op jit(solution)/shard_map/ppermute | solution.py:298
  13.3 0.0 collective-permute-done.6.refs_6_.refs_7_
  13.3 0.5 %collective-permute-start.4 = (bf16[256,128]{1,0:T(8,128)(2,1)S(1)}, bf16[256,128]{1,0:T(8,128)(2,1)S(1)}, u32[]{:S(2)}, u32[]{:S(2)}) collective-permute-start(bf16[256,128]{1,0:T(8,128)(2,1)S(1)} %collective-permute-done.1.refs_5_.refs_6_), channel_id=1, source_target_pairs={{0,2},{2,0},{4,6},{6,4},{8,10},{10,8},{12,14},{14,12},{1,3},{3,1},... | collective-permute-start | bytes 196616 | tf_op jit(solution)/shard_map/ppermute | solution.py:298
  13.8 0.0 collective-permute-done.5.refs_4_.refs_5_
  13.8 1.5 %collective-permute-start.2 = (bf16[256,128]{1,0:T(8,128)(2,1)S(1)}, bf16[256,128]{1,0:T(8,128)(2,1)S(1)}, u32[]{:S(2)}, u32[]{:S(2)}) collective-permute-start(bf16[256,128]{1,0:T(8,128)(2,1)S(1)} %collective-permute-done.1.refs_5_.refs_6_), channel_id=1, source_target_pairs={{0,4},{2,6},{4,0},{6,2},{8,12},{10,14},{12,8},{14,10},{1,5},{3,7},... | collective-permute-start | bytes 196616 | tf_op jit(solution)/shard_map/ppermute | solution.py:298
  15.4 0.6 %collective-permute-done.3.refs_2_.refs_3_ = bf16[256,128]{1,0:T(8,128)(2,1)S(1)} collective-permute-done((bf16[256,128]{1,0:T(8,128)(2,1)S(1)}, bf16[256,128]{1,0:T(8,128)(2,1)S(1)}, u32[]{:S(2)}, u32[]{:S(2)}) %collective-permute-start.3) | collective-permute-done | bytes 65568 | tf_op jit(solution)/shard_map/ppermute | solution.py:298
  15.9 1.0 %collective-permute-done.7.refs_7_.refs_8_ = bf16[256,128]{1,0:T(8,128)(2,1)S(1)} collective-permute-done((bf16[256,128]{1,0:T(8,128)(2,1)S(1)}, bf16[256,128]{1,0:T(8,128)(2,1)S(1)}, u32[]{:S(2)}, u32[]{:S(2)}) %collective-permute-start.7) | collective-permute-done | bytes 65568 | tf_op jit(solution)/shard_map/ppermute | solution.py:298
  17.0 0.7 %collective-permute-done.4.refs_3_.refs_4_ = bf16[256,128]{1,0:T(8,128)(2,1)S(1)} collective-permute-done((bf16[256,128]{1,0:T(8,128)(2,1)S(1)}, bf16[256,128]{1,0:T(8,128)(2,1)S(1)}, u32[]{:S(2)}, u32[]{:S(2)}) %collective-permute-start.4) | collective-permute-done | bytes 65568 | tf_op jit(solution)/shard_map/ppermute | solution.py:298
  17.7 0.4 %collective-permute-done.2.refs_1_.refs_2_ = bf16[256,128]{1,0:T(8,128)(2,1)S(1)} collective-permute-done((bf16[256,128]{1,0:T(8,128)(2,1)S(1)}, bf16[256,128]{1,0:T(8,128)(2,1)S(1)}, u32[]{:S(2)}, u32[]{:S(2)}) %collective-permute-start.2) | collective-permute-done | bytes 65568 | tf_op jit(solution)/shard_map/ppermute | solution.py:298
  18.1 0.0 collective-permute-done.other_in
  18.1 2.0 %shard_map.94 = (f32[256,128]{1,0:T(8,128)S(1)}, bf16[256,128]{1,0:T(8,128)(2,1)S(1)}, bf16[256,128]{1,0:T(8,128)(2,1)S(1)}, bf16[256,128]{1,0:T(8,128)(2,1)S(1)...) custom-call(s32[1024]{0:T(1024)S(1)} %get-tuple-element.18.balance_i, ...), custom_call_target="tpu_custom_call" | custom-call | tf_op jit(solution)/shard_map/pallas_call | solution.py:208
  20.1 1.5 %collective-permute-start.8 = (bf16[256,128]{1,0:T(8,128)(2,1)S(1)}, bf16[256,128]{1,0:T(8,128)(2,1)S(1)}, u32[]{:S(2)}, u32[]{:S(2)}) collective-permute-start(bf16[256,128]{1,0:T(8,128)(2,1)S(1)} %get-tuple-element.23), channel_id=1, source_target_pairs={{0,6},{2,4},{4,2},{6,0},{8,14},{10,12},{12,10},{14,8},{1,7},{3,5},... | collective-permute-start | bytes 196616 | tf_op jit(solution)/shard_map/ppermute | solution.py:298
  21.6 1.6 %collective-permute-start.9 = (bf16[256,128]{1,0:T(8,128)(2,1)S(1)}, bf16[256,128]{1,0:T(8,128)(2,1)S(1)}, u32[]{:S(2)}, u32[]{:S(2)}) collective-permute-start(bf16[256,128]{1,0:T(8,128)(2,1)S(1)} %get-tuple-element.24), channel_id=1, source_target_pairs={{0,4},{2,6},{4,0},{6,2},{8,12},{10,14},{12,8},{14,10},{1,5},{3,7},... | collective-permute-start | bytes 196616 | tf_op jit(solution)/shard_map/ppermute | solution.py:298
  23.2 0.5 %collective-permute-start.10 = (bf16[256,128]{1,0:T(8,128)(2,1)S(1)}, bf16[256,128]{1,0:T(8,128)(2,1)S(1)}, u32[]{:S(2)}, u32[]{:S(2)}) collective-permute-start(bf16[256,128]{1,0:T(8,128)(2,1)S(1)} %get-tuple-element.25), channel_id=1, source_target_pairs={{0,2},{2,0},{4,6},{6,4},{8,10},{10,8},{12,14},{14,12},{1,3},{3,1},... | collective-permute-start | bytes 196616 | tf_op jit(solution)/shard_map/ppermute | solution.py:298
  23.7 1.4 %collective-permute-start.12 = (bf16[256,128]{1,0:T(8,128)(2,1)S(1)}, bf16[256,128]{1,0:T(8,128)(2,1)S(1)}, u32[]{:S(2)}, u32[]{:S(2)}) collective-permute-start(bf16[256,128]{1,0:T(8,128)(2,1)S(1)} %get-tuple-element.29), channel_id=1, source_target_pairs={{0,6},{2,4},{4,2},{6,0},{8,14},{10,12},{12,10},{14,8},{1,7},{3,5},... | collective-permute-start | bytes 196616 | tf_op jit(solution)/shard_map/ppermute | solution.py:298
  25.1 1.6 %collective-permute-start.13 = (bf16[256,128]{1,0:T(8,128)(2,1)S(1)}, bf16[256,128]{1,0:T(8,128)(2,1)S(1)}, u32[]{:S(2)}, u32[]{:S(2)}) collective-permute-start(bf16[256,128]{1,0:T(8,128)(2,1)S(1)} %get-tuple-element.30), channel_id=1, source_target_pairs={{0,2},{2,0},{4,6},{6,4},{8,10},{10,8},{12,14},{14,12},{1,3},{3,1},... | collective-permute-start | bytes 196616 | tf_op jit(solution)/shard_map/ppermute | solution.py:298
  26.7 0.0 collective-permute-done.8
  26.7 0.5 %collective-permute-start.14 = (bf16[256,128]{1,0:T(8,128)(2,1)S(1)}, bf16[256,128]{1,0:T(8,128)(2,1)S(1)}, u32[]{:S(2)}, u32[]{:S(2)}) collective-permute-start(bf16[256,128]{1,0:T(8,128)(2,1)S(1)} %get-tuple-element.31), channel_id=1, source_target_pairs={{0,4},{2,6},{4,0},{6,2},{8,12},{10,14},{12,8},{14,10},{1,5},{3,7},... | collective-permute-start | bytes 196616 | tf_op jit(solution)/shard_map/ppermute | solution.py:298
  27.2 0.0 collective-permute-done.9
  27.2 0.2 collective-permute-done.10
  27.5 2.3 %collective-permute-start.11 = (bf16[256,128]{1,0:T(8,128)(2,1)S(1)}, bf16[256,128]{1,0:T(8,128)(2,1)S(1)}, u32[]{:S(2)}, u32[]{:S(2)}) collective-permute-start(bf16[256,128]{1,0:T(8,128)(2,1)S(1)} %add_convert_fusion.1.refs_0_), channel_id=1, source_target_pairs={{0,8},{2,10},{4,12},{6,14},{8,0},{10,2},{12,4},{14,6},{1,9},{3,11}... | collective-permute-start | bytes 196616 | tf_op jit(solution)/shard_map/ppermute | solution.py:298
  29.8 2.9 %shard_map.95 = (bf16[512,128]{1,0:T(8,128)(2,1)}, bf16[512,128]{1,0:T(8,128)(2,1)}) custom-call(s32[1024]{0:T(1024)S(1)} %get-tuple-element.18.balance_in, s32[8]{0:T(128)S(1)} %get-tuple-element.19.docs_in, bf16[1024,128]{1,0:T(8,128)(2,1)S(1)} %get-tuple-element.20.own_in, bf16[256,128]{1,0:T(8,128)(2,1)S(1)} %add_convert_fusion.1.refs_0_, ...), custom_call_target="tpu_custom_call" | custom-call | tf_op jit(solution)/shard_map/pallas_call | solution.py:271
  32.7 0.0 collective-permute-done.12
  32.7 0.0 collective-permute-done.13
  32.7 0.0 collective-permute-done.14
  32.7 0.0 collective-permute-done.11
  32.8 0.6 %fusion = (bf16[128,128]{1,0:T(8,128)(2,1)}, bf16[128,128]{1,0:T(8,128)(2,1)}) fusion(bf16[256,128]{1,0:T(8,128)(2,1)S(1)} %add_convert_fusion), kind=kLoop, calls=%fused_computation.2 | loop fusion | bytes 131072 | tf_op jit(solution)/shard_map/slice | solution.py:341
  (2 shorter events, 0.1 us)
Async XLA Ops:
  1.7 16.4 %collective-permute-start = (bf16[1024,128]{1,0:T(8,128)(2,1)S(1)}, bf16[1024,128]{1,0:T(8,128)(2,1)S(1)}, u32[]{:S(2)}, u32[]{:S(2)}) collective-permute-start(bf16[1024,128]{1,0:T(8,128)(2,1)S(1)} %get-tuple-element.20.own_in), channel_id=1, source_target_pairs={{0,1},{1,0},{2,3},{3,2},{4,5},{5,4},{6,7},{7,6},{8,9},{9,8},{10,11... | collective-permute-start | bytes 786440 | tf_op jit(solution)/shard_map/ppermute | solution.py:309
  4.7 6.1 %collective-permute-start.1 = (bf16[256,128]{1,0:T(8,128)(2,1)S(1)}, bf16[256,128]{1,0:T(8,128)(2,1)S(1)}, u32[]{:S(2)}, u32[]{:S(2)}) collective-permute-start(bf16[256,128]{1,0:T(8,128)(2,1)S(1)} %get-tuple-element.21.refs_0_.refs_1_), channel_id=1, source_target_pairs={{0,8},{2,10},{4,12},{6,14},{8,0},{10,2},{12,4},{14,6},{1,9},{3,11}... | collective-permute-start | bytes 196616 | tf_op jit(solution)/shard_map/ppermute | solution.py:298
  7.3 6.0 %collective-permute-start.6 = (bf16[256,128]{1,0:T(8,128)(2,1)S(1)}, bf16[256,128]{1,0:T(8,128)(2,1)S(1)}, u32[]{:S(2)}, u32[]{:S(2)}) collective-permute-start(bf16[256,128]{1,0:T(8,128)(2,1)S(1)} %get-tuple-element.21.refs_0_.refs_1_), channel_id=1, source_target_pairs={{0,2},{2,0},{4,6},{6,4},{8,10},{10,8},{12,14},{14,12},{1,3},{3,1},... | collective-permute-start | bytes 196616 | tf_op jit(solution)/shard_map/ppermute | solution.py:298
  8.8 5.0 %collective-permute-start.5 = (bf16[256,128]{1,0:T(8,128)(2,1)S(1)}, bf16[256,128]{1,0:T(8,128)(2,1)S(1)}, u32[]{:S(2)}, u32[]{:S(2)}) collective-permute-start(bf16[256,128]{1,0:T(8,128)(2,1)S(1)} %get-tuple-element.21.refs_0_.refs_1_), channel_id=1, source_target_pairs={{0,4},{2,6},{4,0},{6,2},{8,12},{10,14},{12,8},{14,10},{1,5},{3,7},... | collective-permute-start | bytes 196616 | tf_op jit(solution)/shard_map/ppermute | solution.py:298
  10.4 5.5 %collective-permute-start.3 = (bf16[256,128]{1,0:T(8,128)(2,1)S(1)}, bf16[256,128]{1,0:T(8,128)(2,1)S(1)}, u32[]{:S(2)}, u32[]{:S(2)}) collective-permute-start(bf16[256,128]{1,0:T(8,128)(2,1)S(1)} %get-tuple-element.21.refs_0_.refs_1_), channel_id=1, source_target_pairs={{0,6},{2,4},{4,2},{6,0},{8,14},{10,12},{12,10},{14,8},{1,7},{3,5},... | collective-permute-start | bytes 196616 | tf_op jit(solution)/shard_map/ppermute | solution.py:298
  10.8 6.2 %collective-permute-start.7 = (bf16[256,128]{1,0:T(8,128)(2,1)S(1)}, bf16[256,128]{1,0:T(8,128)(2,1)S(1)}, u32[]{:S(2)}, u32[]{:S(2)}) collective-permute-start(bf16[256,128]{1,0:T(8,128)(2,1)S(1)} %collective-permute-done.1.refs_5_.refs_6_), channel_id=1, source_target_pairs={{0,6},{2,4},{4,2},{6,0},{8,14},{10,12},{12,10},{14,8},{1,7},{3,5},... | collective-permute-start | bytes 196616 | tf_op jit(solution)/shard_map/ppermute | solution.py:298
  13.3 4.3 %collective-permute-start.4 = (bf16[256,128]{1,0:T(8,128)(2,1)S(1)}, bf16[256,128]{1,0:T(8,128)(2,1)S(1)}, u32[]{:S(2)}, u32[]{:S(2)}) collective-permute-start(bf16[256,128]{1,0:T(8,128)(2,1)S(1)} %collective-permute-done.1.refs_5_.refs_6_), channel_id=1, source_target_pairs={{0,2},{2,0},{4,6},{6,4},{8,10},{10,8},{12,14},{14,12},{1,3},{3,1},... | collective-permute-start | bytes 196616 | tf_op jit(solution)/shard_map/ppermute | solution.py:298
  13.8 4.3 %collective-permute-start.2 = (bf16[256,128]{1,0:T(8,128)(2,1)S(1)}, bf16[256,128]{1,0:T(8,128)(2,1)S(1)}, u32[]{:S(2)}, u32[]{:S(2)}) collective-permute-start(bf16[256,128]{1,0:T(8,128)(2,1)S(1)} %collective-permute-done.1.refs_5_.refs_6_), channel_id=1, source_target_pairs={{0,4},{2,6},{4,0},{6,2},{8,12},{10,14},{12,8},{14,10},{1,5},{3,7},... | collective-permute-start | bytes 196616 | tf_op jit(solution)/shard_map/ppermute | solution.py:298
  20.1 6.5 %collective-permute-start.8 = (bf16[256,128]{1,0:T(8,128)(2,1)S(1)}, bf16[256,128]{1,0:T(8,128)(2,1)S(1)}, u32[]{:S(2)}, u32[]{:S(2)}) collective-permute-start(bf16[256,128]{1,0:T(8,128)(2,1)S(1)} %get-tuple-element.23), channel_id=1, source_target_pairs={{0,6},{2,4},{4,2},{6,0},{8,14},{10,12},{12,10},{14,8},{1,7},{3,5},... | collective-permute-start | bytes 196616 | tf_op jit(solution)/shard_map/ppermute | solution.py:298
  21.6 5.6 %collective-permute-start.9 = (bf16[256,128]{1,0:T(8,128)(2,1)S(1)}, bf16[256,128]{1,0:T(8,128)(2,1)S(1)}, u32[]{:S(2)}, u32[]{:S(2)}) collective-permute-start(bf16[256,128]{1,0:T(8,128)(2,1)S(1)} %get-tuple-element.24), channel_id=1, source_target_pairs={{0,4},{2,6},{4,0},{6,2},{8,12},{10,14},{12,8},{14,10},{1,5},{3,7},... | collective-permute-start | bytes 196616 | tf_op jit(solution)/shard_map/ppermute | solution.py:298
  23.2 4.3 %collective-permute-start.10 = (bf16[256,128]{1,0:T(8,128)(2,1)S(1)}, bf16[256,128]{1,0:T(8,128)(2,1)S(1)}, u32[]{:S(2)}, u32[]{:S(2)}) collective-permute-start(bf16[256,128]{1,0:T(8,128)(2,1)S(1)} %get-tuple-element.25), channel_id=1, source_target_pairs={{0,2},{2,0},{4,6},{6,4},{8,10},{10,8},{12,14},{14,12},{1,3},{3,1},... | collective-permute-start | bytes 196616 | tf_op jit(solution)/shard_map/ppermute | solution.py:298
  23.7 9.0 %collective-permute-start.12 = (bf16[256,128]{1,0:T(8,128)(2,1)S(1)}, bf16[256,128]{1,0:T(8,128)(2,1)S(1)}, u32[]{:S(2)}, u32[]{:S(2)}) collective-permute-start(bf16[256,128]{1,0:T(8,128)(2,1)S(1)} %get-tuple-element.29), channel_id=1, source_target_pairs={{0,6},{2,4},{4,2},{6,0},{8,14},{10,12},{12,10},{14,8},{1,7},{3,5},... | collective-permute-start | bytes 196616 | tf_op jit(solution)/shard_map/ppermute | solution.py:298
  25.1 7.6 %collective-permute-start.13 = (bf16[256,128]{1,0:T(8,128)(2,1)S(1)}, bf16[256,128]{1,0:T(8,128)(2,1)S(1)}, u32[]{:S(2)}, u32[]{:S(2)}) collective-permute-start(bf16[256,128]{1,0:T(8,128)(2,1)S(1)} %get-tuple-element.30), channel_id=1, source_target_pairs={{0,2},{2,0},{4,6},{6,4},{8,10},{10,8},{12,14},{14,12},{1,3},{3,1},... | collective-permute-start | bytes 196616 | tf_op jit(solution)/shard_map/ppermute | solution.py:298
  26.7 6.0 %collective-permute-start.14 = (bf16[256,128]{1,0:T(8,128)(2,1)S(1)}, bf16[256,128]{1,0:T(8,128)(2,1)S(1)}, u32[]{:S(2)}, u32[]{:S(2)}) collective-permute-start(bf16[256,128]{1,0:T(8,128)(2,1)S(1)} %get-tuple-element.31), channel_id=1, source_target_pairs={{0,4},{2,6},{4,0},{6,2},{8,12},{10,14},{12,8},{14,10},{1,5},{3,7},... | collective-permute-start | bytes 196616 | tf_op jit(solution)/shard_map/ppermute | solution.py:298
  27.5 5.2 %collective-permute-start.11 = (bf16[256,128]{1,0:T(8,128)(2,1)S(1)}, bf16[256,128]{1,0:T(8,128)(2,1)S(1)}, u32[]{:S(2)}, u32[]{:S(2)}) collective-permute-start(bf16[256,128]{1,0:T(8,128)(2,1)S(1)} %add_convert_fusion.1.refs_0_), channel_id=1, source_target_pairs={{0,8},{2,10},{4,12},{6,14},{8,0},{10,2},{12,4},{14,6},{1,9},{3,11}... | collective-permute-start | bytes 196616 | tf_op jit(solution)/shard_map/ppermute | solution.py:298

commit v5 on v3

--- a/solution.py
+++ b/solution.py
@@ -27,27 +27,40 @@
     return pltpu.CompilerParams(vmem_limit_bytes=(16 << 20) if seq_total <= 1024 else (56 << 20))
 
 
-NEAR = (1, 2, 3, 4)
+MERGED = (3,)
+BLOCK_ORDER = (0, 6, 5, 2, 1, 4, 7, 3)
+FAR_ORDER = (5, 6, 7)
+BACK_ORDER = (7, 6, 5)
+SUM_ORDER = (4, 3, 1, 2)
 
 
 def high_bits(n_ctx):
     return [(1 << b, range(1 << b)) for b in range(3, n_ctx.bit_length() - 1)]
 
 
-BLOCK_ORDER = (0, 4, 1, 2, 3, 7, 6, 5)
-FAR_ORDER = (7, 6, 5)
-SUM_ORDER = (4, 2, 3, 1)
-
-
-def pack_kernel(key_rows, value_rows, q_rows, g_rows, balance, doc_lengths, kv_out, qg_out, balance_out, docs_out, sems):
-    tok_rows, rows = key_rows.shape[0], q_rows.shape[0]
+def join_kernel(first, second, out):
+    rows = first.shape[0]
+    out[:rows, :] = first[...]
+    out[rows:, :] = second[...]
+
+
+def join(first, second, seq_total):
+    return pl.pallas_call(
+        join_kernel,
+        out_shape=jax.ShapeDtypeStruct((2 * first.shape[0], first.shape[1]), first.dtype),
+        in_specs=[VMEM] * 2,
+        out_specs=VMEM,
+        compiler_params=limit(seq_total),
+    )(first, second)
+
+
+def pack_kernel(key_rows, value_rows, balance, doc_lengths, kv_out, balance_out, docs_out, sems):
+    tok_rows = key_rows.shape[0]
     copies = [
         pltpu.make_async_copy(key_rows, kv_out.at[pl.ds(0, tok_rows)], sems.at[0]),
         pltpu.make_async_copy(value_rows, kv_out.at[pl.ds(tok_rows, tok_rows)], sems.at[1]),
-        pltpu.make_async_copy(q_rows, qg_out.at[pl.ds(0, rows)], sems.at[2]),
-        pltpu.make_async_copy(g_rows, qg_out.at[pl.ds(rows, rows)], sems.at[3]),
-        pltpu.make_async_copy(balance, balance_out, sems.at[4]),
-        pltpu.make_async_copy(doc_lengths, docs_out, sems.at[5]),
+        pltpu.make_async_copy(balance, balance_out, sems.at[2]),
+        pltpu.make_async_copy(doc_lengths, docs_out, sems.at[3]),
     ]
     for copy in copies:
         copy.start()
@@ -55,25 +68,19 @@
         copy.wait()
 
 
-def pack(key_rows, value_rows, q_rows, g_rows, balance, doc_lengths):
+def pack(key_rows, value_rows, balance, doc_lengths):
     return pl.pallas_call(
         pack_kernel,
         out_shape=[
             jax.ShapeDtypeStruct((2 * key_rows.shape[0], key_rows.shape[1]), jnp.bfloat16),
-            jax.ShapeDtypeStruct((2 * q_rows.shape[0], q_rows.shape[1]), jnp.bfloat16),
             jax.ShapeDtypeStruct(balance.shape, jnp.int32),
             jax.ShapeDtypeStruct(doc_lengths.shape, jnp.int32),
         ],
-        in_specs=[ANY] * 6,
-        out_specs=[ANY] * 4,
-        scratch_shapes=[pltpu.SemaphoreType.DMA((6,))],
+        in_specs=[ANY] * 4,
+        out_specs=[ANY] * 3,
+        scratch_shapes=[pltpu.SemaphoreType.DMA((4,))],
         compiler_params=limit(balance.shape[0]),
-    )(
-        *[
-            pltpu.with_memory_space_constraint(a, pltpu.HBM)
-            for a in (key_rows, value_rows, q_rows, g_rows, balance, doc_lengths)
-        ]
-    )
+    )(*[pltpu.with_memory_space_constraint(a, pltpu.HBM) for a in (key_rows, value_rows, balance, doc_lengths)])
 
 
 def start_lists(balance_in, docs_in, lists):
@@ -150,31 +157,29 @@
 
 
 def load_blocks(me, listed, blocks, kv_all):
-    rows = blocks[0].shape[0]
-    for k, block in zip(listed, blocks):
-        owner = lax.bitwise_xor(me, k)
-        kv_all[pl.ds(pl.multiple_of(owner * rows, rows), rows), :] = block[...]
-
-
-def terms_kernel(listed, heads, reach, balance_in, docs_in, own_in, other_in, *refs):
-    n_ctx = len(listed)
-    blocks, outs, scratch = refs[:n_ctx], refs[n_ctx : 2 * n_ctx], refs[2 * n_ctx :]
+    rows = min(block.shape[0] for block in blocks)
+    for ks, block in zip(listed, blocks):
+        for i, k in enumerate(ks):
+            owner = lax.bitwise_xor(me, k)
+            kv_all[pl.ds(pl.multiple_of(owner * rows, rows), rows), :] = block[i * rows : (i + 1) * rows, :]
+
+
+def terms_kernel(listed, heads, reach, balance_in, docs_in, q_own, g_own, q_other, g_other, *refs):
+    n_ctx, n_blocks = sum(len(ks) for ks in listed), len(listed)
+    blocks, outs, scratch = refs[:n_blocks], refs[n_blocks : n_blocks + n_ctx], refs[n_blocks + n_ctx :]
     qg_all, kv_all, key_win, value_win, terms, *lists = scratch
     me, head = lax.axis_index("ctx"), lax.axis_index("head")
-    both, width = blocks[0].shape
+    both, width = min(block.shape[0] for block in blocks), blocks[0].shape[1]
     tok_rows = both // 2
     runs_here = tok_rows // RUN
     run_rows = RUN * heads
-    rows_here = tok_rows * heads
-
     copies = start_lists(balance_in, docs_in, lists)
     load_blocks(me, listed, blocks, kv_all)
-    for source, part in ((own_in, head), (other_in, 1 - head)):
+    for sources, part in (((q_own, g_own), head), ((q_other, g_other), 1 - head)):
         at = pl.ds(pl.multiple_of(part * run_rows, run_rows), run_rows)
-        for w in range(2):
+        for w, source in enumerate(sources):
             for r in range(runs_here):
-                here = w * rows_here + r * run_rows
-                qg_all[w, r, at, :] = source[here : here + run_rows, :]
+                qg_all[w, r, at, :] = source[r * run_rows : (r + 1) * run_rows, :]
     terms[...] = jnp.zeros_like(terms)
     finish_lists(copies, lists)
 
@@ -198,8 +203,8 @@
 
 def gradient_terms(balance, doc_lengths, own, other, blocks, heads, reach):
     listed, blocks = zip(*blocks)
-    n_ctx = len(blocks)
-    both, width = blocks[0].shape
+    n_ctx = sum(len(ks) for ks in listed)
+    both, width = min(block.shape[0] for block in blocks), blocks[0].shape[1]
     tok_rows = both // 2
     runs_here = tok_rows // RUN
     kept = [k for k in range(n_ctx) if k in (0, 4) or 8 <= k < n_ctx // 2 or k < min(8, n_ctx // 2) and n_ctx > 8]
@@ -209,7 +214,7 @@
     return pl.pallas_call(
         functools.partial(terms_kernel, listed, heads, reach),
         out_shape=outs,
-        in_specs=[ANY] * 2 + [VMEM] * (2 + n_ctx),
+        in_specs=[ANY] * 2 + [VMEM] * (4 + len(blocks)),
         out_specs=[VMEM] * n_ctx,
         scratch_shapes=[
             pltpu.VMEM((2, runs_here, 2 * RUN * heads, width), jnp.bfloat16),
@@ -223,20 +228,19 @@
             pltpu.SemaphoreType.DMA((2,)),
         ],
         compiler_params=limit(balance.shape[0]),
-    )(balance, doc_lengths, own, other, *blocks)
-
-
-def rows_kernel(n_after, listed, heads, reach, balance_in, docs_in, own_in, *refs):
+    )(balance, doc_lengths, *own, *other, *blocks)
+
+
+def rows_kernel(n_after, listed, heads, reach, balance_in, docs_in, q_own, g_own, *refs):
     refs = refs[n_after:]
-    n_ctx = len(listed)
-    blocks, (att_out, qg_out), scratch = refs[:n_ctx], refs[n_ctx : n_ctx + 2], refs[n_ctx + 2 :]
+    n_blocks = len(listed)
+    blocks, (att_out, qg_out), scratch = refs[:n_blocks], refs[n_blocks : n_blocks + 2], refs[n_blocks + 2 :]
     kv_all, key_win, value_win, att_buf, grad_buf, out_sem, *lists = scratch
     me = lax.axis_index("ctx")
-    both, width = blocks[0].shape
+    both, width = min(block.shape[0] for block in blocks), blocks[0].shape[1]
     tok_rows = both // 2
     runs_here = tok_rows // RUN
     run_rows = RUN * heads
-    rows_here = tok_rows * heads
 
     copies = start_lists(balance_in, docs_in, lists)
     load_blocks(me, listed, blocks, kv_all)
@@ -246,8 +250,8 @@
     for r in range(runs_here):
         place_run, _ = run_window(me, lists, kv_all, key_win, value_win, r, reach, runs_here, tok_rows)
         here = slice(r * run_rows, (r + 1) * run_rows)
-        q_rows = own_in[here, :]
-        g_rows = own_in[rows_here + r * run_rows : rows_here + (r + 1) * run_rows, :]
+        q_rows = q_own[here, :]
+        g_rows = g_own[here, :]
         raw, one_over = weights_of(lists[1], place_run, key_win[r], q_rows, reach, heads)
         attended = contract(value_win[r], raw.astype(jnp.bfloat16), 0, 0) * one_over
         att_buf[here, :] = attended.T.astype(jnp.bfloat16)
@@ -264,15 +268,15 @@
 
 def query_side(balance, doc_lengths, own, after, blocks, heads, reach):
     listed, blocks = zip(*blocks)
-    n_ctx = len(blocks)
-    both, width = blocks[0].shape
+    n_ctx = sum(len(ks) for ks in listed)
+    both, width = min(block.shape[0] for block in blocks), blocks[0].shape[1]
     tok_rows = both // 2
     runs_here = tok_rows // RUN
-    rows = own.shape[0] // 2
+    rows = own[0].shape[0]
     return pl.pallas_call(
         functools.partial(rows_kernel, len(after), listed, heads, reach),
         out_shape=[jax.ShapeDtypeStruct((rows, width), jnp.bfloat16)] * 2,
-        in_specs=[ANY, ANY, VMEM] + [ANY] * len(after) + [VMEM] * n_ctx,
+        in_specs=[ANY, ANY, VMEM, VMEM] + [ANY] * len(after) + [VMEM] * len(blocks),
         out_specs=[HBM] * 2,
         scratch_shapes=[
             pltpu.VMEM((n_ctx * both, width), jnp.bfloat16),
@@ -287,7 +291,7 @@
             pltpu.SemaphoreType.DMA((2,)),
         ],
         compiler_params=limit(balance.shape[0]),
-    )(balance, doc_lengths, own, *after, *blocks)
+    )(balance, doc_lengths, *own, *after, *blocks)
 
 
 def body(n_ctx, n_head, queries, key_rows, value_rows, out_grad, doc_lengths, balance):
@@ -298,33 +302,29 @@
     def swap(array, k):
         return lax.ppermute(array, "ctx", [(i, i ^ k) for i in range(n_ctx)])
 
-    mine, own, balance, doc_lengths = pack(
-        key_rows,
-        value_rows,
-        queries.reshape(tok_rows * heads, width),
-        out_grad.reshape(tok_rows * heads, width),
-        balance,
-        doc_lengths,
-    )
+    own = [array.reshape(tok_rows * heads, width) for array in (queries, out_grad)]
+    mine, balance, doc_lengths = pack(key_rows, value_rows, balance, doc_lengths)
     blocks = {0: mine}
-    other = lax.ppermute(own, "head", [(i, n_head - 1 - i) for i in range(n_head)])
     for k in (4, 1, 2, 3):
-        blocks[k] = swap(mine, k)
+        if k not in MERGED:
+            blocks[k] = swap(mine, k)
+    other = [lax.ppermute(array, "head", [(i, n_head - 1 - i) for i in range(n_head)]) for array in own]
+    merged = {}
     for k in FAR_ORDER:
-        blocks[k] = swap(blocks[4], k - 4)
-    for bit, below in high_bits(n_ctx):
-        for k in below:
-            blocks[bit + k] = swap(blocks[k], bit)
-
-    listed = BLOCK_ORDER + tuple(range(8, n_ctx))
-    blocks = [(k, blocks[k]) for k in listed]
+        if k - 4 in MERGED:
+            merged[k] = swap(join(mine, blocks[4], seq_total), k - 4)
+        else:
+            blocks[k] = swap(blocks[4], k - 4)
+    blocks = [((k - 4, k), merged[k]) if k in merged else ((k,), blocks[k]) for k in BLOCK_ORDER if k not in MERGED]
+    for bit, _ in high_bits(n_ctx):
+        blocks += [(tuple(bit + k for k in ks), swap(block, bit)) for ks, block in blocks]
     terms = list(gradient_terms(balance, doc_lengths, own, other, blocks, heads, reach))
 
     for bit, below in reversed(high_bits(n_ctx)):
         for k in below:
             terms[k] = terms[k] + swap(terms[bit + k].astype(jnp.bfloat16), bit).astype(jnp.float32)
     far = terms[4]
-    for k in FAR_ORDER:
+    for k in BACK_ORDER:
         far = far + swap(terms[k].astype(jnp.bfloat16), k - 4).astype(jnp.float32)
     far = far.astype(jnp.bfloat16)
     total = terms[0]

time: 35.6 us -> 32.7 us (0.919)
  waiting for transfers between devices: 5.94 us -> 2.84 us
    ppermute x14 -> x13, waiting for transfers between devices: 5.94 us -> 2.83 us  [swap(): return lax.ppermute(array, 'ctx', [(i, i ^ k) for i in range(n_ctx)])]
    ppermute x14 -> x13, starting transfers between devices: 19.2 us -> 20.4 us  [swap(): return lax.ppermute(array, 'ctx', [(i, i ^ k) for i in range(n_ctx)])]
    ppermute x1 -> x2, starting transfers between devices: 3 us -> 2.03 us  [body(): lax.ppermute(array, 'head', [(i, n_head - 1 - i) for i in range(n_head)])]
  transfers between devices with their start and end apart: 15 -> 15, of which waited for: 4 -> 3; matrix products, arithmetic and copies ran while one was open for 0% -> 0% of each run, Pallas kernels for 8% -> 9%
where the time goes in v5:
time: 32.7 us; the launch traced here: 32.5 us
  starting transfers between devices  22.5 us (69%)
  Pallas kernels  5.73 us (18%)
  waiting for transfers between devices  2.84 us (9%)
  between operations  0.73 us (2%)
  local copies, waits for them, and re-layouts  0.64 us (2%)
    ppermute x13, starting transfers between devices, swap(): return lax.ppermute(array, 'ctx', [(i, i ^ k) for i in range(n_ctx)])  20.4 us
    pallas_call x1, Pallas kernels, query_side(): pl.pallas_call(functools.partial(rows_kernel, len(after), listed, heads,...  2.87 us
    ppermute x13, waiting for transfers between devices, swap(): return lax.ppermute(array, 'ctx', [(i, i ^ k) for i in range(n_ctx)])  2.83 us
    pallas_call x1, Pallas kernels, gradient_terms(): pl.pallas_call(functools.partial(terms_kernel, listed, heads, reach), out...  2.04 us
    ppermute x2, starting transfers between devices, body(): lax.ppermute(array, 'head', [(i, n_head - 1 - i) for i in range(n_head)])  2.03 us
    pallas_call x1, Pallas kernels, pack(): pl.pallas_call(pack_kernel, out_shape=[jax.ShapeDtypeStruct((2 * key_rows...  0.81 us
  transfers between devices with their start and end apart: 15, of which 3 were waited for; matrix products, arithmetic and copies ran while one was open for 0% of the time, Pallas kernels for 9%

profile of v5, /device:TPU:0, one launch (start us, length us, event | category | flops | bytes accessed | tf_op | source)
XLA Modules:
  0.0 32.5 jit_solution(15968885041551708341)
XLA Ops:
  0.6 0.8 %shard_map.93 = (bf16[256,128]{1,0:T(8,128)(2,1)S(1)}, s32[1024]{0:T(1024)S(1)}, s32[8]{0:T(128)S(1)}) custom-call(bf16[128,128]{1,0:T(8,128)(2,1)} %key_rows.1, bf16[128,128]{1,0:T(8,128)(2,1)} %value_rows.1, s32[1024]{0:T(1024)} %balance.1, s32[8]{0:T(128)} %doc_lengths.1), custom_call_target="tpu_custom_call" | custom-call | tf_op jit(solution)/shard_map/pallas_call | solution.py:72
  1.5 4.1 %collective-permute-start.2 = (bf16[256,128]{1,0:T(8,128)(2,1)S(1)}, bf16[256,128]{1,0:T(8,128)(2,1)S(1)}, u32[]{:S(2)}, u32[]{:S(2)}) collective-permute-start(bf16[256,128]{1,0:T(8,128)(2,1)S(1)} %get-tuple-element.19.first.refs_0_.refs_1_), channel_id=1, source_target_pairs={{0,8},{2,10},{4,12},{6,14},{8,0},{10,2},{12,4},{14,6},{1,9},{3,11}... | collective-permute-start | bytes 196616 | tf_op jit(solution)/shard_map/ppermute | solution.py:303
  5.6 1.5 %collective-permute-start.6 = (bf16[256,128]{1,0:T(8,128)(2,1)S(1)}, bf16[256,128]{1,0:T(8,128)(2,1)S(1)}, u32[]{:S(2)}, u32[]{:S(2)}) collective-permute-start(bf16[256,128]{1,0:T(8,128)(2,1)S(1)} %get-tuple-element.19.first.refs_0_.refs_1_), channel_id=1, source_target_pairs={{0,2},{2,0},{4,6},{6,4},{8,10},{10,8},{12,14},{14,12},{1,3},{3,1},... | collective-permute-start | bytes 196616 | tf_op jit(solution)/shard_map/ppermute | solution.py:303
  7.1 1.6 %collective-permute-start.5 = (bf16[256,128]{1,0:T(8,128)(2,1)S(1)}, bf16[256,128]{1,0:T(8,128)(2,1)S(1)}, u32[]{:S(2)}, u32[]{:S(2)}) collective-permute-start(bf16[256,128]{1,0:T(8,128)(2,1)S(1)} %get-tuple-element.19.first.refs_0_.refs_1_), channel_id=1, source_target_pairs={{0,4},{2,6},{4,0},{6,2},{8,12},{10,14},{12,8},{14,10},{1,5},{3,7},... | collective-permute-start | bytes 196616 | tf_op jit(solution)/shard_map/ppermute | solution.py:303
  8.7 1.5 %collective-permute-start = (bf16[512,128]{1,0:T(8,128)(2,1)}, bf16[512,128]{1,0:T(8,128)(2,1)S(1)}, u32[]{:S(2)}, u32[]{:S(2)}) collective-permute-start(bf16[512,128]{1,0:T(8,128)(2,1)} %bitcast.4), channel_id=1, source_target_pairs={{0,1},{1,0},{2,3},{3,2},{4,5},{5,4},{6,7},{7,6},{8,9},{9,8},{10,11... | collective-permute-start | bytes 393224 | tf_op jit(solution)/shard_map/ppermute | solution.py:311
  10.1 0.0 copy-start
  10.1 0.0 copy-start.1
  10.1 0.5 %collective-permute-start.1 = (bf16[512,128]{1,0:T(8,128)(2,1)}, bf16[512,128]{1,0:T(8,128)(2,1)S(1)}, u32[]{:S(2)}, u32[]{:S(2)}) collective-permute-start(bf16[512,128]{1,0:T(8,128)(2,1)} %bitcast.7), channel_id=1, source_target_pairs={{0,1},{1,0},{2,3},{3,2},{4,5},{5,4},{6,7},{7,6},{8,9},{9,8},{10,11... | collective-permute-start | bytes 393224 | tf_op jit(solution)/shard_map/ppermute | solution.py:311
  10.7 0.0 collective-permute-done.2.second.refs_5_.refs_6_
  10.7 0.5 %collective-permute-start.7 = (bf16[512,128]{1,0:T(8,128)(2,1)S(1)}, bf16[512,128]{1,0:T(8,128)(2,1)S(1)}, u32[]{:S(2)}, u32[]{:S(2)}) collective-permute-start(bf16[512,128]{1,0:T(8,128)(2,1)S(1)} %shard_map.94), channel_id=1, source_target_pairs={{0,6},{2,4},{4,2},{6,0},{8,14},{10,12},{12,10},{14,8},{1,7},{3,5},... | collective-permute-start | bytes 393224 | tf_op jit(solution)/shard_map/ppermute | solution.py:303
  11.2 0.0 collective-permute-done.6.refs_4_.refs_5_
  11.2 1.5 %collective-permute-start.4 = (bf16[256,128]{1,0:T(8,128)(2,1)S(1)}, bf16[256,128]{1,0:T(8,128)(2,1)S(1)}, u32[]{:S(2)}, u32[]{:S(2)}) collective-permute-start(bf16[256,128]{1,0:T(8,128)(2,1)S(1)} %collective-permute-done.2.second.refs_5_.refs_6_), channel_id=1, source_target_pairs={{0,2},{2,0},{4,6},{6,4},{8,10},{10,8},{12,14},{14,12},{1,3},{3,1},... | collective-permute-start | bytes 196616 | tf_op jit(solution)/shard_map/ppermute | solution.py:303
  12.7 0.0 collective-permute-done.5.refs_3_.refs_4_
  12.7 1.6 %collective-permute-start.3 = (bf16[256,128]{1,0:T(8,128)(2,1)S(1)}, bf16[256,128]{1,0:T(8,128)(2,1)S(1)}, u32[]{:S(2)}, u32[]{:S(2)}) collective-permute-start(bf16[256,128]{1,0:T(8,128)(2,1)S(1)} %collective-permute-done.2.second.refs_5_.refs_6_), channel_id=1, source_target_pairs={{0,4},{2,6},{4,0},{6,2},{8,12},{10,14},{12,8},{14,10},{1,5},{3,7},... | collective-permute-start | bytes 196616 | tf_op jit(solution)/shard_map/ppermute | solution.py:303
  14.3 2.6 %collective-permute-done.4.refs_2_.refs_3_ = bf16[256,128]{1,0:T(8,128)(2,1)S(1)} collective-permute-done((bf16[256,128]{1,0:T(8,128)(2,1)S(1)}, bf16[256,128]{1,0:T(8,128)(2,1)S(1)}, u32[]{:S(2)}, u32[]{:S(2)}) %collective-permute-start.4) | collective-permute-done | bytes 65568 | tf_op jit(solution)/shard_map/ppermute | solution.py:303
  16.8 0.1 collective-permute-done.3.refs_1_.refs_2_
  17.0 0.0 collective-permute-done.q_other
  17.0 0.0 collective-permute-done.1.g_other
  17.0 0.0 collective-permute-done.7.refs_6_.refs_7_
  17.0 0.0 copy-done
  17.0 0.0 copy-done.1
  17.0 2.0 %shard_map.95 = (f32[256,128]{1,0:T(8,128)S(1)}, bf16[256,128]{1,0:T(8,128)(2,1)S(1)}, bf16[256,128]{1,0:T(8,128)(2,1)S(1)}, bf16[256,128]{1,0:T(8,128)(2,1)S(1)...) custom-call(s32[1024]{0:T(1024)S(1)} %get-tuple-element.17.balance_i, ...), custom_call_target="tpu_custom_call" | custom-call | tf_op jit(solution)/shard_map/pallas_call | solution.py:214
  19.0 1.6 %collective-permute-start.8 = (bf16[256,128]{1,0:T(8,128)(2,1)S(1)}, bf16[256,128]{1,0:T(8,128)(2,1)S(1)}, u32[]{:S(2)}, u32[]{:S(2)}) collective-permute-start(bf16[256,128]{1,0:T(8,128)(2,1)S(1)} %get-tuple-element.21), channel_id=1, source_target_pairs={{0,6},{2,4},{4,2},{6,0},{8,14},{10,12},{12,10},{14,8},{1,7},{3,5},... | collective-permute-start | bytes 196616 | tf_op jit(solution)/shard_map/ppermute | solution.py:303
  20.6 0.9 %collective-permute-start.9 = (bf16[256,128]{1,0:T(8,128)(2,1)S(1)}, bf16[256,128]{1,0:T(8,128)(2,1)S(1)}, u32[]{:S(2)}, u32[]{:S(2)}) collective-permute-start(bf16[256,128]{1,0:T(8,128)(2,1)S(1)} %get-tuple-element.22), channel_id=1, source_target_pairs={{0,4},{2,6},{4,0},{6,2},{8,12},{10,14},{12,8},{14,10},{1,5},{3,7},... | collective-permute-start | bytes 196616 | tf_op jit(solution)/shard_map/ppermute | solution.py:303
  21.6 1.0 %collective-permute-start.10 = (bf16[256,128]{1,0:T(8,128)(2,1)S(1)}, bf16[256,128]{1,0:T(8,128)(2,1)S(1)}, u32[]{:S(2)}, u32[]{:S(2)}) collective-permute-start(bf16[256,128]{1,0:T(8,128)(2,1)S(1)} %get-tuple-element.23), channel_id=1, source_target_pairs={{0,2},{2,0},{4,6},{6,4},{8,10},{10,8},{12,14},{14,12},{1,3},{3,1},... | collective-permute-start | bytes 196616 | tf_op jit(solution)/shard_map/ppermute | solution.py:303
  22.6 1.5 %collective-permute-start.12 = (bf16[256,128]{1,0:T(8,128)(2,1)S(1)}, bf16[256,128]{1,0:T(8,128)(2,1)S(1)}, u32[]{:S(2)}, u32[]{:S(2)}) collective-permute-start(bf16[256,128]{1,0:T(8,128)(2,1)S(1)} %get-tuple-element.27), channel_id=1, source_target_pairs={{0,6},{2,4},{4,2},{6,0},{8,14},{10,12},{12,10},{14,8},{1,7},{3,5},... | collective-permute-start | bytes 196616 | tf_op jit(solution)/shard_map/ppermute | solution.py:303
  24.1 1.5 %collective-permute-start.13 = (bf16[256,128]{1,0:T(8,128)(2,1)S(1)}, bf16[256,128]{1,0:T(8,128)(2,1)S(1)}, u32[]{:S(2)}, u32[]{:S(2)}) collective-permute-start(bf16[256,128]{1,0:T(8,128)(2,1)S(1)} %get-tuple-element.28), channel_id=1, source_target_pairs={{0,2},{2,0},{4,6},{6,4},{8,10},{10,8},{12,14},{14,12},{1,3},{3,1},... | collective-permute-start | bytes 196616 | tf_op jit(solution)/shard_map/ppermute | solution.py:303
  25.6 0.0 collective-permute-done.8
  25.6 0.9 %collective-permute-start.14 = (bf16[256,128]{1,0:T(8,128)(2,1)S(1)}, bf16[256,128]{1,0:T(8,128)(2,1)S(1)}, u32[]{:S(2)}, u32[]{:S(2)}) collective-permute-start(bf16[256,128]{1,0:T(8,128)(2,1)S(1)} %get-tuple-element.29), channel_id=1, source_target_pairs={{0,4},{2,6},{4,0},{6,2},{8,12},{10,14},{12,8},{14,10},{1,5},{3,7},... | collective-permute-start | bytes 196616 | tf_op jit(solution)/shard_map/ppermute | solution.py:303
  26.5 0.0 collective-permute-done.9
  26.5 0.0 collective-permute-done.10
  26.5 2.2 %collective-permute-start.11 = (bf16[256,128]{1,0:T(8,128)(2,1)S(1)}, bf16[256,128]{1,0:T(8,128)(2,1)S(1)}, u32[]{:S(2)}, u32[]{:S(2)}) collective-permute-start(bf16[256,128]{1,0:T(8,128)(2,1)S(1)} %add_convert_fusion.1.refs_0_), channel_id=1, source_target_pairs={{0,8},{2,10},{4,12},{6,14},{8,0},{10,2},{12,4},{14,6},{1,9},{3,11}... | collective-permute-start | bytes 196616 | tf_op jit(solution)/shard_map/ppermute | solution.py:303
  28.8 2.9 %shard_map.96 = (bf16[512,128]{1,0:T(8,128)(2,1)}, bf16[512,128]{1,0:T(8,128)(2,1)}) custom-call(s32[1024]{0:T(1024)S(1)} %get-tuple-element.17.balance_in, s32[8]{0:T(128)S(1)} %get-tuple-element.18.docs_in, bf16[512,128]{1,0:T(8,128)(2,1)S(1)} %bitcast.6, bf16[512,128]{1,0:T(8,128)(2,1)S(1)} %bitcast.9, bf16[256,128]{1,0:T(8,128)(2,1)S(1)} %add_convert_fusion.1.refs_0_, ...), custom_call_target="tpu_custom_call" | custom-call | tf_op jit(solution)/shard_map/pallas_call | solution.py:276
  31.6 0.0 collective-permute-done.12
  31.6 0.0 collective-permute-done.13
  31.7 0.0 collective-permute-done.14
  31.7 0.1 collective-permute-done.11
  31.8 0.6 %fusion = (bf16[128,128]{1,0:T(8,128)(2,1)}, bf16[128,128]{1,0:T(8,128)(2,1)}) fusion(bf16[256,128]{1,0:T(8,128)(2,1)S(1)} %add_convert_fusion), kind=kLoop, calls=%fused_computation.2 | loop fusion | bytes 131072 | tf_op jit(solution)/shard_map/slice | solution.py:341
  (3 shorter events, 0.1 us)
Async XLA Ops:
  1.5 9.2 %collective-permute-start.2 = (bf16[256,128]{1,0:T(8,128)(2,1)S(1)}, bf16[256,128]{1,0:T(8,128)(2,1)S(1)}, u32[]{:S(2)}, u32[]{:S(2)}) collective-permute-start(bf16[256,128]{1,0:T(8,128)(2,1)S(1)} %get-tuple-element.19.first.refs_0_.refs_1_), channel_id=1, source_target_pairs={{0,8},{2,10},{4,12},{6,14},{8,0},{10,2},{12,4},{14,6},{1,9},{3,11}... | collective-permute-start | bytes 196616 | tf_op jit(solution)/shard_map/ppermute | solution.py:303
  5.6 5.6 %collective-permute-start.6 = (bf16[256,128]{1,0:T(8,128)(2,1)S(1)}, bf16[256,128]{1,0:T(8,128)(2,1)S(1)}, u32[]{:S(2)}, u32[]{:S(2)}) collective-permute-start(bf16[256,128]{1,0:T(8,128)(2,1)S(1)} %get-tuple-element.19.first.refs_0_.refs_1_), channel_id=1, source_target_pairs={{0,2},{2,0},{4,6},{6,4},{8,10},{10,8},{12,14},{14,12},{1,3},{3,1},... | collective-permute-start | bytes 196616 | tf_op jit(solution)/shard_map/ppermute | solution.py:303
  7.1 5.6 %collective-permute-start.5 = (bf16[256,128]{1,0:T(8,128)(2,1)S(1)}, bf16[256,128]{1,0:T(8,128)(2,1)S(1)}, u32[]{:S(2)}, u32[]{:S(2)}) collective-permute-start(bf16[256,128]{1,0:T(8,128)(2,1)S(1)} %get-tuple-element.19.first.refs_0_.refs_1_), channel_id=1, source_target_pairs={{0,4},{2,6},{4,0},{6,2},{8,12},{10,14},{12,8},{14,10},{1,5},{3,7},... | collective-permute-start | bytes 196616 | tf_op jit(solution)/shard_map/ppermute | solution.py:303
  8.7 8.3 %collective-permute-start = (bf16[512,128]{1,0:T(8,128)(2,1)}, bf16[512,128]{1,0:T(8,128)(2,1)S(1)}, u32[]{:S(2)}, u32[]{:S(2)}) collective-permute-start(bf16[512,128]{1,0:T(8,128)(2,1)} %bitcast.4), channel_id=1, source_target_pairs={{0,1},{1,0},{2,3},{3,2},{4,5},{5,4},{6,7},{7,6},{8,9},{9,8},{10,11... | collective-permute-start | bytes 393224 | tf_op jit(solution)/shard_map/ppermute | solution.py:311
  10.1 6.8 %copy-start = (bf16[128,4,128]{2,1,0:T(4,128)(2,1)S(1)}, bf16[128,4,128]{2,1,0:T(4,128)(2,1)}, u32[]{:S(2)}) copy-start(bf16[128,4,128]{2,1,0:T(4,128)(2,1)} %param.6) | copy-start | bytes 393220
  10.1 6.8 %copy-start.1 = (bf16[128,4,128]{2,1,0:T(4,128)(2,1)S(1)}, bf16[128,4,128]{2,1,0:T(4,128)(2,1)}, u32[]{:S(2)}) copy-start(bf16[128,4,128]{2,1,0:T(4,128)(2,1)} %param.9) | copy-start | bytes 393220
  10.1 6.8 %collective-permute-start.1 = (bf16[512,128]{1,0:T(8,128)(2,1)}, bf16[512,128]{1,0:T(8,128)(2,1)S(1)}, u32[]{:S(2)}, u32[]{:S(2)}) collective-permute-start(bf16[512,128]{1,0:T(8,128)(2,1)} %bitcast.7), channel_id=1, source_target_pairs={{0,1},{1,0},{2,3},{3,2},{4,5},{5,4},{6,7},{7,6},{8,9},{9,8},{10,11... | collective-permute-start | bytes 393224 | tf_op jit(solution)/shard_map/ppermute | solution.py:311
  10.7 6.3 %collective-permute-start.7 = (bf16[512,128]{1,0:T(8,128)(2,1)S(1)}, bf16[512,128]{1,0:T(8,128)(2,1)S(1)}, u32[]{:S(2)}, u32[]{:S(2)}) collective-permute-start(bf16[512,128]{1,0:T(8,128)(2,1)S(1)} %shard_map.94), channel_id=1, source_target_pairs={{0,6},{2,4},{4,2},{6,0},{8,14},{10,12},{12,10},{14,8},{1,7},{3,5},... | collective-permute-start | bytes 393224 | tf_op jit(solution)/shard_map/ppermute | solution.py:303
  11.2 5.7 %collective-permute-start.4 = (bf16[256,128]{1,0:T(8,128)(2,1)S(1)}, bf16[256,128]{1,0:T(8,128)(2,1)S(1)}, u32[]{:S(2)}, u32[]{:S(2)}) collective-permute-start(bf16[256,128]{1,0:T(8,128)(2,1)S(1)} %collective-permute-done.2.second.refs_5_.refs_6_), channel_id=1, source_target_pairs={{0,2},{2,0},{4,6},{6,4},{8,10},{10,8},{12,14},{14,12},{1,3},{3,1},... | collective-permute-start | bytes 196616 | tf_op jit(solution)/shard_map/ppermute | solution.py:303
  12.7 4.3 %collective-permute-start.3 = (bf16[256,128]{1,0:T(8,128)(2,1)S(1)}, bf16[256,128]{1,0:T(8,128)(2,1)S(1)}, u32[]{:S(2)}, u32[]{:S(2)}) collective-permute-start(bf16[256,128]{1,0:T(8,128)(2,1)S(1)} %collective-permute-done.2.second.refs_5_.refs_6_), channel_id=1, source_target_pairs={{0,4},{2,6},{4,0},{6,2},{8,12},{10,14},{12,8},{14,10},{1,5},{3,7},... | collective-permute-start | bytes 196616 | tf_op jit(solution)/shard_map/ppermute | solution.py:303
  19.0 6.6 %collective-permute-start.8 = (bf16[256,128]{1,0:T(8,128)(2,1)S(1)}, bf16[256,128]{1,0:T(8,128)(2,1)S(1)}, u32[]{:S(2)}, u32[]{:S(2)}) collective-permute-start(bf16[256,128]{1,0:T(8,128)(2,1)S(1)} %get-tuple-element.21), channel_id=1, source_target_pairs={{0,6},{2,4},{4,2},{6,0},{8,14},{10,12},{12,10},{14,8},{1,7},{3,5},... | collective-permute-start | bytes 196616 | tf_op jit(solution)/shard_map/ppermute | solution.py:303
  20.6 5.9 %collective-permute-start.9 = (bf16[256,128]{1,0:T(8,128)(2,1)S(1)}, bf16[256,128]{1,0:T(8,128)(2,1)S(1)}, u32[]{:S(2)}, u32[]{:S(2)}) collective-permute-start(bf16[256,128]{1,0:T(8,128)(2,1)S(1)} %get-tuple-element.22), channel_id=1, source_target_pairs={{0,4},{2,6},{4,0},{6,2},{8,12},{10,14},{12,8},{14,10},{1,5},{3,7},... | collective-permute-start | bytes 196616 | tf_op jit(solution)/shard_map/ppermute | solution.py:303
  21.6 5.0 %collective-permute-start.10 = (bf16[256,128]{1,0:T(8,128)(2,1)S(1)}, bf16[256,128]{1,0:T(8,128)(2,1)S(1)}, u32[]{:S(2)}, u32[]{:S(2)}) collective-permute-start(bf16[256,128]{1,0:T(8,128)(2,1)S(1)} %get-tuple-element.23), channel_id=1, source_target_pairs={{0,2},{2,0},{4,6},{6,4},{8,10},{10,8},{12,14},{14,12},{1,3},{3,1},... | collective-permute-start | bytes 196616 | tf_op jit(solution)/shard_map/ppermute | solution.py:303
  22.6 9.1 %collective-permute-start.12 = (bf16[256,128]{1,0:T(8,128)(2,1)S(1)}, bf16[256,128]{1,0:T(8,128)(2,1)S(1)}, u32[]{:S(2)}, u32[]{:S(2)}) collective-permute-start(bf16[256,128]{1,0:T(8,128)(2,1)S(1)} %get-tuple-element.27), channel_id=1, source_target_pairs={{0,6},{2,4},{4,2},{6,0},{8,14},{10,12},{12,10},{14,8},{1,7},{3,5},... | collective-permute-start | bytes 196616 | tf_op jit(solution)/shard_map/ppermute | solution.py:303
  24.1 7.5 %collective-permute-start.13 = (bf16[256,128]{1,0:T(8,128)(2,1)S(1)}, bf16[256,128]{1,0:T(8,128)(2,1)S(1)}, u32[]{:S(2)}, u32[]{:S(2)}) collective-permute-start(bf16[256,128]{1,0:T(8,128)(2,1)S(1)} %get-tuple-element.28), channel_id=1, source_target_pairs={{0,2},{2,0},{4,6},{6,4},{8,10},{10,8},{12,14},{14,12},{1,3},{3,1},... | collective-permute-start | bytes 196616 | tf_op jit(solution)/shard_map/ppermute | solution.py:303
  25.6 6.0 %collective-permute-start.14 = (bf16[256,128]{1,0:T(8,128)(2,1)S(1)}, bf16[256,128]{1,0:T(8,128)(2,1)S(1)}, u32[]{:S(2)}, u32[]{:S(2)}) collective-permute-start(bf16[256,128]{1,0:T(8,128)(2,1)S(1)} %get-tuple-element.29), channel_id=1, source_target_pairs={{0,4},{2,6},{4,0},{6,2},{8,12},{10,14},{12,8},{14,10},{1,5},{3,7},... | collective-permute-start | bytes 196616 | tf_op jit(solution)/shard_map/ppermute | solution.py:303
  26.5 5.2 %collective-permute-start.11 = (bf16[256,128]{1,0:T(8,128)(2,1)S(1)}, bf16[256,128]{1,0:T(8,128)(2,1)S(1)}, u32[]{:S(2)}, u32[]{:S(2)}) collective-permute-start(bf16[256,128]{1,0:T(8,128)(2,1)S(1)} %add_convert_fusion.1.refs_0_), channel_id=1, source_target_pairs={{0,8},{2,10},{4,12},{6,14},{8,0},{10,2},{12,4},{14,6},{1,9},{3,11}... | collective-permute-start | bytes 196616 | tf_op jit(solution)/shard_map/ppermute | solution.py:303

commit v6 on v5

--- a/solution.py
+++ b/solution.py
@@ -28,7 +28,7 @@
 
 
 MERGED = (3,)
-BLOCK_ORDER = (0, 6, 5, 2, 1, 4, 7, 3)
+BLOCK_ORDER = (0, 1, 5, 2, 6, 4, 7, 3)
 FAR_ORDER = (5, 6, 7)
 BACK_ORDER = (7, 6, 5)
 SUM_ORDER = (4, 3, 1, 2)

time: 32.7 us -> 32.6 us (level)
  starting transfers between devices: 22.5 us -> 21.4 us
  waiting for transfers between devices: 2.84 us -> 3.85 us
    ppermute x13, starting transfers between devices: 20.4 us -> 19.4 us  [swap(): return lax.ppermute(array, 'ctx', [(i, i ^ k) for i in range(n_ctx)])]
    ppermute x13, waiting for transfers between devices: 2.83 us -> 3.84 us  [swap(): return lax.ppermute(array, 'ctx', [(i, i ^ k) for i in range(n_ctx)])]
  transfers between devices with their start and end apart: 15 -> 15, of which waited for: 3 -> 4; matrix products, arithmetic and copies ran while one was open for 0% -> 0% of each run, Pallas kernels for 9% -> 9%
where the time goes in v6:
time: 32.6 us; the launch traced here: 32.4 us
  starting transfers between devices  21.4 us (66%)
  Pallas kernels  5.73 us (18%)
  waiting for transfers between devices  3.85 us (12%)
  between operations  0.73 us (2%)
  local copies, waits for them, and re-layouts  0.64 us (2%)
    ppermute x13, starting transfers between devices, swap(): return lax.ppermute(array, 'ctx', [(i, i ^ k) for i in range(n_ctx)])  19.4 us
    ppermute x13, waiting for transfers between devices, swap(): return lax.ppermute(array, 'ctx', [(i, i ^ k) for i in range(n_ctx)])  3.84 us
    pallas_call x1, Pallas kernels, query_side(): pl.pallas_call(functools.partial(rows_kernel, len(after), listed, heads,...  2.87 us
    pallas_call x1, Pallas kernels, gradient_terms(): pl.pallas_call(functools.partial(terms_kernel, listed, heads, reach), out...  2.04 us
    ppermute x2, starting transfers between devices, body(): lax.ppermute(array, 'head', [(i, n_head - 1 - i) for i in range(n_head)])  2.03 us
    pallas_call x1, Pallas kernels, pack(): pl.pallas_call(pack_kernel, out_shape=[jax.ShapeDtypeStruct((2 * key_rows...  0.81 us
  transfers between devices with their start and end apart: 15, of which 4 were waited for; matrix products, arithmetic and copies ran while one was open for 0% of the time, Pallas kernels for 9%

profile of v6, /device:TPU:0, one launch (start us, length us, event | category | flops | bytes accessed | tf_op | source)
XLA Modules:
  0.0 32.4 jit_solution(11732471904686245395)
XLA Ops:
  0.6 0.8 %shard_map.93 = (bf16[256,128]{1,0:T(8,128)(2,1)S(1)}, s32[1024]{0:T(1024)S(1)}, s32[8]{0:T(128)S(1)}) custom-call(bf16[128,128]{1,0:T(8,128)(2,1)} %key_rows.1, bf16[128,128]{1,0:T(8,128)(2,1)} %value_rows.1, s32[1024]{0:T(1024)} %balance.1, s32[8]{0:T(128)} %doc_lengths.1), custom_call_target="tpu_custom_call" | custom-call | tf_op jit(solution)/shard_map/pallas_call | solution.py:72
  1.5 4.1 %collective-permute-start.3 = (bf16[256,128]{1,0:T(8,128)(2,1)S(1)}, bf16[256,128]{1,0:T(8,128)(2,1)S(1)}, u32[]{:S(2)}, u32[]{:S(2)}) collective-permute-start(bf16[256,128]{1,0:T(8,128)(2,1)S(1)} %get-tuple-element.19.first.refs_0_.refs_1_), channel_id=1, source_target_pairs={{0,8},{2,10},{4,12},{6,14},{8,0},{10,2},{12,4},{14,6},{1,9},{3,11}... | collective-permute-start | bytes 196616 | tf_op jit(solution)/shard_map/ppermute | solution.py:303
  5.6 1.6 %collective-permute-start.5 = (bf16[256,128]{1,0:T(8,128)(2,1)S(1)}, bf16[256,128]{1,0:T(8,128)(2,1)S(1)}, u32[]{:S(2)}, u32[]{:S(2)}) collective-permute-start(bf16[256,128]{1,0:T(8,128)(2,1)S(1)} %get-tuple-element.19.first.refs_0_.refs_1_), channel_id=1, source_target_pairs={{0,4},{2,6},{4,0},{6,2},{8,12},{10,14},{12,8},{14,10},{1,5},{3,7},... | collective-permute-start | bytes 196616 | tf_op jit(solution)/shard_map/ppermute | solution.py:303
  7.1 1.5 %collective-permute-start.2 = (bf16[256,128]{1,0:T(8,128)(2,1)S(1)}, bf16[256,128]{1,0:T(8,128)(2,1)S(1)}, u32[]{:S(2)}, u32[]{:S(2)}) collective-permute-start(bf16[256,128]{1,0:T(8,128)(2,1)S(1)} %get-tuple-element.19.first.refs_0_.refs_1_), channel_id=1, source_target_pairs={{0,2},{2,0},{4,6},{6,4},{8,10},{10,8},{12,14},{14,12},{1,3},{3,1},... | collective-permute-start | bytes 196616 | tf_op jit(solution)/shard_map/ppermute | solution.py:303
  8.7 1.5 %collective-permute-start = (bf16[512,128]{1,0:T(8,128)(2,1)}, bf16[512,128]{1,0:T(8,128)(2,1)S(1)}, u32[]{:S(2)}, u32[]{:S(2)}) collective-permute-start(bf16[512,128]{1,0:T(8,128)(2,1)} %bitcast.4), channel_id=1, source_target_pairs={{0,1},{1,0},{2,3},{3,2},{4,5},{5,4},{6,7},{7,6},{8,9},{9,8},{10,11... | collective-permute-start | bytes 393224 | tf_op jit(solution)/shard_map/ppermute | solution.py:311
  10.1 0.0 copy-start
  10.1 0.0 copy-start.1
  10.1 0.5 %collective-permute-start.1 = (bf16[512,128]{1,0:T(8,128)(2,1)}, bf16[512,128]{1,0:T(8,128)(2,1)S(1)}, u32[]{:S(2)}, u32[]{:S(2)}) collective-permute-start(bf16[512,128]{1,0:T(8,128)(2,1)} %bitcast.7), channel_id=1, source_target_pairs={{0,1},{1,0},{2,3},{3,2},{4,5},{5,4},{6,7},{7,6},{8,9},{9,8},{10,11... | collective-permute-start | bytes 393224 | tf_op jit(solution)/shard_map/ppermute | solution.py:311
  10.7 0.0 collective-permute-done.3.second.refs_5_.refs_6_
  10.7 0.5 %collective-permute-start.7 = (bf16[512,128]{1,0:T(8,128)(2,1)S(1)}, bf16[512,128]{1,0:T(8,128)(2,1)S(1)}, u32[]{:S(2)}, u32[]{:S(2)}) collective-permute-start(bf16[512,128]{1,0:T(8,128)(2,1)S(1)} %shard_map.94), channel_id=1, source_target_pairs={{0,6},{2,4},{4,2},{6,0},{8,14},{10,12},{12,10},{14,8},{1,7},{3,5},... | collective-permute-start | bytes 393224 | tf_op jit(solution)/shard_map/ppermute | solution.py:303
  11.2 0.0 collective-permute-done.5.refs_3_.refs_4_
  11.2 1.6 %collective-permute-start.6 = (bf16[256,128]{1,0:T(8,128)(2,1)S(1)}, bf16[256,128]{1,0:T(8,128)(2,1)S(1)}, u32[]{:S(2)}, u32[]{:S(2)}) collective-permute-start(bf16[256,128]{1,0:T(8,128)(2,1)S(1)} %collective-permute-done.3.second.refs_5_.refs_6_), channel_id=1, source_target_pairs={{0,4},{2,6},{4,0},{6,2},{8,12},{10,14},{12,8},{14,10},{1,5},{3,7},... | collective-permute-start | bytes 196616 | tf_op jit(solution)/shard_map/ppermute | solution.py:303
  12.7 0.0 collective-permute-done.2.refs_1_.refs_2_
  12.7 1.5 %collective-permute-start.4 = (bf16[256,128]{1,0:T(8,128)(2,1)S(1)}, bf16[256,128]{1,0:T(8,128)(2,1)S(1)}, u32[]{:S(2)}, u32[]{:S(2)}) collective-permute-start(bf16[256,128]{1,0:T(8,128)(2,1)S(1)} %collective-permute-done.3.second.refs_5_.refs_6_), channel_id=1, source_target_pairs={{0,2},{2,0},{4,6},{6,4},{8,10},{10,8},{12,14},{14,12},{1,3},{3,1},... | collective-permute-start | bytes 196616 | tf_op jit(solution)/shard_map/ppermute | solution.py:303
  14.3 2.1 %collective-permute-done.6.refs_4_.refs_5_ = bf16[256,128]{1,0:T(8,128)(2,1)S(1)} collective-permute-done((bf16[256,128]{1,0:T(8,128)(2,1)S(1)}, bf16[256,128]{1,0:T(8,128)(2,1)S(1)}, u32[]{:S(2)}, u32[]{:S(2)}) %collective-permute-start.6) | collective-permute-done | bytes 65568 | tf_op jit(solution)/shard_map/ppermute | solution.py:303
  16.4 1.0 %collective-permute-done.4.refs_2_.refs_3_ = bf16[256,128]{1,0:T(8,128)(2,1)S(1)} collective-permute-done((bf16[256,128]{1,0:T(8,128)(2,1)S(1)}, bf16[256,128]{1,0:T(8,128)(2,1)S(1)}, u32[]{:S(2)}, u32[]{:S(2)}) %collective-permute-start.4) | collective-permute-done | bytes 65568 | tf_op jit(solution)/shard_map/ppermute | solution.py:303
  17.3 0.0 collective-permute-done.q_other
  17.3 0.0 collective-permute-done.1.g_other
  17.3 0.0 collective-permute-done.7.refs_6_.refs_7_
  17.3 0.0 copy-done
  17.4 0.0 copy-done.1
  17.4 2.0 %shard_map.95 = (f32[256,128]{1,0:T(8,128)S(1)}, bf16[256,128]{1,0:T(8,128)(2,1)S(1)}, bf16[256,128]{1,0:T(8,128)(2,1)S(1)}, bf16[256,128]{1,0:T(8,128)(2,1)S(1)...) custom-call(s32[1024]{0:T(1024)S(1)} %get-tuple-element.17.balance_i, ...), custom_call_target="tpu_custom_call" | custom-call | tf_op jit(solution)/shard_map/pallas_call | solution.py:214
  19.4 1.1 %collective-permute-start.8 = (bf16[256,128]{1,0:T(8,128)(2,1)S(1)}, bf16[256,128]{1,0:T(8,128)(2,1)S(1)}, u32[]{:S(2)}, u32[]{:S(2)}) collective-permute-start(bf16[256,128]{1,0:T(8,128)(2,1)S(1)} %get-tuple-element.21), channel_id=1, source_target_pairs={{0,6},{2,4},{4,2},{6,0},{8,14},{10,12},{12,10},{14,8},{1,7},{3,5},... | collective-permute-start | bytes 196616 | tf_op jit(solution)/shard_map/ppermute | solution.py:303
  20.6 1.6 %collective-permute-start.9 = (bf16[256,128]{1,0:T(8,128)(2,1)S(1)}, bf16[256,128]{1,0:T(8,128)(2,1)S(1)}, u32[]{:S(2)}, u32[]{:S(2)}) collective-permute-start(bf16[256,128]{1,0:T(8,128)(2,1)S(1)} %get-tuple-element.22), channel_id=1, source_target_pairs={{0,4},{2,6},{4,0},{6,2},{8,12},{10,14},{12,8},{14,10},{1,5},{3,7},... | collective-permute-start | bytes 196616 | tf_op jit(solution)/shard_map/ppermute | solution.py:303
  22.1 0.8 %collective-permute-start.10 = (bf16[256,128]{1,0:T(8,128)(2,1)S(1)}, bf16[256,128]{1,0:T(8,128)(2,1)S(1)}, u32[]{:S(2)}, u32[]{:S(2)}) collective-permute-start(bf16[256,128]{1,0:T(8,128)(2,1)S(1)} %get-tuple-element.23), channel_id=1, source_target_pairs={{0,2},{2,0},{4,6},{6,4},{8,10},{10,8},{12,14},{14,12},{1,3},{3,1},... | collective-permute-start | bytes 196616 | tf_op jit(solution)/shard_map/ppermute | solution.py:303
  23.0 1.1 %collective-permute-start.12 = (bf16[256,128]{1,0:T(8,128)(2,1)S(1)}, bf16[256,128]{1,0:T(8,128)(2,1)S(1)}, u32[]{:S(2)}, u32[]{:S(2)}) collective-permute-start(bf16[256,128]{1,0:T(8,128)(2,1)S(1)} %get-tuple-element.27), channel_id=1, source_target_pairs={{0,6},{2,4},{4,2},{6,0},{8,14},{10,12},{12,10},{14,8},{1,7},{3,5},... | collective-permute-start | bytes 196616 | tf_op jit(solution)/shard_map/ppermute | solution.py:303
  24.0 0.8 %collective-permute-start.13 = (bf16[256,128]{1,0:T(8,128)(2,1)S(1)}, bf16[256,128]{1,0:T(8,128)(2,1)S(1)}, u32[]{:S(2)}, u32[]{:S(2)}) collective-permute-start(bf16[256,128]{1,0:T(8,128)(2,1)S(1)} %get-tuple-element.28), channel_id=1, source_target_pairs={{0,2},{2,0},{4,6},{6,4},{8,10},{10,8},{12,14},{14,12},{1,3},{3,1},... | collective-permute-start | bytes 196616 | tf_op jit(solution)/shard_map/ppermute | solution.py:303
  24.9 0.4 %collective-permute-done.8 = bf16[256,128]{1,0:T(8,128)(2,1)S(1)} collective-permute-done((bf16[256,128]{1,0:T(8,128)(2,1)S(1)}, bf16[256,128]{1,0:T(8,128)(2,1)S(1)}, u32[]{:S(2)}, u32[]{:S(2)}) %collective-permute-start.8) | collective-permute-done | bytes 65568 | tf_op jit(solution)/shard_map/ppermute | solution.py:303
  25.3 1.1 %collective-permute-start.14 = (bf16[256,128]{1,0:T(8,128)(2,1)S(1)}, bf16[256,128]{1,0:T(8,128)(2,1)S(1)}, u32[]{:S(2)}, u32[]{:S(2)}) collective-permute-start(bf16[256,128]{1,0:T(8,128)(2,1)S(1)} %get-tuple-element.29), channel_id=1, source_target_pairs={{0,4},{2,6},{4,0},{6,2},{8,12},{10,14},{12,8},{14,10},{1,5},{3,7},... | collective-permute-start | bytes 196616 | tf_op jit(solution)/shard_map/ppermute | solution.py:303
  26.5 0.0 collective-permute-done.9
  26.5 0.0 collective-permute-done.10
  26.5 2.0 %collective-permute-start.11 = (bf16[256,128]{1,0:T(8,128)(2,1)S(1)}, bf16[256,128]{1,0:T(8,128)(2,1)S(1)}, u32[]{:S(2)}, u32[]{:S(2)}) collective-permute-start(bf16[256,128]{1,0:T(8,128)(2,1)S(1)} %add_convert_fusion.1.refs_0_), channel_id=1, source_target_pairs={{0,8},{2,10},{4,12},{6,14},{8,0},{10,2},{12,4},{14,6},{1,9},{3,11}... | collective-permute-start | bytes 196616 | tf_op jit(solution)/shard_map/ppermute | solution.py:303
  28.5 2.9 %shard_map.96 = (bf16[512,128]{1,0:T(8,128)(2,1)}, bf16[512,128]{1,0:T(8,128)(2,1)}) custom-call(s32[1024]{0:T(1024)S(1)} %get-tuple-element.17.balance_in, s32[8]{0:T(128)S(1)} %get-tuple-element.18.docs_in, bf16[512,128]{1,0:T(8,128)(2,1)S(1)} %bitcast.6, bf16[512,128]{1,0:T(8,128)(2,1)S(1)} %bitcast.9, bf16[256,128]{1,0:T(8,128)(2,1)S(1)} %add_convert_fusion.1.refs_0_, ...), custom_call_target="tpu_custom_call" | custom-call | tf_op jit(solution)/shard_map/pallas_call | solution.py:276
  31.4 0.0 collective-permute-done.12
  31.4 0.0 collective-permute-done.13
  31.4 0.0 collective-permute-done.14
  31.4 0.3 collective-permute-done.11
  31.8 0.6 %fusion = (bf16[128,128]{1,0:T(8,128)(2,1)}, bf16[128,128]{1,0:T(8,128)(2,1)}) fusion(bf16[256,128]{1,0:T(8,128)(2,1)S(1)} %add_convert_fusion), kind=kLoop, calls=%fused_computation.2 | loop fusion | bytes 131072 | tf_op jit(solution)/shard_map/slice | solution.py:341
  (3 shorter events, 0.1 us)
Async XLA Ops:
  1.5 9.2 %collective-permute-start.3 = (bf16[256,128]{1,0:T(8,128)(2,1)S(1)}, bf16[256,128]{1,0:T(8,128)(2,1)S(1)}, u32[]{:S(2)}, u32[]{:S(2)}) collective-permute-start(bf16[256,128]{1,0:T(8,128)(2,1)S(1)} %get-tuple-element.19.first.refs_0_.refs_1_), channel_id=1, source_target_pairs={{0,8},{2,10},{4,12},{6,14},{8,0},{10,2},{12,4},{14,6},{1,9},{3,11}... | collective-permute-start | bytes 196616 | tf_op jit(solution)/shard_map/ppermute | solution.py:303
  5.6 5.6 %collective-permute-start.5 = (bf16[256,128]{1,0:T(8,128)(2,1)S(1)}, bf16[256,128]{1,0:T(8,128)(2,1)S(1)}, u32[]{:S(2)}, u32[]{:S(2)}) collective-permute-start(bf16[256,128]{1,0:T(8,128)(2,1)S(1)} %get-tuple-element.19.first.refs_0_.refs_1_), channel_id=1, source_target_pairs={{0,4},{2,6},{4,0},{6,2},{8,12},{10,14},{12,8},{14,10},{1,5},{3,7},... | collective-permute-start | bytes 196616 | tf_op jit(solution)/shard_map/ppermute | solution.py:303
  7.1 5.6 %collective-permute-start.2 = (bf16[256,128]{1,0:T(8,128)(2,1)S(1)}, bf16[256,128]{1,0:T(8,128)(2,1)S(1)}, u32[]{:S(2)}, u32[]{:S(2)}) collective-permute-start(bf16[256,128]{1,0:T(8,128)(2,1)S(1)} %get-tuple-element.19.first.refs_0_.refs_1_), channel_id=1, source_target_pairs={{0,2},{2,0},{4,6},{6,4},{8,10},{10,8},{12,14},{14,12},{1,3},{3,1},... | collective-permute-start | bytes 196616 | tf_op jit(solution)/shard_map/ppermute | solution.py:303
  8.7 8.7 %collective-permute-start = (bf16[512,128]{1,0:T(8,128)(2,1)}, bf16[512,128]{1,0:T(8,128)(2,1)S(1)}, u32[]{:S(2)}, u32[]{:S(2)}) collective-permute-start(bf16[512,128]{1,0:T(8,128)(2,1)} %bitcast.4), channel_id=1, source_target_pairs={{0,1},{1,0},{2,3},{3,2},{4,5},{5,4},{6,7},{7,6},{8,9},{9,8},{10,11... | collective-permute-start | bytes 393224 | tf_op jit(solution)/shard_map/ppermute | solution.py:311
  10.1 7.2 %copy-start = (bf16[128,4,128]{2,1,0:T(4,128)(2,1)S(1)}, bf16[128,4,128]{2,1,0:T(4,128)(2,1)}, u32[]{:S(2)}) copy-start(bf16[128,4,128]{2,1,0:T(4,128)(2,1)} %param.6) | copy-start | bytes 393220
  10.1 7.2 %copy-start.1 = (bf16[128,4,128]{2,1,0:T(4,128)(2,1)S(1)}, bf16[128,4,128]{2,1,0:T(4,128)(2,1)}, u32[]{:S(2)}) copy-start(bf16[128,4,128]{2,1,0:T(4,128)(2,1)} %param.9) | copy-start | bytes 393220
  10.1 7.2 %collective-permute-start.1 = (bf16[512,128]{1,0:T(8,128)(2,1)}, bf16[512,128]{1,0:T(8,128)(2,1)S(1)}, u32[]{:S(2)}, u32[]{:S(2)}) collective-permute-start(bf16[512,128]{1,0:T(8,128)(2,1)} %bitcast.7), channel_id=1, source_target_pairs={{0,1},{1,0},{2,3},{3,2},{4,5},{5,4},{6,7},{7,6},{8,9},{9,8},{10,11... | collective-permute-start | bytes 393224 | tf_op jit(solution)/shard_map/ppermute | solution.py:311
  10.7 6.6 %collective-permute-start.7 = (bf16[512,128]{1,0:T(8,128)(2,1)S(1)}, bf16[512,128]{1,0:T(8,128)(2,1)S(1)}, u32[]{:S(2)}, u32[]{:S(2)}) collective-permute-start(bf16[512,128]{1,0:T(8,128)(2,1)S(1)} %shard_map.94), channel_id=1, source_target_pairs={{0,6},{2,4},{4,2},{6,0},{8,14},{10,12},{12,10},{14,8},{1,7},{3,5},... | collective-permute-start | bytes 393224 | tf_op jit(solution)/shard_map/ppermute | solution.py:303
  11.2 5.2 %collective-permute-start.6 = (bf16[256,128]{1,0:T(8,128)(2,1)S(1)}, bf16[256,128]{1,0:T(8,128)(2,1)S(1)}, u32[]{:S(2)}, u32[]{:S(2)}) collective-permute-start(bf16[256,128]{1,0:T(8,128)(2,1)S(1)} %collective-permute-done.3.second.refs_5_.refs_6_), channel_id=1, source_target_pairs={{0,4},{2,6},{4,0},{6,2},{8,12},{10,14},{12,8},{14,10},{1,5},{3,7},... | collective-permute-start | bytes 196616 | tf_op jit(solution)/shard_map/ppermute | solution.py:303
  12.7 4.6 %collective-permute-start.4 = (bf16[256,128]{1,0:T(8,128)(2,1)S(1)}, bf16[256,128]{1,0:T(8,128)(2,1)S(1)}, u32[]{:S(2)}, u32[]{:S(2)}) collective-permute-start(bf16[256,128]{1,0:T(8,128)(2,1)S(1)} %collective-permute-done.3.second.refs_5_.refs_6_), channel_id=1, source_target_pairs={{0,2},{2,0},{4,6},{6,4},{8,10},{10,8},{12,14},{14,12},{1,3},{3,1},... | collective-permute-start | bytes 196616 | tf_op jit(solution)/shard_map/ppermute | solution.py:303
  19.4 5.9 %collective-permute-start.8 = (bf16[256,128]{1,0:T(8,128)(2,1)S(1)}, bf16[256,128]{1,0:T(8,128)(2,1)S(1)}, u32[]{:S(2)}, u32[]{:S(2)}) collective-permute-start(bf16[256,128]{1,0:T(8,128)(2,1)S(1)} %get-tuple-element.21), channel_id=1, source_target_pairs={{0,6},{2,4},{4,2},{6,0},{8,14},{10,12},{12,10},{14,8},{1,7},{3,5},... | collective-permute-start | bytes 196616 | tf_op jit(solution)/shard_map/ppermute | solution.py:303
  20.6 5.9 %collective-permute-start.9 = (bf16[256,128]{1,0:T(8,128)(2,1)S(1)}, bf16[256,128]{1,0:T(8,128)(2,1)S(1)}, u32[]{:S(2)}, u32[]{:S(2)}) collective-permute-start(bf16[256,128]{1,0:T(8,128)(2,1)S(1)} %get-tuple-element.22), channel_id=1, source_target_pairs={{0,4},{2,6},{4,0},{6,2},{8,12},{10,14},{12,8},{14,10},{1,5},{3,7},... | collective-permute-start | bytes 196616 | tf_op jit(solution)/shard_map/ppermute | solution.py:303
  22.1 4.3 %collective-permute-start.10 = (bf16[256,128]{1,0:T(8,128)(2,1)S(1)}, bf16[256,128]{1,0:T(8,128)(2,1)S(1)}, u32[]{:S(2)}, u32[]{:S(2)}) collective-permute-start(bf16[256,128]{1,0:T(8,128)(2,1)S(1)} %get-tuple-element.23), channel_id=1, source_target_pairs={{0,2},{2,0},{4,6},{6,4},{8,10},{10,8},{12,14},{14,12},{1,3},{3,1},... | collective-permute-start | bytes 196616 | tf_op jit(solution)/shard_map/ppermute | solution.py:303
  23.0 8.4 %collective-permute-start.12 = (bf16[256,128]{1,0:T(8,128)(2,1)S(1)}, bf16[256,128]{1,0:T(8,128)(2,1)S(1)}, u32[]{:S(2)}, u32[]{:S(2)}) collective-permute-start(bf16[256,128]{1,0:T(8,128)(2,1)S(1)} %get-tuple-element.27), channel_id=1, source_target_pairs={{0,6},{2,4},{4,2},{6,0},{8,14},{10,12},{12,10},{14,8},{1,7},{3,5},... | collective-permute-start | bytes 196616 | tf_op jit(solution)/shard_map/ppermute | solution.py:303
  24.0 7.4 %collective-permute-start.13 = (bf16[256,128]{1,0:T(8,128)(2,1)S(1)}, bf16[256,128]{1,0:T(8,128)(2,1)S(1)}, u32[]{:S(2)}, u32[]{:S(2)}) collective-permute-start(bf16[256,128]{1,0:T(8,128)(2,1)S(1)} %get-tuple-element.28), channel_id=1, source_target_pairs={{0,2},{2,0},{4,6},{6,4},{8,10},{10,8},{12,14},{14,12},{1,3},{3,1},... | collective-permute-start | bytes 196616 | tf_op jit(solution)/shard_map/ppermute | solution.py:303
  25.3 6.1 %collective-permute-start.14 = (bf16[256,128]{1,0:T(8,128)(2,1)S(1)}, bf16[256,128]{1,0:T(8,128)(2,1)S(1)}, u32[]{:S(2)}, u32[]{:S(2)}) collective-permute-start(bf16[256,128]{1,0:T(8,128)(2,1)S(1)} %get-tuple-element.29), channel_id=1, source_target_pairs={{0,4},{2,6},{4,0},{6,2},{8,12},{10,14},{12,8},{14,10},{1,5},{3,7},... | collective-permute-start | bytes 196616 | tf_op jit(solution)/shard_map/ppermute | solution.py:303
  26.5 5.2 %collective-permute-start.11 = (bf16[256,128]{1,0:T(8,128)(2,1)S(1)}, bf16[256,128]{1,0:T(8,128)(2,1)S(1)}, u32[]{:S(2)}, u32[]{:S(2)}) collective-permute-start(bf16[256,128]{1,0:T(8,128)(2,1)S(1)} %add_convert_fusion.1.refs_0_), channel_id=1, source_target_pairs={{0,8},{2,10},{4,12},{6,14},{8,0},{10,2},{12,4},{14,6},{1,9},{3,11}... | collective-permute-start | bytes 196616 | tf_op jit(solution)/shard_map/ppermute | solution.py:303

commit v7 on v6

--- a/solution.py
+++ b/solution.py
@@ -28,10 +28,10 @@
 
 
 MERGED = (3,)
-BLOCK_ORDER = (0, 1, 5, 2, 6, 4, 7, 3)
+BLOCK_ORDER = (0, 6, 4, 1, 2, 5, 3, 7)
 FAR_ORDER = (5, 6, 7)
 BACK_ORDER = (7, 6, 5)
-SUM_ORDER = (4, 3, 1, 2)
+SUM_ORDER = (1, 2, 3, 4)
 
 
 def high_bits(n_ctx):

time: 32.6 us -> 32.4 us (level)
  waiting for transfers between devices: 3.85 us -> 2.88 us
  starting transfers between devices: 21.4 us -> 22.2 us
    ppermute x13, waiting for transfers between devices: 3.84 us -> 2.87 us  [swap(): return lax.ppermute(array, 'ctx', [(i, i ^ k) for i in range(n_ctx)])]
    ppermute x13, starting transfers between devices: 19.4 us -> 20.1 us  [swap(): return lax.ppermute(array, 'ctx', [(i, i ^ k) for i in range(n_ctx)])]
  transfers between devices with their start and end apart: 15 -> 15, of which waited for: 4 -> 3; matrix products, arithmetic and copies ran while one was open for 0% -> 0% of each run, Pallas kernels for 9% -> 9%
where the time goes in v7:
time: 32.4 us; the launch traced here: 32.2 us
  starting transfers between devices  22.2 us (69%)
  Pallas kernels  5.73 us (18%)
  waiting for transfers between devices  2.88 us (9%)
  between operations  0.73 us (2%)
  local copies, waits for them, and re-layouts  0.64 us (2%)
    ppermute x13, starting transfers between devices, swap(): return lax.ppermute(array, 'ctx', [(i, i ^ k) for i in range(n_ctx)])  20.1 us
    ppermute x13, waiting for transfers between devices, swap(): return lax.ppermute(array, 'ctx', [(i, i ^ k) for i in range(n_ctx)])  2.87 us
    pallas_call x1, Pallas kernels, query_side(): pl.pallas_call(functools.partial(rows_kernel, len(after), listed, heads,...  2.87 us
    pallas_call x1, Pallas kernels, gradient_terms(): pl.pallas_call(functools.partial(terms_kernel, listed, heads, reach), out...  2.04 us
    ppermute x2, starting transfers between devices, body(): lax.ppermute(array, 'head', [(i, n_head - 1 - i) for i in range(n_head)])  2.03 us
    pallas_call x1, Pallas kernels, pack(): pl.pallas_call(pack_kernel, out_shape=[jax.ShapeDtypeStruct((2 * key_rows...  0.81 us
  transfers between devices with their start and end apart: 15, of which 3 were waited for; matrix products, arithmetic and copies ran while one was open for 0% of the time, Pallas kernels for 9%

profile of v7, /device:TPU:0, one launch (start us, length us, event | category | flops | bytes accessed | tf_op | source)
XLA Modules:
  0.0 32.2 jit_solution(1814526655736544695)
XLA Ops:
  0.6 0.8 %shard_map.93 = (bf16[256,128]{1,0:T(8,128)(2,1)S(1)}, s32[1024]{0:T(1024)S(1)}, s32[8]{0:T(128)S(1)}) custom-call(bf16[128,128]{1,0:T(8,128)(2,1)} %key_rows.1, bf16[128,128]{1,0:T(8,128)(2,1)} %value_rows.1, s32[1024]{0:T(1024)} %balance.1, s32[8]{0:T(128)} %doc_lengths.1), custom_call_target="tpu_custom_call" | custom-call | tf_op jit(solution)/shard_map/pallas_call | solution.py:72
  1.5 4.1 %collective-permute-start.2 = (bf16[256,128]{1,0:T(8,128)(2,1)S(1)}, bf16[256,128]{1,0:T(8,128)(2,1)S(1)}, u32[]{:S(2)}, u32[]{:S(2)}) collective-permute-start(bf16[256,128]{1,0:T(8,128)(2,1)S(1)} %get-tuple-element.19.first.refs_0_.refs_1_), channel_id=1, source_target_pairs={{0,8},{2,10},{4,12},{6,14},{8,0},{10,2},{12,4},{14,6},{1,9},{3,11}... | collective-permute-start | bytes 196616 | tf_op jit(solution)/shard_map/ppermute | solution.py:303
  5.6 1.6 %collective-permute-start.5 = (bf16[256,128]{1,0:T(8,128)(2,1)S(1)}, bf16[256,128]{1,0:T(8,128)(2,1)S(1)}, u32[]{:S(2)}, u32[]{:S(2)}) collective-permute-start(bf16[256,128]{1,0:T(8,128)(2,1)S(1)} %get-tuple-element.19.first.refs_0_.refs_1_), channel_id=1, source_target_pairs={{0,4},{2,6},{4,0},{6,2},{8,12},{10,14},{12,8},{14,10},{1,5},{3,7},... | collective-permute-start | bytes 196616 | tf_op jit(solution)/shard_map/ppermute | solution.py:303
  7.1 1.5 %collective-permute-start.4 = (bf16[256,128]{1,0:T(8,128)(2,1)S(1)}, bf16[256,128]{1,0:T(8,128)(2,1)S(1)}, u32[]{:S(2)}, u32[]{:S(2)}) collective-permute-start(bf16[256,128]{1,0:T(8,128)(2,1)S(1)} %get-tuple-element.19.first.refs_0_.refs_1_), channel_id=1, source_target_pairs={{0,2},{2,0},{4,6},{6,4},{8,10},{10,8},{12,14},{14,12},{1,3},{3,1},... | collective-permute-start | bytes 196616 | tf_op jit(solution)/shard_map/ppermute | solution.py:303
  8.7 1.5 %collective-permute-start = (bf16[512,128]{1,0:T(8,128)(2,1)}, bf16[512,128]{1,0:T(8,128)(2,1)S(1)}, u32[]{:S(2)}, u32[]{:S(2)}) collective-permute-start(bf16[512,128]{1,0:T(8,128)(2,1)} %bitcast.4), channel_id=1, source_target_pairs={{0,1},{1,0},{2,3},{3,2},{4,5},{5,4},{6,7},{7,6},{8,9},{9,8},{10,11... | collective-permute-start | bytes 393224 | tf_op jit(solution)/shard_map/ppermute | solution.py:311
  10.1 0.0 copy-start
  10.1 0.0 copy-start.1
  10.1 0.5 %collective-permute-start.1 = (bf16[512,128]{1,0:T(8,128)(2,1)}, bf16[512,128]{1,0:T(8,128)(2,1)S(1)}, u32[]{:S(2)}, u32[]{:S(2)}) collective-permute-start(bf16[512,128]{1,0:T(8,128)(2,1)} %bitcast.7), channel_id=1, source_target_pairs={{0,1},{1,0},{2,3},{3,2},{4,5},{5,4},{6,7},{7,6},{8,9},{9,8},{10,11... | collective-permute-start | bytes 393224 | tf_op jit(solution)/shard_map/ppermute | solution.py:311
  10.7 0.0 collective-permute-done.2.second.refs_2_.refs_3_
  10.7 0.5 %collective-permute-start.7 = (bf16[512,128]{1,0:T(8,128)(2,1)S(1)}, bf16[512,128]{1,0:T(8,128)(2,1)S(1)}, u32[]{:S(2)}, u32[]{:S(2)}) collective-permute-start(bf16[512,128]{1,0:T(8,128)(2,1)S(1)} %shard_map.94), channel_id=1, source_target_pairs={{0,6},{2,4},{4,2},{6,0},{8,14},{10,12},{12,10},{14,8},{1,7},{3,5},... | collective-permute-start | bytes 393224 | tf_op jit(solution)/shard_map/ppermute | solution.py:303
  11.2 0.0 collective-permute-done.5.refs_4_.refs_5_
  11.2 1.5 %collective-permute-start.6 = (bf16[256,128]{1,0:T(8,128)(2,1)S(1)}, bf16[256,128]{1,0:T(8,128)(2,1)S(1)}, u32[]{:S(2)}, u32[]{:S(2)}) collective-permute-start(bf16[256,128]{1,0:T(8,128)(2,1)S(1)} %collective-permute-done.2.second.refs_2_.refs_3_), channel_id=1, source_target_pairs={{0,2},{2,0},{4,6},{6,4},{8,10},{10,8},{12,14},{14,12},{1,3},{3,1},... | collective-permute-start | bytes 196616 | tf_op jit(solution)/shard_map/ppermute | solution.py:303
  12.7 0.0 collective-permute-done.4.refs_3_.refs_4_
  12.7 1.6 %collective-permute-start.3 = (bf16[256,128]{1,0:T(8,128)(2,1)S(1)}, bf16[256,128]{1,0:T(8,128)(2,1)S(1)}, u32[]{:S(2)}, u32[]{:S(2)}) collective-permute-start(bf16[256,128]{1,0:T(8,128)(2,1)S(1)} %collective-permute-done.2.second.refs_2_.refs_3_), channel_id=1, source_target_pairs={{0,4},{2,6},{4,0},{6,2},{8,12},{10,14},{12,8},{14,10},{1,5},{3,7},... | collective-permute-start | bytes 196616 | tf_op jit(solution)/shard_map/ppermute | solution.py:303
  14.3 2.6 %collective-permute-done.6.refs_5_.refs_6_ = bf16[256,128]{1,0:T(8,128)(2,1)S(1)} collective-permute-done((bf16[256,128]{1,0:T(8,128)(2,1)S(1)}, bf16[256,128]{1,0:T(8,128)(2,1)S(1)}, u32[]{:S(2)}, u32[]{:S(2)}) %collective-permute-start.6) | collective-permute-done | bytes 65568 | tf_op jit(solution)/shard_map/ppermute | solution.py:303
  16.8 0.1 collective-permute-done.3.refs_1_.refs_2_
  17.0 0.0 collective-permute-done.q_other
  17.0 0.0 collective-permute-done.1.g_other
  17.0 0.0 collective-permute-done.7.refs_6_.refs_7_
  17.0 0.0 copy-done
  17.0 0.0 copy-done.1
  17.0 2.0 %shard_map.95 = (f32[256,128]{1,0:T(8,128)S(1)}, bf16[256,128]{1,0:T(8,128)(2,1)S(1)}, bf16[256,128]{1,0:T(8,128)(2,1)S(1)}, bf16[256,128]{1,0:T(8,128)(2,1)S(1)...) custom-call(s32[1024]{0:T(1024)S(1)} %get-tuple-element.17.balance_i, ...), custom_call_target="tpu_custom_call" | custom-call | tf_op jit(solution)/shard_map/pallas_call | solution.py:214
  19.0 1.6 %collective-permute-start.8 = (bf16[256,128]{1,0:T(8,128)(2,1)S(1)}, bf16[256,128]{1,0:T(8,128)(2,1)S(1)}, u32[]{:S(2)}, u32[]{:S(2)}) collective-permute-start(bf16[256,128]{1,0:T(8,128)(2,1)S(1)} %get-tuple-element.21), channel_id=1, source_target_pairs={{0,6},{2,4},{4,2},{6,0},{8,14},{10,12},{12,10},{14,8},{1,7},{3,5},... | collective-permute-start | bytes 196616 | tf_op jit(solution)/shard_map/ppermute | solution.py:303
  20.6 0.9 %collective-permute-start.9 = (bf16[256,128]{1,0:T(8,128)(2,1)S(1)}, bf16[256,128]{1,0:T(8,128)(2,1)S(1)}, u32[]{:S(2)}, u32[]{:S(2)}) collective-permute-start(bf16[256,128]{1,0:T(8,128)(2,1)S(1)} %get-tuple-element.22), channel_id=1, source_target_pairs={{0,4},{2,6},{4,0},{6,2},{8,12},{10,14},{12,8},{14,10},{1,5},{3,7},... | collective-permute-start | bytes 196616 | tf_op jit(solution)/shard_map/ppermute | solution.py:303
  21.6 1.0 %collective-permute-start.10 = (bf16[256,128]{1,0:T(8,128)(2,1)S(1)}, bf16[256,128]{1,0:T(8,128)(2,1)S(1)}, u32[]{:S(2)}, u32[]{:S(2)}) collective-permute-start(bf16[256,128]{1,0:T(8,128)(2,1)S(1)} %get-tuple-element.23), channel_id=1, source_target_pairs={{0,2},{2,0},{4,6},{6,4},{8,10},{10,8},{12,14},{14,12},{1,3},{3,1},... | collective-permute-start | bytes 196616 | tf_op jit(solution)/shard_map/ppermute | solution.py:303
  22.6 1.0 %collective-permute-start.11 = (bf16[256,128]{1,0:T(8,128)(2,1)S(1)}, bf16[256,128]{1,0:T(8,128)(2,1)S(1)}, u32[]{:S(2)}, u32[]{:S(2)}) collective-permute-start(bf16[256,128]{1,0:T(8,128)(2,1)S(1)} %get-tuple-element.27), channel_id=1, source_target_pairs={{0,2},{2,0},{4,6},{6,4},{8,10},{10,8},{12,14},{14,12},{1,3},{3,1},... | collective-permute-start | bytes 196616 | tf_op jit(solution)/shard_map/ppermute | solution.py:303
  23.6 1.1 %collective-permute-start.12 = (bf16[256,128]{1,0:T(8,128)(2,1)S(1)}, bf16[256,128]{1,0:T(8,128)(2,1)S(1)}, u32[]{:S(2)}, u32[]{:S(2)}) collective-permute-start(bf16[256,128]{1,0:T(8,128)(2,1)S(1)} %get-tuple-element.28), channel_id=1, source_target_pairs={{0,4},{2,6},{4,0},{6,2},{8,12},{10,14},{12,8},{14,10},{1,5},{3,7},... | collective-permute-start | bytes 196616 | tf_op jit(solution)/shard_map/ppermute | solution.py:303
  24.7 0.0 collective-permute-done.8
  24.7 1.5 %collective-permute-start.13 = (bf16[256,128]{1,0:T(8,128)(2,1)S(1)}, bf16[256,128]{1,0:T(8,128)(2,1)S(1)}, u32[]{:S(2)}, u32[]{:S(2)}) collective-permute-start(bf16[256,128]{1,0:T(8,128)(2,1)S(1)} %get-tuple-element.29), channel_id=1, source_target_pairs={{0,6},{2,4},{4,2},{6,0},{8,14},{10,12},{12,10},{14,8},{1,7},{3,5},... | collective-permute-start | bytes 196616 | tf_op jit(solution)/shard_map/ppermute | solution.py:303
  26.3 0.0 collective-permute-done.9
  26.3 0.0 collective-permute-done.10
  26.3 2.2 %collective-permute-start.14 = (bf16[256,128]{1,0:T(8,128)(2,1)S(1)}, bf16[256,128]{1,0:T(8,128)(2,1)S(1)}, u32[]{:S(2)}, u32[]{:S(2)}) collective-permute-start(bf16[256,128]{1,0:T(8,128)(2,1)S(1)} %add_convert_fusion.1.refs_0_), channel_id=1, source_target_pairs={{0,8},{2,10},{4,12},{6,14},{8,0},{10,2},{12,4},{14,6},{1,9},{3,11}... | collective-permute-start | bytes 196616 | tf_op jit(solution)/shard_map/ppermute | solution.py:303
  28.5 2.9 %shard_map.96 = (bf16[512,128]{1,0:T(8,128)(2,1)}, bf16[512,128]{1,0:T(8,128)(2,1)}) custom-call(s32[1024]{0:T(1024)S(1)} %get-tuple-element.17.balance_in, s32[8]{0:T(128)S(1)} %get-tuple-element.18.docs_in, bf16[512,128]{1,0:T(8,128)(2,1)S(1)} %bitcast.6, bf16[512,128]{1,0:T(8,128)(2,1)S(1)} %bitcast.9, bf16[256,128]{1,0:T(8,128)(2,1)S(1)} %add_convert_fusion.1.refs_0_, ...), custom_call_target="tpu_custom_call" | custom-call | tf_op jit(solution)/shard_map/pallas_call | solution.py:276
  31.4 0.0 collective-permute-done.11
  31.4 0.0 collective-permute-done.12
  31.4 0.0 collective-permute-done.13
  31.4 0.1 collective-permute-done.14
  31.6 0.6 %fusion = (bf16[128,128]{1,0:T(8,128)(2,1)}, bf16[128,128]{1,0:T(8,128)(2,1)}) fusion(bf16[256,128]{1,0:T(8,128)(2,1)S(1)} %add_convert_fusion), kind=kLoop, calls=%fused_computation.2 | loop fusion | bytes 131072 | tf_op jit(solution)/shard_map/slice | solution.py:341
  (3 shorter events, 0.1 us)
Async XLA Ops:
  1.5 9.2 %collective-permute-start.2 = (bf16[256,128]{1,0:T(8,128)(2,1)S(1)}, bf16[256,128]{1,0:T(8,128)(2,1)S(1)}, u32[]{:S(2)}, u32[]{:S(2)}) collective-permute-start(bf16[256,128]{1,0:T(8,128)(2,1)S(1)} %get-tuple-element.19.first.refs_0_.refs_1_), channel_id=1, source_target_pairs={{0,8},{2,10},{4,12},{6,14},{8,0},{10,2},{12,4},{14,6},{1,9},{3,11}... | collective-permute-start | bytes 196616 | tf_op jit(solution)/shard_map/ppermute | solution.py:303
  5.6 5.6 %collective-permute-start.5 = (bf16[256,128]{1,0:T(8,128)(2,1)S(1)}, bf16[256,128]{1,0:T(8,128)(2,1)S(1)}, u32[]{:S(2)}, u32[]{:S(2)}) collective-permute-start(bf16[256,128]{1,0:T(8,128)(2,1)S(1)} %get-tuple-element.19.first.refs_0_.refs_1_), channel_id=1, source_target_pairs={{0,4},{2,6},{4,0},{6,2},{8,12},{10,14},{12,8},{14,10},{1,5},{3,7},... | collective-permute-start | bytes 196616 | tf_op jit(solution)/shard_map/ppermute | solution.py:303
  7.1 5.6 %collective-permute-start.4 = (bf16[256,128]{1,0:T(8,128)(2,1)S(1)}, bf16[256,128]{1,0:T(8,128)(2,1)S(1)}, u32[]{:S(2)}, u32[]{:S(2)}) collective-permute-start(bf16[256,128]{1,0:T(8,128)(2,1)S(1)} %get-tuple-element.19.first.refs_0_.refs_1_), channel_id=1, source_target_pairs={{0,2},{2,0},{4,6},{6,4},{8,10},{10,8},{12,14},{14,12},{1,3},{3,1},... | collective-permute-start | bytes 196616 | tf_op jit(solution)/shard_map/ppermute | solution.py:303
  8.7 8.3 %collective-permute-start = (bf16[512,128]{1,0:T(8,128)(2,1)}, bf16[512,128]{1,0:T(8,128)(2,1)S(1)}, u32[]{:S(2)}, u32[]{:S(2)}) collective-permute-start(bf16[512,128]{1,0:T(8,128)(2,1)} %bitcast.4), channel_id=1, source_target_pairs={{0,1},{1,0},{2,3},{3,2},{4,5},{5,4},{6,7},{7,6},{8,9},{9,8},{10,11... | collective-permute-start | bytes 393224 | tf_op jit(solution)/shard_map/ppermute | solution.py:311
  10.1 6.8 %copy-start = (bf16[128,4,128]{2,1,0:T(4,128)(2,1)S(1)}, bf16[128,4,128]{2,1,0:T(4,128)(2,1)}, u32[]{:S(2)}) copy-start(bf16[128,4,128]{2,1,0:T(4,128)(2,1)} %param.6) | copy-start | bytes 393220
  10.1 6.8 %copy-start.1 = (bf16[128,4,128]{2,1,0:T(4,128)(2,1)S(1)}, bf16[128,4,128]{2,1,0:T(4,128)(2,1)}, u32[]{:S(2)}) copy-start(bf16[128,4,128]{2,1,0:T(4,128)(2,1)} %param.9) | copy-start | bytes 393220
  10.1 6.8 %collective-permute-start.1 = (bf16[512,128]{1,0:T(8,128)(2,1)}, bf16[512,128]{1,0:T(8,128)(2,1)S(1)}, u32[]{:S(2)}, u32[]{:S(2)}) collective-permute-start(bf16[512,128]{1,0:T(8,128)(2,1)} %bitcast.7), channel_id=1, source_target_pairs={{0,1},{1,0},{2,3},{3,2},{4,5},{5,4},{6,7},{7,6},{8,9},{9,8},{10,11... | collective-permute-start | bytes 393224 | tf_op jit(solution)/shard_map/ppermute | solution.py:311
  10.7 6.3 %collective-permute-start.7 = (bf16[512,128]{1,0:T(8,128)(2,1)S(1)}, bf16[512,128]{1,0:T(8,128)(2,1)S(1)}, u32[]{:S(2)}, u32[]{:S(2)}) collective-permute-start(bf16[512,128]{1,0:T(8,128)(2,1)S(1)} %shard_map.94), channel_id=1, source_target_pairs={{0,6},{2,4},{4,2},{6,0},{8,14},{10,12},{12,10},{14,8},{1,7},{3,5},... | collective-permute-start | bytes 393224 | tf_op jit(solution)/shard_map/ppermute | solution.py:303
  11.2 5.7 %collective-permute-start.6 = (bf16[256,128]{1,0:T(8,128)(2,1)S(1)}, bf16[256,128]{1,0:T(8,128)(2,1)S(1)}, u32[]{:S(2)}, u32[]{:S(2)}) collective-permute-start(bf16[256,128]{1,0:T(8,128)(2,1)S(1)} %collective-permute-done.2.second.refs_2_.refs_3_), channel_id=1, source_target_pairs={{0,2},{2,0},{4,6},{6,4},{8,10},{10,8},{12,14},{14,12},{1,3},{3,1},... | collective-permute-start | bytes 196616 | tf_op jit(solution)/shard_map/ppermute | solution.py:303
  12.7 4.3 %collective-permute-start.3 = (bf16[256,128]{1,0:T(8,128)(2,1)S(1)}, bf16[256,128]{1,0:T(8,128)(2,1)S(1)}, u32[]{:S(2)}, u32[]{:S(2)}) collective-permute-start(bf16[256,128]{1,0:T(8,128)(2,1)S(1)} %collective-permute-done.2.second.refs_2_.refs_3_), channel_id=1, source_target_pairs={{0,4},{2,6},{4,0},{6,2},{8,12},{10,14},{12,8},{14,10},{1,5},{3,7},... | collective-permute-start | bytes 196616 | tf_op jit(solution)/shard_map/ppermute | solution.py:303
  19.0 5.7 %collective-permute-start.8 = (bf16[256,128]{1,0:T(8,128)(2,1)S(1)}, bf16[256,128]{1,0:T(8,128)(2,1)S(1)}, u32[]{:S(2)}, u32[]{:S(2)}) collective-permute-start(bf16[256,128]{1,0:T(8,128)(2,1)S(1)} %get-tuple-element.21), channel_id=1, source_target_pairs={{0,6},{2,4},{4,2},{6,0},{8,14},{10,12},{12,10},{14,8},{1,7},{3,5},... | collective-permute-start | bytes 196616 | tf_op jit(solution)/shard_map/ppermute | solution.py:303
  20.6 5.7 %collective-permute-start.9 = (bf16[256,128]{1,0:T(8,128)(2,1)S(1)}, bf16[256,128]{1,0:T(8,128)(2,1)S(1)}, u32[]{:S(2)}, u32[]{:S(2)}) collective-permute-start(bf16[256,128]{1,0:T(8,128)(2,1)S(1)} %get-tuple-element.22), channel_id=1, source_target_pairs={{0,4},{2,6},{4,0},{6,2},{8,12},{10,14},{12,8},{14,10},{1,5},{3,7},... | collective-permute-start | bytes 196616 | tf_op jit(solution)/shard_map/ppermute | solution.py:303
  21.6 4.7 %collective-permute-start.10 = (bf16[256,128]{1,0:T(8,128)(2,1)S(1)}, bf16[256,128]{1,0:T(8,128)(2,1)S(1)}, u32[]{:S(2)}, u32[]{:S(2)}) collective-permute-start(bf16[256,128]{1,0:T(8,128)(2,1)S(1)} %get-tuple-element.23), channel_id=1, source_target_pairs={{0,2},{2,0},{4,6},{6,4},{8,10},{10,8},{12,14},{14,12},{1,3},{3,1},... | collective-permute-start | bytes 196616 | tf_op jit(solution)/shard_map/ppermute | solution.py:303
  22.6 8.8 %collective-permute-start.11 = (bf16[256,128]{1,0:T(8,128)(2,1)S(1)}, bf16[256,128]{1,0:T(8,128)(2,1)S(1)}, u32[]{:S(2)}, u32[]{:S(2)}) collective-permute-start(bf16[256,128]{1,0:T(8,128)(2,1)S(1)} %get-tuple-element.27), channel_id=1, source_target_pairs={{0,2},{2,0},{4,6},{6,4},{8,10},{10,8},{12,14},{14,12},{1,3},{3,1},... | collective-permute-start | bytes 196616 | tf_op jit(solution)/shard_map/ppermute | solution.py:303
  23.6 7.8 %collective-permute-start.12 = (bf16[256,128]{1,0:T(8,128)(2,1)S(1)}, bf16[256,128]{1,0:T(8,128)(2,1)S(1)}, u32[]{:S(2)}, u32[]{:S(2)}) collective-permute-start(bf16[256,128]{1,0:T(8,128)(2,1)S(1)} %get-tuple-element.28), channel_id=1, source_target_pairs={{0,4},{2,6},{4,0},{6,2},{8,12},{10,14},{12,8},{14,10},{1,5},{3,7},... | collective-permute-start | bytes 196616 | tf_op jit(solution)/shard_map/ppermute | solution.py:303
  24.7 6.7 %collective-permute-start.13 = (bf16[256,128]{1,0:T(8,128)(2,1)S(1)}, bf16[256,128]{1,0:T(8,128)(2,1)S(1)}, u32[]{:S(2)}, u32[]{:S(2)}) collective-permute-start(bf16[256,128]{1,0:T(8,128)(2,1)S(1)} %get-tuple-element.29), channel_id=1, source_target_pairs={{0,6},{2,4},{4,2},{6,0},{8,14},{10,12},{12,10},{14,8},{1,7},{3,5},... | collective-permute-start | bytes 196616 | tf_op jit(solution)/shard_map/ppermute | solution.py:303
  26.3 5.2 %collective-permute-start.14 = (bf16[256,128]{1,0:T(8,128)(2,1)S(1)}, bf16[256,128]{1,0:T(8,128)(2,1)S(1)}, u32[]{:S(2)}, u32[]{:S(2)}) collective-permute-start(bf16[256,128]{1,0:T(8,128)(2,1)S(1)} %add_convert_fusion.1.refs_0_), channel_id=1, source_target_pairs={{0,8},{2,10},{4,12},{6,14},{8,0},{10,2},{12,4},{14,6},{1,9},{3,11}... | collective-permute-start | bytes 196616 | tf_op jit(solution)/shard_map/ppermute | solution.py:303

commit v8 on v7

--- a/solution.py
+++ b/solution.py
@@ -164,22 +164,17 @@
             kv_all[pl.ds(pl.multiple_of(owner * rows, rows), rows), :] = block[i * rows : (i + 1) * rows, :]
 
 
-def terms_kernel(listed, heads, reach, balance_in, docs_in, q_own, g_own, q_other, g_other, *refs):
+def terms_kernel(listed, heads, reach, balance_in, docs_in, qg_all, *refs):
     n_ctx, n_blocks = sum(len(ks) for ks in listed), len(listed)
     blocks, outs, scratch = refs[:n_blocks], refs[n_blocks : n_blocks + n_ctx], refs[n_blocks + n_ctx :]
-    qg_all, kv_all, key_win, value_win, terms, *lists = scratch
-    me, head = lax.axis_index("ctx"), lax.axis_index("head")
+    kv_all, key_win, value_win, terms, *lists = scratch
+    me = lax.axis_index("ctx")
     both, width = min(block.shape[0] for block in blocks), blocks[0].shape[1]
     tok_rows = both // 2
     runs_here = tok_rows // RUN
     run_rows = RUN * heads
     copies = start_lists(balance_in, docs_in, lists)
     load_blocks(me, listed, blocks, kv_all)
-    for sources, part in (((q_own, g_own), head), ((q_other, g_other), 1 - head)):
-        at = pl.ds(pl.multiple_of(part * run_rows, run_rows), run_rows)
-        for w, source in enumerate(sources):
-            for r in range(runs_here):
-                qg_all[w, r, at, :] = source[r * run_rows : (r + 1) * run_rows, :]
     terms[...] = jnp.zeros_like(terms)
     finish_lists(copies, lists)
 
@@ -201,7 +196,28 @@
         outs[k][...] = terms[at, :].astype(outs[k].dtype)
 
 
-def gradient_terms(balance, doc_lengths, own, other, blocks, heads, reach):
+def order_kernel(run_rows, q_own, g_own, q_other, g_other, out):
+    head = lax.axis_index("head")
+    for sources, part in (((q_own, g_own), head), ((q_other, g_other), 1 - head)):
+        at = pl.ds(pl.multiple_of(part * run_rows, run_rows), run_rows)
+        for w, source in enumerate(sources):
+            for r in range(out.shape[1]):
+                out[w, r, at, :] = source[r * run_rows : (r + 1) * run_rows, :]
+
+
+def order_heads(own, other, heads, seq_total):
+    rows, width = own[0].shape
+    run_rows = RUN * heads
+    return pl.pallas_call(
+        functools.partial(order_kernel, run_rows),
+        out_shape=jax.ShapeDtypeStruct((2, rows // run_rows, 2 * run_rows, width), jnp.bfloat16),
+        in_specs=[VMEM] * 4,
+        out_specs=VMEM,
+        compiler_params=limit(seq_total),
+    )(*own, *other)
+
+
+def gradient_terms(balance, doc_lengths, by_head, blocks, heads, reach):
     listed, blocks = zip(*blocks)
     n_ctx = sum(len(ks) for ks in listed)
     both, width = min(block.shape[0] for block in blocks), blocks[0].shape[1]
@@ -214,10 +230,9 @@
     return pl.pallas_call(
         functools.partial(terms_kernel, listed, heads, reach),
         out_shape=outs,
-        in_specs=[ANY] * 2 + [VMEM] * (4 + len(blocks)),
+        in_specs=[ANY] * 2 + [VMEM] * (1 + len(blocks)),
         out_specs=[VMEM] * n_ctx,
         scratch_shapes=[
-            pltpu.VMEM((2, runs_here, 2 * RUN * heads, width), jnp.bfloat16),
             pltpu.VMEM((n_ctx * both, width), jnp.bfloat16),
             pltpu.VMEM((runs_here, reach * RUN, width), jnp.bfloat16),
             pltpu.VMEM((runs_here, reach * RUN, width), jnp.bfloat16),
@@ -228,7 +243,7 @@
             pltpu.SemaphoreType.DMA((2,)),
         ],
         compiler_params=limit(balance.shape[0]),
-    )(balance, doc_lengths, *own, *other, *blocks)
+    )(balance, doc_lengths, by_head, *blocks)
 
 
 def rows_kernel(n_after, listed, heads, reach, balance_in, docs_in, q_own, g_own, *refs):
@@ -318,7 +333,7 @@
     blocks = [((k - 4, k), merged[k]) if k in merged else ((k,), blocks[k]) for k in BLOCK_ORDER if k not in MERGED]
     for bit, _ in high_bits(n_ctx):
         blocks += [(tuple(bit + k for k in ks), swap(block, bit)) for ks, block in blocks]
-    terms = list(gradient_terms(balance, doc_lengths, own, other, blocks, heads, reach))
+    terms = list(gradient_terms(balance, doc_lengths, order_heads(own, other, heads, seq_total), blocks, heads, reach))
 
     for bit, below in reversed(high_bits(n_ctx)):
         for k in below:

time: 32.4 us -> 34.2 us (1.056)
  waiting for transfers between devices: 2.88 us -> 5.14 us
  starting transfers between devices: 22.2 us -> 21.7 us
    ppermute x13, waiting for transfers between devices: 2.87 us -> 5.13 us  [swap(): return lax.ppermute(array, 'ctx', [(i, i ^ k) for i in range(n_ctx)])]
    ppermute x13, starting transfers between devices: 20.1 us -> 19.7 us  [swap(): return lax.ppermute(array, 'ctx', [(i, i ^ k) for i in range(n_ctx)])]
  transfers between devices with their start and end apart: 15 -> 15, of which waited for: 3 -> 4; matrix products, arithmetic and copies ran while one was open for 0% -> 0% of each run, Pallas kernels for 9% -> 9%
where the time goes in v8:
time: 34.2 us; the launch traced here: 34 us
  starting transfers between devices  21.7 us (63%)
  Pallas kernels  5.79 us (17%)
  waiting for transfers between devices  5.14 us (15%)
  between operations  0.72 us (2%)
  local copies, waits for them, and re-layouts  0.64 us (2%)
    ppermute x13, starting transfers between devices, swap(): return lax.ppermute(array, 'ctx', [(i, i ^ k) for i in range(n_ctx)])  19.7 us
    ppermute x13, waiting for transfers between devices, swap(): return lax.ppermute(array, 'ctx', [(i, i ^ k) for i in range(n_ctx)])  5.13 us
    pallas_call x1, Pallas kernels, query_side(): pl.pallas_call(functools.partial(rows_kernel, len(after), listed, heads,...  2.87 us
    pallas_call x1, Pallas kernels, gradient_terms(): pl.pallas_call(functools.partial(terms_kernel, listed, heads, reach), out...  2.06 us
    ppermute x2, starting transfers between devices, body(): lax.ppermute(array, 'head', [(i, n_head - 1 - i) for i in range(n_head)])  2.03 us
    pallas_call x1, Pallas kernels, pack(): pl.pallas_call(pack_kernel, out_shape=[jax.ShapeDtypeStruct((2 * key_rows...  0.81 us
  transfers between devices with their start and end apart: 15, of which 4 were waited for; matrix products, arithmetic and copies ran while one was open for 0% of the time, Pallas kernels for 9%

profile of v8, /device:TPU:0, one launch (start us, length us, event | category | flops | bytes accessed | tf_op | source)
XLA Modules:
  0.0 34.0 jit_solution(14023465673782380764)
XLA Ops:
  0.6 0.8 %shard_map.93 = (bf16[256,128]{1,0:T(8,128)(2,1)S(1)}, s32[1024]{0:T(1024)S(1)}, s32[8]{0:T(128)S(1)}) custom-call(bf16[128,128]{1,0:T(8,128)(2,1)} %key_rows.1, bf16[128,128]{1,0:T(8,128)(2,1)} %value_rows.1, s32[1024]{0:T(1024)} %balance.1, s32[8]{0:T(128)} %doc_lengths.1), custom_call_target="tpu_custom_call" | custom-call | tf_op jit(solution)/shard_map/pallas_call | solution.py:72
  1.5 4.1 %collective-permute-start.2 = (bf16[256,128]{1,0:T(8,128)(2,1)S(1)}, bf16[256,128]{1,0:T(8,128)(2,1)S(1)}, u32[]{:S(2)}, u32[]{:S(2)}) collective-permute-start(bf16[256,128]{1,0:T(8,128)(2,1)S(1)} %get-tuple-element.19.first.refs_0_.refs_1_), channel_id=1, source_target_pairs={{0,8},{2,10},{4,12},{6,14},{8,0},{10,2},{12,4},{14,6},{1,9},{3,11}... | collective-permute-start | bytes 196616 | tf_op jit(solution)/shard_map/ppermute | solution.py:318
  5.6 1.5 %collective-permute-start = (bf16[512,128]{1,0:T(8,128)(2,1)}, bf16[512,128]{1,0:T(8,128)(2,1)S(1)}, u32[]{:S(2)}, u32[]{:S(2)}) collective-permute-start(bf16[512,128]{1,0:T(8,128)(2,1)} %bitcast.4), channel_id=1, source_target_pairs={{0,1},{1,0},{2,3},{3,2},{4,5},{5,4},{6,7},{7,6},{8,9},{9,8},{10,11... | collective-permute-start | bytes 393224 | tf_op jit(solution)/shard_map/ppermute | solution.py:326
  7.0 0.0 copy-start
  7.0 0.0 copy-start.1
  7.1 0.5 %collective-permute-start.1 = (bf16[512,128]{1,0:T(8,128)(2,1)}, bf16[512,128]{1,0:T(8,128)(2,1)S(1)}, u32[]{:S(2)}, u32[]{:S(2)}) collective-permute-start(bf16[512,128]{1,0:T(8,128)(2,1)} %bitcast.7), channel_id=1, source_target_pairs={{0,1},{1,0},{2,3},{3,2},{4,5},{5,4},{6,7},{7,6},{8,9},{9,8},{10,11... | collective-permute-start | bytes 393224 | tf_op jit(solution)/shard_map/ppermute | solution.py:326
  7.6 1.6 %collective-permute-done.2.second.refs_2_.refs_3_ = bf16[256,128]{1,0:T(8,128)(2,1)S(1)} collective-permute-done((bf16[256,128]{1,0:T(8,128)(2,1)S(1)}, bf16[256,128]{1,0:T(8,128)(2,1)S(1)}, u32[]{:S(2)}, u32[]{:S(2)}) %collective-permute-start.2) | collective-permute-done | bytes 65568 | tf_op jit(solution)/shard_map/ppermute | solution.py:318
  9.2 1.6 %collective-permute-start.7 = (bf16[512,128]{1,0:T(8,128)(2,1)S(1)}, bf16[512,128]{1,0:T(8,128)(2,1)S(1)}, u32[]{:S(2)}, u32[]{:S(2)}) collective-permute-start(bf16[512,128]{1,0:T(8,128)(2,1)S(1)} %shard_map.95), channel_id=1, source_target_pairs={{0,6},{2,4},{4,2},{6,0},{8,14},{10,12},{12,10},{14,8},{1,7},{3,5},... | collective-permute-start | bytes 393224 | tf_op jit(solution)/shard_map/ppermute | solution.py:318
  10.8 1.7 %collective-permute-start.5 = (bf16[256,128]{1,0:T(8,128)(2,1)S(1)}, bf16[256,128]{1,0:T(8,128)(2,1)S(1)}, u32[]{:S(2)}, u32[]{:S(2)}) collective-permute-start(bf16[256,128]{1,0:T(8,128)(2,1)S(1)} %get-tuple-element.19.first.refs_0_.refs_1_), channel_id=1, source_target_pairs={{0,4},{2,6},{4,0},{6,2},{8,12},{10,14},{12,8},{14,10},{1,5},{3,7},... | collective-permute-start | bytes 196616 | tf_op jit(solution)/shard_map/ppermute | solution.py:318
  12.5 0.3 collective-permute-start.4
  12.8 0.0 collective-permute-done.q_other
  12.8 1.7 %collective-permute-start.6 = (bf16[256,128]{1,0:T(8,128)(2,1)S(1)}, bf16[256,128]{1,0:T(8,128)(2,1)S(1)}, u32[]{:S(2)}, u32[]{:S(2)}) collective-permute-start(bf16[256,128]{1,0:T(8,128)(2,1)S(1)} %collective-permute-done.2.second.refs_2_.refs_3_), channel_id=1, source_target_pairs={{0,2},{2,0},{4,6},{6,4},{8,10},{10,8},{12,14},{14,12},{1,3},{3,1},... | collective-permute-start | bytes 196616 | tf_op jit(solution)/shard_map/ppermute | solution.py:318
  14.5 0.0 collective-permute-done.1.g_other
  14.5 0.7 %collective-permute-start.3 = (bf16[256,128]{1,0:T(8,128)(2,1)S(1)}, bf16[256,128]{1,0:T(8,128)(2,1)S(1)}, u32[]{:S(2)}, u32[]{:S(2)}) collective-permute-start(bf16[256,128]{1,0:T(8,128)(2,1)S(1)} %collective-permute-done.2.second.refs_2_.refs_3_), channel_id=1, source_target_pairs={{0,4},{2,6},{4,0},{6,2},{8,12},{10,14},{12,8},{14,10},{1,5},{3,7},... | collective-permute-start | bytes 196616 | tf_op jit(solution)/shard_map/ppermute | solution.py:318
  15.2 0.0 copy-done
  15.2 0.0 copy-done.1
  15.3 1.5 %collective-permute-done.5.refs_4_.refs_5_ = bf16[256,128]{1,0:T(8,128)(2,1)S(1)} collective-permute-done((bf16[256,128]{1,0:T(8,128)(2,1)S(1)}, bf16[256,128]{1,0:T(8,128)(2,1)S(1)}, u32[]{:S(2)}, u32[]{:S(2)}) %collective-permute-start.5) | collective-permute-done | bytes 65568 | tf_op jit(solution)/shard_map/ppermute | solution.py:318
  16.8 0.0 collective-permute-done.4.refs_3_.refs_4_
  16.8 0.6 %collective-permute-done.6.refs_5_.refs_6_ = bf16[256,128]{1,0:T(8,128)(2,1)S(1)} collective-permute-done((bf16[256,128]{1,0:T(8,128)(2,1)S(1)}, bf16[256,128]{1,0:T(8,128)(2,1)S(1)}, u32[]{:S(2)}, u32[]{:S(2)}) %collective-permute-start.6) | collective-permute-done | bytes 65568 | tf_op jit(solution)/shard_map/ppermute | solution.py:318
  17.4 1.3 %collective-permute-done.3.refs_1_.refs_2_ = bf16[256,128]{1,0:T(8,128)(2,1)S(1)} collective-permute-done((bf16[256,128]{1,0:T(8,128)(2,1)S(1)}, bf16[256,128]{1,0:T(8,128)(2,1)S(1)}, u32[]{:S(2)}, u32[]{:S(2)}) %collective-permute-start.3) | collective-permute-done | bytes 65568 | tf_op jit(solution)/shard_map/ppermute | solution.py:318
  18.8 0.0 collective-permute-done.7.refs_6_.refs_7_
  18.8 2.1 %shard_map.96 = (f32[256,128]{1,0:T(8,128)S(1)}, bf16[256,128]{1,0:T(8,128)(2,1)S(1)}, bf16[256,128]{1,0:T(8,128)(2,1)S(1)}, bf16[256,128]{1,0:T(8,128)(2,1)S(1)...) custom-call(s32[1024]{0:T(1024)S(1)} %get-tuple-element.17.balance_i, ...), custom_call_target="tpu_custom_call" | custom-call | tf_op jit(solution)/shard_map/pallas_call | solution.py:230
  20.8 1.6 %collective-permute-start.8 = (bf16[256,128]{1,0:T(8,128)(2,1)S(1)}, bf16[256,128]{1,0:T(8,128)(2,1)S(1)}, u32[]{:S(2)}, u32[]{:S(2)}) collective-permute-start(bf16[256,128]{1,0:T(8,128)(2,1)S(1)} %get-tuple-element.21), channel_id=1, source_target_pairs={{0,6},{2,4},{4,2},{6,0},{8,14},{10,12},{12,10},{14,8},{1,7},{3,5},... | collective-permute-start | bytes 196616 | tf_op jit(solution)/shard_map/ppermute | solution.py:318
  22.5 0.4 %collective-permute-start.9 = (bf16[256,128]{1,0:T(8,128)(2,1)S(1)}, bf16[256,128]{1,0:T(8,128)(2,1)S(1)}, u32[]{:S(2)}, u32[]{:S(2)}) collective-permute-start(bf16[256,128]{1,0:T(8,128)(2,1)S(1)} %get-tuple-element.22), channel_id=1, source_target_pairs={{0,4},{2,6},{4,0},{6,2},{8,12},{10,14},{12,8},{14,10},{1,5},{3,7},... | collective-permute-start | bytes 196616 | tf_op jit(solution)/shard_map/ppermute | solution.py:318
  22.9 1.5 %collective-permute-start.10 = (bf16[256,128]{1,0:T(8,128)(2,1)S(1)}, bf16[256,128]{1,0:T(8,128)(2,1)S(1)}, u32[]{:S(2)}, u32[]{:S(2)}) collective-permute-start(bf16[256,128]{1,0:T(8,128)(2,1)S(1)} %get-tuple-element.23), channel_id=1, source_target_pairs={{0,2},{2,0},{4,6},{6,4},{8,10},{10,8},{12,14},{14,12},{1,3},{3,1},... | collective-permute-start | bytes 196616 | tf_op jit(solution)/shard_map/ppermute | solution.py:318
  24.4 0.5 %collective-permute-start.11 = (bf16[256,128]{1,0:T(8,128)(2,1)S(1)}, bf16[256,128]{1,0:T(8,128)(2,1)S(1)}, u32[]{:S(2)}, u32[]{:S(2)}) collective-permute-start(bf16[256,128]{1,0:T(8,128)(2,1)S(1)} %get-tuple-element.27), channel_id=1, source_target_pairs={{0,2},{2,0},{4,6},{6,4},{8,10},{10,8},{12,14},{14,12},{1,3},{3,1},... | collective-permute-start | bytes 196616 | tf_op jit(solution)/shard_map/ppermute | solution.py:318
  24.9 1.6 %collective-permute-start.12 = (bf16[256,128]{1,0:T(8,128)(2,1)S(1)}, bf16[256,128]{1,0:T(8,128)(2,1)S(1)}, u32[]{:S(2)}, u32[]{:S(2)}) collective-permute-start(bf16[256,128]{1,0:T(8,128)(2,1)S(1)} %get-tuple-element.28), channel_id=1, source_target_pairs={{0,4},{2,6},{4,0},{6,2},{8,12},{10,14},{12,8},{14,10},{1,5},{3,7},... | collective-permute-start | bytes 196616 | tf_op jit(solution)/shard_map/ppermute | solution.py:318
  26.5 0.0 collective-permute-done.8
  26.5 1.4 %collective-permute-start.13 = (bf16[256,128]{1,0:T(8,128)(2,1)S(1)}, bf16[256,128]{1,0:T(8,128)(2,1)S(1)}, u32[]{:S(2)}, u32[]{:S(2)}) collective-permute-start(bf16[256,128]{1,0:T(8,128)(2,1)S(1)} %get-tuple-element.29), channel_id=1, source_target_pairs={{0,6},{2,4},{4,2},{6,0},{8,14},{10,12},{12,10},{14,8},{1,7},{3,5},... | collective-permute-start | bytes 196616 | tf_op jit(solution)/shard_map/ppermute | solution.py:318
  27.9 0.0 collective-permute-done.9
  27.9 0.0 collective-permute-done.10
  27.9 2.5 %collective-permute-start.14 = (bf16[256,128]{1,0:T(8,128)(2,1)S(1)}, bf16[256,128]{1,0:T(8,128)(2,1)S(1)}, u32[]{:S(2)}, u32[]{:S(2)}) collective-permute-start(bf16[256,128]{1,0:T(8,128)(2,1)S(1)} %add_convert_fusion.1.refs_0_), channel_id=1, source_target_pairs={{0,8},{2,10},{4,12},{6,14},{8,0},{10,2},{12,4},{14,6},{1,9},{3,11}... | collective-permute-start | bytes 196616 | tf_op jit(solution)/shard_map/ppermute | solution.py:318
  30.4 2.9 %shard_map.97 = (bf16[512,128]{1,0:T(8,128)(2,1)}, bf16[512,128]{1,0:T(8,128)(2,1)}) custom-call(s32[1024]{0:T(1024)S(1)} %get-tuple-element.17.balance_in, s32[8]{0:T(128)S(1)} %get-tuple-element.18.docs_in, bf16[512,128]{1,0:T(8,128)(2,1)S(1)} %bitcast.6, bf16[512,128]{1,0:T(8,128)(2,1)S(1)} %bitcast.9, bf16[256,128]{1,0:T(8,128)(2,1)S(1)} %add_convert_fusion.1.refs_0_, ...), custom_call_target="tpu_custom_call" | custom-call | tf_op jit(solution)/shard_map/pallas_call | solution.py:291
  33.3 0.0 collective-permute-done.11
  33.3 0.0 collective-permute-done.12
  33.3 0.0 collective-permute-done.13
  33.3 0.0 collective-permute-done.14
  33.4 0.6 %fusion = (bf16[128,128]{1,0:T(8,128)(2,1)}, bf16[128,128]{1,0:T(8,128)(2,1)}) fusion(bf16[256,128]{1,0:T(8,128)(2,1)S(1)} %add_convert_fusion), kind=kLoop, calls=%fused_computation.2 | loop fusion | bytes 131072 | tf_op jit(solution)/shard_map/slice | solution.py:356
  (4 shorter events, 0.1 us)
Async XLA Ops:
  1.5 7.8 %collective-permute-start.2 = (bf16[256,128]{1,0:T(8,128)(2,1)S(1)}, bf16[256,128]{1,0:T(8,128)(2,1)S(1)}, u32[]{:S(2)}, u32[]{:S(2)}) collective-permute-start(bf16[256,128]{1,0:T(8,128)(2,1)S(1)} %get-tuple-element.19.first.refs_0_.refs_1_), channel_id=1, source_target_pairs={{0,8},{2,10},{4,12},{6,14},{8,0},{10,2},{12,4},{14,6},{1,9},{3,11}... | collective-permute-start | bytes 196616 | tf_op jit(solution)/shard_map/ppermute | solution.py:318
  5.6 7.2 %collective-permute-start = (bf16[512,128]{1,0:T(8,128)(2,1)}, bf16[512,128]{1,0:T(8,128)(2,1)S(1)}, u32[]{:S(2)}, u32[]{:S(2)}) collective-permute-start(bf16[512,128]{1,0:T(8,128)(2,1)} %bitcast.4), channel_id=1, source_target_pairs={{0,1},{1,0},{2,3},{3,2},{4,5},{5,4},{6,7},{7,6},{8,9},{9,8},{10,11... | collective-permute-start | bytes 393224 | tf_op jit(solution)/shard_map/ppermute | solution.py:326
  7.0 8.2 %copy-start = (bf16[128,4,128]{2,1,0:T(4,128)(2,1)S(1)}, bf16[128,4,128]{2,1,0:T(4,128)(2,1)}, u32[]{:S(2)}) copy-start(bf16[128,4,128]{2,1,0:T(4,128)(2,1)} %param.6) | copy-start | bytes 393220
  7.0 8.2 %copy-start.1 = (bf16[128,4,128]{2,1,0:T(4,128)(2,1)S(1)}, bf16[128,4,128]{2,1,0:T(4,128)(2,1)}, u32[]{:S(2)}) copy-start(bf16[128,4,128]{2,1,0:T(4,128)(2,1)} %param.9) | copy-start | bytes 393220
  7.1 7.5 %collective-permute-start.1 = (bf16[512,128]{1,0:T(8,128)(2,1)}, bf16[512,128]{1,0:T(8,128)(2,1)S(1)}, u32[]{:S(2)}, u32[]{:S(2)}) collective-permute-start(bf16[512,128]{1,0:T(8,128)(2,1)} %bitcast.7), channel_id=1, source_target_pairs={{0,1},{1,0},{2,3},{3,2},{4,5},{5,4},{6,7},{7,6},{8,9},{9,8},{10,11... | collective-permute-start | bytes 393224 | tf_op jit(solution)/shard_map/ppermute | solution.py:326
  9.2 9.6 %collective-permute-start.7 = (bf16[512,128]{1,0:T(8,128)(2,1)S(1)}, bf16[512,128]{1,0:T(8,128)(2,1)S(1)}, u32[]{:S(2)}, u32[]{:S(2)}) collective-permute-start(bf16[512,128]{1,0:T(8,128)(2,1)S(1)} %shard_map.95), channel_id=1, source_target_pairs={{0,6},{2,4},{4,2},{6,0},{8,14},{10,12},{12,10},{14,8},{1,7},{3,5},... | collective-permute-start | bytes 393224 | tf_op jit(solution)/shard_map/ppermute | solution.py:318
  10.8 6.0 %collective-permute-start.5 = (bf16[256,128]{1,0:T(8,128)(2,1)S(1)}, bf16[256,128]{1,0:T(8,128)(2,1)S(1)}, u32[]{:S(2)}, u32[]{:S(2)}) collective-permute-start(bf16[256,128]{1,0:T(8,128)(2,1)S(1)} %get-tuple-element.19.first.refs_0_.refs_1_), channel_id=1, source_target_pairs={{0,4},{2,6},{4,0},{6,2},{8,12},{10,14},{12,8},{14,10},{1,5},{3,7},... | collective-permute-start | bytes 196616 | tf_op jit(solution)/shard_map/ppermute | solution.py:318
  12.5 4.3 %collective-permute-start.4 = (bf16[256,128]{1,0:T(8,128)(2,1)S(1)}, bf16[256,128]{1,0:T(8,128)(2,1)S(1)}, u32[]{:S(2)}, u32[]{:S(2)}) collective-permute-start(bf16[256,128]{1,0:T(8,128)(2,1)S(1)} %get-tuple-element.19.first.refs_0_.refs_1_), channel_id=1, source_target_pairs={{0,2},{2,0},{4,6},{6,4},{8,10},{10,8},{12,14},{14,12},{1,3},{3,1},... | collective-permute-start | bytes 196616 | tf_op jit(solution)/shard_map/ppermute | solution.py:318
  12.8 4.7 %collective-permute-start.6 = (bf16[256,128]{1,0:T(8,128)(2,1)S(1)}, bf16[256,128]{1,0:T(8,128)(2,1)S(1)}, u32[]{:S(2)}, u32[]{:S(2)}) collective-permute-start(bf16[256,128]{1,0:T(8,128)(2,1)S(1)} %collective-permute-done.2.second.refs_2_.refs_3_), channel_id=1, source_target_pairs={{0,2},{2,0},{4,6},{6,4},{8,10},{10,8},{12,14},{14,12},{1,3},{3,1},... | collective-permute-start | bytes 196616 | tf_op jit(solution)/shard_map/ppermute | solution.py:318
  14.5 4.3 %collective-permute-start.3 = (bf16[256,128]{1,0:T(8,128)(2,1)S(1)}, bf16[256,128]{1,0:T(8,128)(2,1)S(1)}, u32[]{:S(2)}, u32[]{:S(2)}) collective-permute-start(bf16[256,128]{1,0:T(8,128)(2,1)S(1)} %collective-permute-done.2.second.refs_2_.refs_3_), channel_id=1, source_target_pairs={{0,4},{2,6},{4,0},{6,2},{8,12},{10,14},{12,8},{14,10},{1,5},{3,7},... | collective-permute-start | bytes 196616 | tf_op jit(solution)/shard_map/ppermute | solution.py:318
  20.8 5.7 %collective-permute-start.8 = (bf16[256,128]{1,0:T(8,128)(2,1)S(1)}, bf16[256,128]{1,0:T(8,128)(2,1)S(1)}, u32[]{:S(2)}, u32[]{:S(2)}) collective-permute-start(bf16[256,128]{1,0:T(8,128)(2,1)S(1)} %get-tuple-element.21), channel_id=1, source_target_pairs={{0,6},{2,4},{4,2},{6,0},{8,14},{10,12},{12,10},{14,8},{1,7},{3,5},... | collective-permute-start | bytes 196616 | tf_op jit(solution)/shard_map/ppermute | solution.py:318
  22.5 5.4 %collective-permute-start.9 = (bf16[256,128]{1,0:T(8,128)(2,1)S(1)}, bf16[256,128]{1,0:T(8,128)(2,1)S(1)}, u32[]{:S(2)}, u32[]{:S(2)}) collective-permute-start(bf16[256,128]{1,0:T(8,128)(2,1)S(1)} %get-tuple-element.22), channel_id=1, source_target_pairs={{0,4},{2,6},{4,0},{6,2},{8,12},{10,14},{12,8},{14,10},{1,5},{3,7},... | collective-permute-start | bytes 196616 | tf_op jit(solution)/shard_map/ppermute | solution.py:318
  22.9 5.0 %collective-permute-start.10 = (bf16[256,128]{1,0:T(8,128)(2,1)S(1)}, bf16[256,128]{1,0:T(8,128)(2,1)S(1)}, u32[]{:S(2)}, u32[]{:S(2)}) collective-permute-start(bf16[256,128]{1,0:T(8,128)(2,1)S(1)} %get-tuple-element.23), channel_id=1, source_target_pairs={{0,2},{2,0},{4,6},{6,4},{8,10},{10,8},{12,14},{14,12},{1,3},{3,1},... | collective-permute-start | bytes 196616 | tf_op jit(solution)/shard_map/ppermute | solution.py:318
  24.4 8.9 %collective-permute-start.11 = (bf16[256,128]{1,0:T(8,128)(2,1)S(1)}, bf16[256,128]{1,0:T(8,128)(2,1)S(1)}, u32[]{:S(2)}, u32[]{:S(2)}) collective-permute-start(bf16[256,128]{1,0:T(8,128)(2,1)S(1)} %get-tuple-element.27), channel_id=1, source_target_pairs={{0,2},{2,0},{4,6},{6,4},{8,10},{10,8},{12,14},{14,12},{1,3},{3,1},... | collective-permute-start | bytes 196616 | tf_op jit(solution)/shard_map/ppermute | solution.py:318
  24.9 8.4 %collective-permute-start.12 = (bf16[256,128]{1,0:T(8,128)(2,1)S(1)}, bf16[256,128]{1,0:T(8,128)(2,1)S(1)}, u32[]{:S(2)}, u32[]{:S(2)}) collective-permute-start(bf16[256,128]{1,0:T(8,128)(2,1)S(1)} %get-tuple-element.28), channel_id=1, source_target_pairs={{0,4},{2,6},{4,0},{6,2},{8,12},{10,14},{12,8},{14,10},{1,5},{3,7},... | collective-permute-start | bytes 196616 | tf_op jit(solution)/shard_map/ppermute | solution.py:318
  26.5 6.8 %collective-permute-start.13 = (bf16[256,128]{1,0:T(8,128)(2,1)S(1)}, bf16[256,128]{1,0:T(8,128)(2,1)S(1)}, u32[]{:S(2)}, u32[]{:S(2)}) collective-permute-start(bf16[256,128]{1,0:T(8,128)(2,1)S(1)} %get-tuple-element.29), channel_id=1, source_target_pairs={{0,6},{2,4},{4,2},{6,0},{8,14},{10,12},{12,10},{14,8},{1,7},{3,5},... | collective-permute-start | bytes 196616 | tf_op jit(solution)/shard_map/ppermute | solution.py:318
  27.9 5.4 %collective-permute-start.14 = (bf16[256,128]{1,0:T(8,128)(2,1)S(1)}, bf16[256,128]{1,0:T(8,128)(2,1)S(1)}, u32[]{:S(2)}, u32[]{:S(2)}) collective-permute-start(bf16[256,128]{1,0:T(8,128)(2,1)S(1)} %add_convert_fusion.1.refs_0_), channel_id=1, source_target_pairs={{0,8},{2,10},{4,12},{6,14},{8,0},{10,2},{12,4},{14,6},{1,9},{3,11}... | collective-permute-start | bytes 196616 | tf_op jit(solution)/shard_map/ppermute | solution.py:318
